TPU v7x, 32 devices: a whole 2x2x4 slice. The times are simulated.
32 devices in a mesh: dp: 8 (over z, x), mp: 4 (over y, core).
Axes of the slice: x: 2, y: 2, z: 4, core: 2. Of those that a mesh axis runs over, the one named last changes fastest.
Arguments:
- tokens: bfloat16 [16384, 768], P('dp'), may hold values from -6 to 6
- cotangent: bfloat16 [16384, 768], P('dp'), may hold values from -30 to 30
- exit_layer: int32 [16], P('dp'), may hold values from 1 to 12, as said below
- labels: int32 [16], P('dp'), may hold values from 0 to 2
- qkv_weight: float32 [768, 3, 768], P('dp', None, 'mp'), may hold values from -0.21875 to 0.21875
- qkv_first: float32 [768, 3, 768], P('dp', None, 'mp'), may hold values from -80 to 80
- qkv_second: float32 [768, 3, 768], P('dp', None, 'mp'), may hold values from 360.448 to 1425.408
- out_weight: float32 [768, 768], P('mp', 'dp'), may hold values from -6 to 6
- out_first: float32 [768, 768], P('mp', 'dp'), may hold values from -8 to 8
- out_second: float32 [768, 768], P('mp', 'dp'), may hold values from 3.60448 to 14.25408
- up_weight: float32 [768, 3072], P('dp', 'mp'), may hold values from -0.21875 to 0.21875
- up_first: float32 [768, 3072], P('dp', 'mp'), may hold values from -40 to 40
- up_second: float32 [768, 3072], P('dp', 'mp'), may hold values from 88.4736 to 355.5328
- down_weight: float32 [3072, 768], P('mp', 'dp'), may hold values from -0.109375 to 0.109375
- down_first: float32 [3072, 768], P('mp', 'dp'), may hold values from -80 to 80
- down_second: float32 [3072, 768], P('mp', 'dp'), may hold values from 360.448 to 1425.408
- pool_weight: float32 [768, 768], P('dp'), may hold values from -0.21875 to 0.21875
- pool_first: float32 [768, 768], P('dp'), may hold values from -0.0078125 to 0.0078125
- pool_second: float32 [768, 768], P('dp'), may hold values from 3.125e-06 to 1.25e-05
- qv_bias: float32 [2, 768], P(None, 'mp'), may hold values from -0.6 to 0.6
- qv_first: float32 [2, 768], P(None, 'mp'), may hold values from -80 to 80
- qv_second: float32 [2, 768], P(None, 'mp'), may hold values from 360.448 to 1425.408
- up_bias: float32 [3072], P('mp'), may hold values from -3 to 3
- upb_first: float32 [3072], P('mp'), may hold values from -40 to 40
- upb_second: float32 [3072], P('mp'), may hold values from 88.4736 to 355.5328
- layer_vectors: float32 [7, 768], replicated, may hold values from -1.5 to 1.5, as said below
- vector_first: float32 [7, 768], replicated, may hold values from -128 to 128
- vector_second: float32 [7, 768], replicated, may hold values from 901.12 to 3604.48
- class_weight: float32 [769, 3], replicated, may hold values from -0.4375 to 0.4375
- class_first: float32 [769, 3], replicated, may hold values from -0.0625 to 0.0625
- class_second: float32 [769, 3], replicated, may hold values from 0.0002 to 0.0008
Outputs:
- block_out: bfloat16 [16384, 768], P('dp')
- tokens_grad: bfloat16 [16384, 768], P('dp')
- ramp_entropy: float32 [], replicated
- qkv_new: float32 [768, 3, 768], P('dp', None, 'mp')
- qkv_first_new: float32 [768, 3, 768], P('dp', None, 'mp')
- qkv_second_new: float32 [768, 3, 768], P('dp', None, 'mp')
- qkv_copy: bfloat16 [768, 3, 768], P('dp', None, 'mp')
- out_new: float32 [768, 768], P('mp', 'dp')
- out_first_new: float32 [768, 768], P('mp', 'dp')
- out_second_new: float32 [768, 768], P('mp', 'dp')
- out_copy: bfloat16 [768, 768], P('mp', 'dp')
- up_new: float32 [768, 3072], P('dp', 'mp')
- up_first_new: float32 [768, 3072], P('dp', 'mp')
- up_second_new: float32 [768, 3072], P('dp', 'mp')
- up_copy: bfloat16 [768, 3072], P('dp', 'mp')
- down_new: float32 [3072, 768], P('mp', 'dp')
- down_first_new: float32 [3072, 768], P('mp', 'dp')
- down_second_new: float32 [3072, 768], P('mp', 'dp')
- down_copy: bfloat16 [3072, 768], P('mp', 'dp')
- pool_new: float32 [768, 768], P('dp')
- pool_first_new: float32 [768, 768], P('dp')
- pool_second_new: float32 [768, 768], P('dp')
- pool_copy: bfloat16 [768, 768], P('dp')
- qv_new: float32 [2, 768], P(None, 'mp')
- qv_first_new: float32 [2, 768], P(None, 'mp')
- qv_second_new: float32 [2, 768], P(None, 'mp')
- upb_new: float32 [3072], P('mp')
- upb_first_new: float32 [3072], P('mp')
- upb_second_new: float32 [3072], P('mp')
- vector_new: float32 [7, 768], replicated
- vector_first_new: float32 [7, 768], replicated
- vector_second_new: float32 [7, 768], replicated
- class_new: float32 [769, 3], replicated
- class_first_new: float32 [769, 3], replicated
- class_second_new: float32 [769, 3], replicated
Inputs may be any that keep to these rules, and one draw needn't show every extreme that they name: `exit_layer`: the first sequence has exit layer 1; the second and the last have 12. `layer_vectors`: rows 0 and 2 lie between 0.5 and 1.5.
All inputs are finite; a program needn't handle non-finite values.
Results may differ from a plain program's by a relative error of at most 0.025.
Values may be sent and summed in bfloat16 or wider, within the bound.
No kernel may reach another device: no remote copies, remote signals or barrier semaphores. Data moves between devices by JAX's collectives and lax.ppermute only.
A program may use at most 192 MiB of HBM per device.

v0:
```python
import jax
import jax.numpy as jnp
from jax import lax
from jax.sharding import PartitionSpec as P

D = 768
HD = 64
FF = 3072
LAYER = 6
STEP = 10
LEN = 1024


EPS_NORM = 1e-06
BETA_ONE = 0.9
BETA_TWO = 0.98
EPS_ADAM = 1e-08
DECAY = 0.01
RATE = 0.8
VECTOR_RATE = 0.3


def normalize(hidden):
    centred = hidden - jnp.mean(hidden, axis=-1, keepdims=True)
    spread = lax.rsqrt(jnp.mean(centred * centred, axis=-1, keepdims=True) + EPS_NORM)
    return (centred * spread, spread)


def norm_back(grad_normed, normed, spread):
    return spread * (
        grad_normed
        - jnp.mean(grad_normed, axis=-1, keepdims=True)
        - normed * jnp.mean(grad_normed * normed, axis=-1, keepdims=True)
    )


def gelu_slope(pre_act):
    cumulative = 0.5 * (1.0 + lax.erf(pre_act * 0.7071067811865476))
    density = jnp.exp(-0.5 * pre_act * pre_act) * 0.3989422804014327
    return cumulative + pre_act * density


def adamw(weight, first, second, grad, rate, decay):
    first_new = BETA_ONE * first + (1.0 - BETA_ONE) * grad
    second_new = BETA_TWO * second + (1.0 - BETA_TWO) * grad * grad
    first_hat = first_new / (1.0 - BETA_ONE**STEP)
    second_hat = second_new / (1.0 - BETA_TWO**STEP)
    weight_new = weight - rate * (first_hat / (jnp.sqrt(second_hat) + EPS_ADAM) + decay * weight)
    return (weight_new, first_new, second_new)


def attend_forward(queries, key_rows, value_rows, seq_dev):
    seq_len = queries.shape[0] // seq_dev
    head_dev = queries.shape[1] // HD
    block_rows = min(512, seq_len)
    block_count = seq_len // block_rows
    score_scale = HD ** (-0.5)
    query_blocks = queries.reshape(seq_dev * block_count, block_rows, head_dev, HD)
    key_seqs = key_rows.reshape(seq_dev, seq_len, head_dev, HD)
    value_seqs = value_rows.reshape(seq_dev, seq_len, head_dev, HD)

    def attend_one_block(item_index):
        query_block = query_blocks[item_index]
        key_all = key_seqs[item_index // block_count]
        value_all = value_seqs[item_index // block_count]
        scores = (
            jnp.einsum("qhd,khd->hqk", query_block, key_all, preferred_element_type=jnp.float32)
            * score_scale
        )
        top_score = jnp.max(scores, axis=-1, keepdims=True)
        expo = jnp.exp(scores - top_score)
        row_total = jnp.sum(expo, axis=-1, keepdims=True)
        weights = (expo / row_total).astype(jnp.bfloat16)
        outputs = jnp.einsum(
            "hqk,khd->qhd", weights, value_all, preferred_element_type=jnp.float32
        ).astype(jnp.bfloat16)
        return (outputs, (top_score + jnp.log(row_total))[:, :, 0])

    outputs, log_totals = lax.map(attend_one_block, jnp.arange(seq_dev * block_count))
    return (
        outputs.reshape(seq_dev * seq_len, head_dev * HD),
        log_totals.reshape(seq_dev, block_count, head_dev, block_rows),
    )


def attend_backward(queries, key_rows, value_rows, grad_attn, log_totals):
    seq_dev, block_count, head_dev, block_rows = log_totals.shape
    seq_len = block_count * block_rows
    score_scale = HD ** (-0.5)
    block_shape = (seq_dev, block_count, block_rows, head_dev, HD)
    seq_shape = (seq_dev, seq_len, head_dev, HD)
    query_blocks = queries.reshape(block_shape)
    grad_blocks = grad_attn.reshape(block_shape)
    key_seqs = key_rows.reshape(seq_shape)
    value_seqs = value_rows.reshape(seq_shape)

    def one_sequence(seq_index):
        key_all = key_seqs[seq_index]
        value_all = value_seqs[seq_index]

        def one_one_block(running, triple):
            grad_keys, grad_values = running
            query_block, grad_block, log_block = triple
            scores = (
                jnp.einsum("qhd,khd->hqk", query_block, key_all, preferred_element_type=jnp.float32)
                * score_scale
            )
            weights = jnp.exp(scores - log_block[:, :, None])
            grad_values = grad_values + jnp.einsum(
                "hqk,qhd->khd",
                weights.astype(jnp.bfloat16),
                grad_block,
                preferred_element_type=jnp.float32,
            )
            grad_weights = jnp.einsum(
                "qhd,khd->hqk", grad_block, value_all, preferred_element_type=jnp.float32
            )
            row_inner = jnp.sum(weights * grad_weights, axis=-1, keepdims=True)
            grad_scores = (score_scale * weights * (grad_weights - row_inner)).astype(jnp.bfloat16)
            grad_query = jnp.einsum(
                "hqk,khd->qhd", grad_scores, key_all, preferred_element_type=jnp.float32
            )
            grad_keys = grad_keys + jnp.einsum(
                "hqk,qhd->khd", grad_scores, query_block, preferred_element_type=jnp.float32
            )
            return ((grad_keys, grad_values), grad_query.astype(jnp.bfloat16))

        empty_sum = jnp.zeros((seq_len, head_dev, HD), jnp.float32)
        (grad_keys, grad_values), grad_query = lax.scan(
            one_one_block,
            (empty_sum, empty_sum),
            (query_blocks[seq_index], grad_blocks[seq_index], log_totals[seq_index]),
        )
        return (grad_query, grad_keys.astype(jnp.bfloat16), grad_values.astype(jnp.bfloat16))

    query_grads, key_grads, value_grads = lax.map(one_sequence, jnp.arange(seq_dev))
    flat_shape = (seq_dev * seq_len, head_dev * HD)
    return (
        query_grads.reshape(flat_shape),
        key_grads.reshape(flat_shape),
        value_grads.reshape(flat_shape),
    )


def per_device(
    tokens,
    cotangent,
    exit_layer,
    labels,
    qkv_weight,
    qkv_first,
    qkv_second,
    out_weight,
    out_first,
    out_second,
    up_weight,
    up_first,
    up_second,
    down_weight,
    down_first,
    down_second,
    pool_weight,
    pool_first,
    pool_second,
    qv_bias,
    qv_first,
    qv_second,
    up_bias,
    upb_first,
    upb_second,
    layer_vectors,
    vector_first,
    vector_second,
    class_weight,
    class_first,
    class_second,
):
    tok_count, width = tokens.shape
    seq_dev = exit_layer.shape[0]
    seq_len = tok_count // seq_dev
    col_dev = qkv_weight.shape[2]
    live_mask = (exit_layer >= LAYER).astype(jnp.float32)
    carry_mask = (exit_layer > LAYER).astype(jnp.float32)
    qkv_full, out_full, up_full, down_full, pool_full = (
        lax.all_gather(qkv_weight.astype(jnp.bfloat16), "dp", axis=0, tiled=True),
        lax.all_gather(out_weight.astype(jnp.bfloat16), "dp", axis=1, tiled=True),
        lax.all_gather(up_weight.astype(jnp.bfloat16), "dp", axis=0, tiled=True),
        lax.all_gather(down_weight.astype(jnp.bfloat16), "dp", axis=1, tiled=True),
        lax.all_gather(pool_weight.astype(jnp.bfloat16), "dp", axis=0, tiled=True),
    )
    qkv_flat = qkv_full.reshape(width, 3 * col_dev)
    projected = jnp.dot(tokens, qkv_flat, preferred_element_type=jnp.float32)
    queries = (projected[:, :col_dev] + qv_bias[0]).astype(jnp.bfloat16)
    key_rows = projected[:, col_dev : 2 * col_dev].astype(jnp.bfloat16)
    value_rows = (projected[:, 2 * col_dev :] + qv_bias[1]).astype(jnp.bfloat16)
    attended, log_totals = attend_forward(queries, key_rows, value_rows, seq_dev)
    attn_total = lax.psum(
        jnp.dot(attended, out_full, preferred_element_type=jnp.float32).astype(jnp.bfloat16), "mp"
    ).astype(jnp.float32)
    first_in = tokens.astype(jnp.float32) + attn_total + layer_vectors[4]
    normed_one, spread_one = normalize(first_in)
    middle = normed_one * layer_vectors[0] + layer_vectors[1]
    middle_part = middle.astype(jnp.bfloat16)
    ffn_pre = jnp.dot(middle_part, up_full, preferred_element_type=jnp.float32) + up_bias
    ffn_act = jax.nn.gelu(ffn_pre, approximate=False).astype(jnp.bfloat16)
    ffn_total = lax.psum(
        jnp.dot(ffn_act, down_full, preferred_element_type=jnp.float32).astype(jnp.bfloat16), "mp"
    ).astype(jnp.float32)
    second_in = middle + ffn_total + layer_vectors[5]
    normed_two, spread_two = normalize(second_in)
    result_part = (normed_two * layer_vectors[2] + layer_vectors[3]).astype(jnp.bfloat16)
    cls_rows = result_part.reshape(seq_dev, seq_len, width)[:, 0]
    pool_pre = jnp.dot(cls_rows, pool_full, preferred_element_type=jnp.float32) + layer_vectors[6]
    pooled = jnp.tanh(pool_pre)
    pooled_low = pooled.astype(jnp.bfloat16)
    class_low = class_weight[:width].astype(jnp.bfloat16)
    logits = (
        jnp.dot(pooled_low, class_low, preferred_element_type=jnp.float32) + class_weight[width]
    )
    log_probs = logits - jax.nn.logsumexp(logits, axis=-1, keepdims=True)
    class_probs = jnp.exp(log_probs)
    entropy_local = -jnp.sum(live_mask * jnp.sum(class_probs * log_probs, axis=-1))
    live_total, entropy_total = lax.psum((jnp.sum(live_mask), entropy_local), "dp")
    onehot = (
        labels[:, None] == jnp.arange(class_weight.shape[1], dtype=jnp.int32)[None, :]
    ).astype(jnp.float32)
    grad_logits = (live_mask[:, None] * (class_probs - onehot) / live_total).astype(jnp.bfloat16)
    grad_class = jnp.concatenate(
        [
            jnp.einsum("sd,sc->dc", pooled_low, grad_logits, preferred_element_type=jnp.float32),
            jnp.sum(grad_logits, axis=0, keepdims=True, dtype=jnp.float32),
        ],
        axis=0,
    )
    grad_pooled = jnp.einsum(
        "sc,dc->sd", grad_logits, class_low, preferred_element_type=jnp.float32
    )
    grad_pool_pre = (grad_pooled * (1.0 - pooled * pooled)).astype(jnp.bfloat16)
    grad_pool = jnp.einsum("sd,se->de", cls_rows, grad_pool_pre, preferred_element_type=jnp.float32)
    grad_cls = jnp.einsum("se,de->sd", grad_pool_pre, pool_full, preferred_element_type=jnp.float32)
    grad_result = (
        cotangent.astype(jnp.float32).reshape(seq_dev, seq_len, width) * carry_mask[:, None, None]
    )
    grad_result = grad_result.at[:, 0].add(grad_cls).reshape(tok_count, width)
    grad_second = norm_back(grad_result * layer_vectors[2], normed_two, spread_two)
    grad_second_part = grad_second.astype(jnp.bfloat16)
    grad_down = jnp.einsum(
        "tf,td->fd", ffn_act, grad_second_part, preferred_element_type=jnp.float32
    )
    grad_act = jnp.einsum(
        "td,fd->tf", grad_second_part, down_full, preferred_element_type=jnp.float32
    )
    grad_ffn_pre = (grad_act * gelu_slope(ffn_pre)).astype(jnp.bfloat16)
    grad_up = jnp.einsum("td,tf->df", middle_part, grad_ffn_pre, preferred_element_type=jnp.float32)
    middle_total = lax.psum(
        jnp.einsum("tf,df->td", grad_ffn_pre, up_full, preferred_element_type=jnp.float32).astype(
            jnp.bfloat16
        ),
        "mp",
    ).astype(jnp.float32)
    grad_middle = grad_second + middle_total
    grad_first = norm_back(grad_middle * layer_vectors[0], normed_one, spread_one)
    grad_first_part = grad_first.astype(jnp.bfloat16)
    grad_out = jnp.einsum(
        "tc,td->cd", attended, grad_first_part, preferred_element_type=jnp.float32
    )
    grad_attended = jnp.einsum(
        "td,cd->tc", grad_first_part, out_full, preferred_element_type=jnp.float32
    ).astype(jnp.bfloat16)
    grad_query, grad_key, grad_value = attend_backward(
        queries, key_rows, value_rows, grad_attended, log_totals
    )
    grad_proj = jnp.concatenate([grad_query, grad_key, grad_value], axis=1)
    grad_qkv = jnp.einsum(
        "td,tc->dc", tokens, grad_proj, preferred_element_type=jnp.float32
    ).reshape(width, 3, col_dev)
    token_total = lax.psum(
        jnp.einsum("tc,dc->td", grad_proj, qkv_flat, preferred_element_type=jnp.float32).astype(
            jnp.bfloat16
        ),
        "mp",
    ).astype(jnp.float32)
    tokens_grad = (grad_first + token_total).astype(jnp.bfloat16)
    row_vectors = jnp.stack(
        [
            jnp.sum(grad_middle * normed_one, axis=0),
            jnp.sum(grad_middle, axis=0),
            jnp.sum(grad_result * normed_two, axis=0),
            jnp.sum(grad_result, axis=0),
            jnp.sum(grad_first, axis=0),
            jnp.sum(grad_second, axis=0),
        ]
    )
    vector_grads = jnp.concatenate(
        [row_vectors, jnp.sum(grad_pool_pre, axis=0, keepdims=True, dtype=jnp.float32)], axis=0
    )
    bias_grads = jnp.stack(
        [
            jnp.sum(grad_query, axis=0, dtype=jnp.float32),
            jnp.sum(grad_value, axis=0, dtype=jnp.float32),
        ]
    )
    upb_grad = jnp.sum(grad_ffn_pre, axis=0, dtype=jnp.float32)
    vector_sum, bias_sum, upb_sum, class_sum = lax.psum(
        (vector_grads, bias_grads, upb_grad, grad_class), "dp"
    )
    reduced_qkv, reduced_out, reduced_pool, reduced_down, reduced_up = (
        lax.psum_scatter(grad_qkv, "dp", scatter_dimension=0, tiled=True),
        lax.psum_scatter(grad_out, "dp", scatter_dimension=1, tiled=True),
        lax.psum_scatter(grad_pool, "dp", scatter_dimension=0, tiled=True),
        lax.psum_scatter(grad_down, "dp", scatter_dimension=1, tiled=True),
        lax.psum_scatter(grad_up, "dp", scatter_dimension=0, tiled=True),
    )
    qkv_new, qkv_first_new, qkv_second_new = adamw(
        qkv_weight, qkv_first, qkv_second, reduced_qkv, RATE * D ** (-0.5), DECAY
    )
    out_new, out_first_new, out_second_new = adamw(
        out_weight, out_first, out_second, reduced_out, RATE * max(1, 2 * D // LEN) ** (-0.5), DECAY
    )
    up_new, up_first_new, up_second_new = adamw(
        up_weight, up_first, up_second, reduced_up, RATE * D ** (-0.5), DECAY
    )
    down_new, down_first_new, down_second_new = adamw(
        down_weight, down_first, down_second, reduced_down, RATE * FF ** (-0.5), DECAY
    )
    pool_new, pool_first_new, pool_second_new = adamw(
        pool_weight, pool_first, pool_second, reduced_pool, RATE * D ** (-0.5), DECAY
    )
    qv_new, qv_first_new, qv_second_new = adamw(
        qv_bias, qv_first, qv_second, bias_sum, VECTOR_RATE, 0.0
    )
    upb_new, upb_first_new, upb_second_new = adamw(
        up_bias, upb_first, upb_second, upb_sum, VECTOR_RATE, 0.0
    )
    vector_new, vector_first_new, vector_second_new = adamw(
        layer_vectors, vector_first, vector_second, vector_sum, VECTOR_RATE, 0.0
    )
    class_new, class_first_new, class_second_new = adamw(
        class_weight, class_first, class_second, class_sum, RATE * (D // 4) ** (-0.5), DECAY
    )
    return (
        result_part,
        tokens_grad,
        entropy_total / live_total,
        qkv_new,
        qkv_first_new,
        qkv_second_new,
        qkv_new.astype(jnp.bfloat16),
        out_new,
        out_first_new,
        out_second_new,
        out_new.astype(jnp.bfloat16),
        up_new,
        up_first_new,
        up_second_new,
        up_new.astype(jnp.bfloat16),
        down_new,
        down_first_new,
        down_second_new,
        down_new.astype(jnp.bfloat16),
        pool_new,
        pool_first_new,
        pool_second_new,
        pool_new.astype(jnp.bfloat16),
        qv_new,
        qv_first_new,
        qv_second_new,
        upb_new,
        upb_first_new,
        upb_second_new,
        vector_new,
        vector_first_new,
        vector_second_new,
        class_new,
        class_first_new,
        class_second_new,
    )


def solution(mesh):
    in_specs = (
        P("dp", None),
        P("dp", None),
        P("dp"),
        P("dp"),
        P("dp", None, "mp"),
        P("dp", None, "mp"),
        P("dp", None, "mp"),
        P("mp", "dp"),
        P("mp", "dp"),
        P("mp", "dp"),
        P("dp", "mp"),
        P("dp", "mp"),
        P("dp", "mp"),
        P("mp", "dp"),
        P("mp", "dp"),
        P("mp", "dp"),
        P("dp", None),
        P("dp", None),
        P("dp", None),
        P(None, "mp"),
        P(None, "mp"),
        P(None, "mp"),
        P("mp"),
        P("mp"),
        P("mp"),
        P(),
        P(),
        P(),
        P(),
        P(),
        P(),
    )
    out_specs = (
        P("dp", None),
        P("dp", None),
        P(),
        P("dp", None, "mp"),
        P("dp", None, "mp"),
        P("dp", None, "mp"),
        P("dp", None, "mp"),
        P("mp", "dp"),
        P("mp", "dp"),
        P("mp", "dp"),
        P("mp", "dp"),
        P("dp", "mp"),
        P("dp", "mp"),
        P("dp", "mp"),
        P("dp", "mp"),
        P("mp", "dp"),
        P("mp", "dp"),
        P("mp", "dp"),
        P("mp", "dp"),
        P("dp", None),
        P("dp", None),
        P("dp", None),
        P("dp", None),
        P(None, "mp"),
        P(None, "mp"),
        P(None, "mp"),
        P("mp"),
        P("mp"),
        P("mp"),
        P(),
        P(),
        P(),
        P(),
        P(),
        P(),
    )
    return jax.shard_map(
        per_device, mesh=mesh, in_specs=in_specs, out_specs=out_specs, check_vma=False
    )
```

profile of v0, /device:TPU:0, one launch (start us, length us, event | category | flops | bytes accessed | tf_op | source)
XLA Modules:
  0.0 862.3 jit_solution(14293581950723858955)
XLA Ops:
  11.0 33.2 %all_gather.16 = bf16[192,768]{0,1:T(8,128)(2,1)S(1)} all-gather(bf16[192,96]{0,1:T(8,128)(2,1)S(1)} %copy.138), channel_id=1, replica_groups=mesh['dp'=8,'mp'=4] {'dp'}, dimensions={1}, use_global_device_ids=true | all-gather | bytes 331776 | tf_op jit(solution)/shard_map/all_gather | solution.py:186
  44.2 39.1 %all_gather.15 = bf16[768,3,192]{2,1,0:T(4,128)(2,1)S(1)} all-gather(bf16[96,3,192]{2,1,0:T(4,128)(2,1)S(1)} %copy.132), channel_id=1, replica_groups=mesh['dp'=8,'mp'=4] {'dp'}, dimensions={0}, use_global_device_ids=true | all-gather | bytes 995328 | tf_op jit(solution)/shard_map/all_gather | solution.py:185
  93.0 48.0 %while.44 = (s32[]{:T(128)}, bf16[4,512,3,64]{1,3,2,0:T(8,128)(2,1)}, f32[4,3,512]{2,1,0:T(4,128)}, s32[4]{0:T(128)S(1)}, bf16[2,1024,3,64]{1,3,2,0:T(8,128)(2,1...) while((s32[]{:T(128)}, ...), condition=%wide.region_3.4_spmd, body=%wide.region_0.3_spmd.sunk | while | flops 416905728 | bytes 20105580 | solution.py:79
  152.0 64.4 %all-reduce.6.cloned.1.call-done = bf16[2048,768]{1,0:T(8,128)(2,1)} async-done(((bf16[2048,768]{1,0:T(8,128)(2,1)}), bf16[2048,768]{1,0:T(8,128)(2,1)}) %all-reduce.6.cloned.1.call-update) | async-done | bytes 3145744 | tf_op jit(solution)/shard_map/psum | solution.py:197
  221.9 20.2 %fusion.46 = (bf16[2048,768]{1,0:T(8,128)(2,1)}, f32[2048,768]{1,0:T(8,128)}) fusion(f32[768]{0:T(1024)} %param.61, bf16[768,768]{1,0:T(8,128)(2,1)} %all-gather.4.cloned.1.call-done, f32[768]{0:T(1024)} %get-tuple-element.374, f32[768]{0:T(1024)S(1)} %get-tuple-element.375, f32[2048]{0:T(1024)} %add_rsqrt_fusion.1, f32[2048]{0:T(1024)S(1)} %broadcast_multiply_fusion.5, ...), kind=kOutput, calls=%fused_computation.63 | convolution fusion | flops 2533883904 | bytes 16936960 | tf_op jit(solution)/shard_map/dot_general | solution.py:204
  242.1 6.5 convolution_convert_fusion.2
  258.7 10.5 %copy_multiply_fusion = f32[2,1024,768]{2,0,1:T(2,128)} fusion(f32[2,1024,768]{2,1,0:T(8,128)} %convert.9, f32[2]{0:T(128)S(1)} %get-tuple-element.485), kind=kLoop, calls=%fused_computation.73 | loop fusion | flops 1572864 | bytes 12582920 | tf_op jit(solution)/shard_map/mul | solution.py:242
  269.2 48.2 %all-reduce.8.cloned.1.call-done = bf16[2048,768]{1,0:T(8,128)(2,1)} async-done(((bf16[2048,768]{1,0:T(8,128)(2,1)}), bf16[2048,768]{1,0:T(8,128)(2,1)}) %all-reduce.8.cloned.1.call-update) | async-done | bytes 3145744 | tf_op jit(solution)/shard_map/psum | solution.py:206
  331.8 22.2 %psum.72 = f32[]{:T(128)} all-reduce(f32[]{:T(128)} %get-tuple-element.378), channel_id=1, replica_groups=mesh['dp'=8,'mp'=4] {'dp'}, use_global_device_ids=true, to_apply=%region_13.14 | all-reduce | flops 1 | bytes 8 | tf_op jit(solution)/shard_map/psum | solution.py:223
  360.8 7.7 fusion.102
  379.4 6.2 subtract_multiply_fusion.1
  385.7 8.5 convert_reduce_fusion
  403.7 61.2 %all-reduce.10.cloned.1.call-done = bf16[2048,768]{1,0:T(8,128)(2,1)} async-done(((bf16[2048,768]{1,0:T(8,128)(2,1)}), bf16[2048,768]{1,0:T(8,128)(2,1)}) %all-reduce.10.cloned.1.call-update) | async-done | bytes 3145744 | tf_op jit(solution)/shard_map/psum | solution.py:255
  464.9 9.3 %multiply_reduce_fusion.2 = (f32[768]{0:T(1024)}, f32[2048]{0:T(1024)S(1)}, f32[2048]{0:T(1024)S(1)}, f32[768]{0:T(1024)}, f32[768]{0:T(1024)}) fusion(f32[2048,768]{1,0:T(8,128)} %copy-done.6, bf16[2048,768]{1,0:T(8,128)(2,1)} %all-reduce.10.cloned.1.call-done, f32[2048]{0:T(1024)} %add_rsqrt_fusion.1, f32[2048]{0:T(1024)S(1)} %broadcast_multiply_fusion.5, ...), kind=kLoop, calls=%fused_computation.74 | loop fusion | flops 25159424 | bytes 15776768 | tf_op jit(solution)/shard_map/reduce_sum | solution.py:286
  491.6 54.0 %while.46 = (s32[]{:T(128)}, bf16[2,2,512,3,64]{2,4,3,1,0:T(8,128)(2,1)}, bf16[2,1024,3,64]{1,3,2,0:T(8,128)(2,1)}, bf16[2,1024,3,64]{1,3,2,0:T(8,128)(2,1)}, s3...) while((s32[]{:T(128)}, ...), condition=%wide.region_23.24_spmd, body=%wide.region_19.23_spmd.sunk | while | flops 1028356608 | bytes 60430800 | solution.py:136
  500.3 16.6 %while.47 = (s32[]{:T(128)}, f32[1024,3,64]{0,2,1:T(8,128)S(1)}, f32[1024,3,64]{0,2,1:T(8,128)S(1)}, bf16[2,512,3,64]{1,3,2,0:T(8,128)(2,1)S(1)}, bf16[2,512,3,6...) while((s32[]{:T(128)}, f32[1024,3,64]{0,2,1:T(8,128)S(1)}, ...), condition=%wide.region_22.22_spmd.clone, body=%wide.region_20.21_spmd.clone.sunk | while | flops 1027963392 | bytes 52541588 | solution.py:129
  527.3 16.5 %while.47 = (s32[]{:T(128)}, f32[1024,3,64]{0,2,1:T(8,128)S(1)}, f32[1024,3,64]{0,2,1:T(8,128)S(1)}, bf16[2,512,3,64]{1,3,2,0:T(8,128)(2,1)S(1)}, bf16[2,512,3,6...) while((s32[]{:T(128)}, f32[1024,3,64]{0,2,1:T(8,128)S(1)}, ...), condition=%wide.region_22.22_spmd.clone, body=%wide.region_20.21_spmd.clone.sunk | while | flops 1027963392 | bytes 52541588 | solution.py:129
  558.8 8.0 fusion.68
  567.0 7.7 fusion.78
  586.9 38.8 %all-reduce = (f32[]{:T(128)}, f32[2,192]{1,0:T(2,128)S(1)}, f32[768]{0:T(1024)S(1)}, f32[7,768]{1,0:T(8,128)S(1)}, f32[769,3]{0,1:T(4,128)S(1)}) all-reduce(f32[]{:T(128)S(6)} %neg.7, f32[2,192]{1,0:T(2,128)S(1)} %pad_maximum_fusion.1, f32[768]{0:T(1024)S(1)} %copy-done.72, ...), channel_id=1, replica_groups=mesh['dp'=8,'mp'=4] {'dp'}, use_global_device_ids=true, to_apply=%region_27.28 | all-reduce | flops 8836 | bytes 70688 | tf_op jit(solution)/shard_map/psum | solution.py:223
  631.6 6.3 add_convert_fusion
  640.0 68.3 %reduce-scatter.10.cloned.1.call-done = f32[96,768]{1,0:T(8,128)} async-done(((f32[768,768]{1,0:T(8,128)}), f32[96,768]{1,0:T(8,128)}) %reduce-scatter.10.cloned.1.call-update) | async-done | bytes 294928 | tf_op jit(solution)/shard_map/reduce_scatter | solution.py:312
  710.4 69.6 %reduce-scatter.14.cloned.1.call-done = f32[96,768]{1,0:T(8,128)} async-done(((f32[768,768]{1,0:T(8,128)}), f32[96,768]{1,0:T(8,128)}) %reduce-scatter.14.cloned.1.call-update) | async-done | bytes 294928 | tf_op jit(solution)/shard_map/reduce_scatter | solution.py:310
  782.1 69.6 %reduce-scatter.8.cloned.1.call-done = f32[96,3,192]{2,0,1:T(8,128)} async-done(((f32[768,3,192]{2,0,1:T(8,128)}), f32[96,3,192]{2,0,1:T(8,128)}) %reduce-scatter.8.cloned.1.call-update) | async-done | bytes 221200 | tf_op jit(solution)/shard_map/reduce_scatter | solution.py:308
  (378 shorter events, 216.9 us)
Async XLA Ops:
  8.0 208.3 %all-reduce.6.cloned.1.call-start = ((), (), s32[]{:S(2)}) async-start(), calls=%async_computation.5 | async-start | bytes 6291456 | tf_op jit(solution)/shard_map/psum | solution.py:197
  146.7 75.3 %all-gather.4.cloned.1.call-start = ((), (), s32[]{:S(2)}) async-start(), calls=%async_computation.6 | async-start | bytes 1327104 | tf_op jit(solution)/shard_map/all_gather | solution.py:187
  148.4 93.7 %all-gather.6.cloned.1.call-start = ((), (), s32[]{:S(2)}) async-start(), calls=%async_computation.7 | async-start | bytes 1327104 | tf_op jit(solution)/shard_map/all_gather | solution.py:188
  150.1 167.3 %all-reduce.8.cloned.1.call-start = ((), (), s32[]{:S(2)}) async-start(), calls=%async_computation.8 | async-start | bytes 6291456 | tf_op jit(solution)/shard_map/psum | solution.py:206
  152.0 165.4 %copy-start.33 = (f32[768]{0:T(1024)}, f32[768]{0:T(1024)S(1)}, u32[]{:S(2)}) copy-start(f32[768]{0:T(1024)S(1)} %get-tuple-element.376) | copy-start | bytes 9220
  152.0 165.4 %copy-start.45 = (f32[768]{0:T(1024)}, f32[768]{0:T(1024)S(1)}, u32[]{:S(2)}) copy-start(f32[768]{0:T(1024)S(1)} %get-tuple-element.375) | copy-start | bytes 9220
  219.5 254.8 %copy-start.31 = (f32[2048]{0:T(1024)}, f32[2048]{0:T(1024)S(1)}, u32[]{:S(2)}) copy-start(f32[2048]{0:T(1024)S(1)} %broadcast_multiply_fusion.5) | copy-start | bytes 24580
  248.7 78.5 %all-gather.8.cloned.1.call-start = ((), (), s32[]{:S(2)}) async-start(), calls=%async_computation.9 | async-start | bytes 1327104 | tf_op jit(solution)/shard_map/all_gather | solution.py:189
  250.4 214.5 %all-reduce.10.cloned.1.call-start = ((), (), s32[]{:S(2)}) async-start(), calls=%async_computation.10 | async-start | bytes 6291456 | tf_op jit(solution)/shard_map/psum | solution.py:255
  399.9 229.8 %reduce-scatter.16.cloned.1.call-start = ((), (), s32[]{:S(2)}) async-start(), calls=%async_computation.16 | async-start | bytes 884736
  489.4 142.1 %all-reduce.12.cloned.1.call-start = ((), (), s32[]{:S(2)}) async-start(), calls=%async_computation.11 | async-start | bytes 6291456 | tf_op jit(solution)/shard_map/psum | solution.py:277
  558.5 79.3 %reduce-scatter.12.cloned.1.call-start = ((), (), s32[]{:S(2)}) async-start(), calls=%async_computation.14 | async-start | bytes 2654208 | tf_op jit(solution)/shard_map/reduce_scatter | solution.py:311
  566.9 141.4 %reduce-scatter.10.cloned.1.call-start = ((), (), s32[]{:S(2)}) async-start(), calls=%async_computation.13 | async-start | bytes 2654208 | tf_op jit(solution)/shard_map/reduce_scatter | solution.py:312
  574.7 205.3 %reduce-scatter.14.cloned.1.call-start = ((), (), s32[]{:S(2)}) async-start(), calls=%async_computation.15 | async-start | bytes 2654208 | tf_op jit(solution)/shard_map/reduce_scatter | solution.py:310
  576.7 275.0 %reduce-scatter.8.cloned.1.call-start = ((), (), s32[]{:S(2)}) async-start(), calls=%async_computation.12 | async-start | bytes 2654208 | tf_op jit(solution)/shard_map/reduce_scatter | solution.py:308
  631.5 76.8 %copy-start.17 = (f32[96,768]{1,0:T(8,128)S(1)}, f32[96,768]{1,0:T(8,128)}, u32[]{:S(2)}) copy-start(f32[96,768]{1,0:T(8,128)} %param.49) | copy-start | bytes 884740
  631.5 76.8 %copy-start.24 = (f32[96,768]{1,0:T(8,128)S(1)}, f32[96,768]{1,0:T(8,128)}, u32[]{:S(2)}) copy-start(f32[96,768]{1,0:T(8,128)} %param.50) | copy-start | bytes 884740
  631.5 76.8 %copy-start.25 = (f32[96,768]{1,0:T(8,128)S(1)}, f32[96,768]{1,0:T(8,128)}, u32[]{:S(2)}) copy-start(f32[96,768]{1,0:T(8,128)} %param.51) | copy-start | bytes 884740
  631.5 148.5 %copy-start.18 = (f32[96,768]{1,0:T(8,128)S(1)}, f32[96,768]{1,0:T(8,128)}, u32[]{:S(2)}) copy-start(f32[96,768]{1,0:T(8,128)} %param.55) | copy-start | bytes 884740
  631.5 148.5 %copy-start.26 = (f32[96,768]{1,0:T(8,128)S(1)}, f32[96,768]{1,0:T(8,128)}, u32[]{:S(2)}) copy-start(f32[96,768]{1,0:T(8,128)} %param.56) | copy-start | bytes 884740
  631.5 148.5 %copy-start.27 = (f32[96,768]{1,0:T(8,128)S(1)}, f32[96,768]{1,0:T(8,128)}, u32[]{:S(2)}) copy-start(f32[96,768]{1,0:T(8,128)} %param.57) | copy-start | bytes 884740
  637.8 213.9 %copy-start.19 = (f32[96,3,192]{2,0,1:T(8,128)S(1)}, f32[96,3,192]{2,0,1:T(8,128)}, u32[]{:S(2)}) copy-start(f32[96,3,192]{2,0,1:T(8,128)} %param.43) | copy-start | bytes 663556
  637.8 213.9 %copy-start.28 = (f32[96,3,192]{2,0,1:T(8,128)S(1)}, f32[96,3,192]{2,0,1:T(8,128)}, u32[]{:S(2)}) copy-start(f32[96,3,192]{2,0,1:T(8,128)} %param.44) | copy-start | bytes 663556
  637.8 213.9 %copy-start.29 = (f32[96,3,192]{2,0,1:T(8,128)S(1)}, f32[96,3,192]{2,0,1:T(8,128)}, u32[]{:S(2)}) copy-start(f32[96,3,192]{2,0,1:T(8,128)} %param.45) | copy-start | bytes 663556
  (73 other events, 1189.0 us)
Sparse Core Ops, SparseCore 0:
  146.8 69.5 all-reduce.5
  248.8 68.5 all-reduce.7
  400.0 64.8 all-reduce.9
  558.6 68.5 all-reduce.11
Sparse Core Ops, SparseCore 1:
  149.9 42.4 all-gather.3
  195.0 39.9 all-gather.5
  251.9 41.5 all-gather.7
  489.5 62.7 reduce-scatter.15
  566.9 69.4 reduce-scatter.11
  640.3 67.9 reduce-scatter.9
  712.1 67.9 reduce-scatter.13
  783.8 67.9 reduce-scatter.7
where the time goes:
time: 872 us; the launch traced here: 862 us
  waiting for transfers between devices  382 us (44%)
  matrix products  135 us (15%)
  blocking collectives  133 us (15%)
  other arithmetic  108 us (12%)
  local copies, waits for them, and re-layouts  62.8 us (7%)
  loops' own time  19.9 us (2%)
  between operations  19.9 us (2%)
    reduce_scatter x1, waiting for transfers between devices, per_device(): lax.psum_scatter(grad_pool, 'dp', scatter_dimension=0, tiled=True)  69.6 us
    reduce_scatter x1, waiting for transfers between devices, per_device(): lax.psum_scatter(grad_qkv, 'dp', scatter_dimension=0, tiled=True)  69.6 us
    reduce_scatter x1, waiting for transfers between devices, per_device(): lax.psum_scatter(grad_up, 'dp', scatter_dimension=0, tiled=True)  68.3 us
    psum x1, waiting for transfers between devices, per_device(): lax.psum(jnp.dot(attended, out_full, preferred_element_type=jnp.float32)....  64.4 us
    psum x1, waiting for transfers between devices, per_device(): lax.psum(jnp.einsum('tf,df->td', grad_ffn_pre, up_full, preferred_element...  61.2 us
    psum x2, blocking collectives, per_device(): lax.psum((jnp.sum(live_mask), entropy_local), 'dp')  61 us
    psum x1, waiting for transfers between devices, per_device(): lax.psum(jnp.dot(ffn_act, down_full, preferred_element_type=jnp.float32)....  48.2 us
    all_gather x1, blocking collectives, per_device(): lax.all_gather(qkv_weight.astype(jnp.bfloat16), 'dp', axis=0, tiled=True)  39.1 us
  transfers between devices with their start and end apart: 12, of which 6 were waited for; matrix products, arithmetic and copies ran while one was open for 19% of the time, Pallas kernels for 0%

commit v1 on v0

v1 whole, which is shorter than its diff:
```python
import functools

import jax
import jax.numpy as jnp
import numpy as np
from jax import lax
from jax.experimental import pallas as pl
from jax.experimental.pallas import tpu as pltpu
from jax.sharding import PartitionSpec as P

D = 768
HD = 64
FF = 3072
LAYER = 6
STEP = 10
LEN = 1024


EPS_NORM = 1e-06
BETA_ONE = 0.9
BETA_TWO = 0.98
EPS_ADAM = 1e-08
DECAY = 0.01
RATE = 0.8
VECTOR_RATE = 0.3

LOW = jnp.bfloat16
WIDE = jnp.float32
LOG2_E = 1.4426950408889634
MIB = 2**20

CORE, SIDE, X_BIT, Z_LOW, Z_HIGH = 1, 2, 4, 8, 16
BLOCKS = 8
BLOCK_ROWS = D // BLOCKS
ORDERS = {
    "query": (Z_HIGH, Z_LOW, X_BIT, SIDE),
    "key": (SIDE, Z_HIGH, Z_LOW, X_BIT),
    "value": (X_BIT, SIDE, Z_HIGH, Z_LOW),
    "out": (X_BIT, SIDE, Z_HIGH, Z_LOW),
    "up": (Z_HIGH, Z_LOW, X_BIT, SIDE),
    "down": (Z_HIGH, Z_LOW, SIDE, X_BIT),
}
NAMES = tuple(ORDERS)


def dot(left, right):
    return lax.dot_general(
        left, right, (((1,), (0,)), ((), ())), preferred_element_type=WIDE
    )


def dot_nt(left, right):
    return lax.dot_general(
        left, right, (((1,), (1,)), ((), ())), preferred_element_type=WIDE
    )


def dot_tn(left, right):
    return lax.dot_general(
        left, right, (((0,), (0,)), ((), ())), preferred_element_type=WIDE
    )


def adamw(weight, first, second, grad, rate, decay):
    first_new = BETA_ONE * first + (1.0 - BETA_ONE) * grad
    second_new = BETA_TWO * second + (1.0 - BETA_TWO) * grad * grad
    first_hat = first_new / (1.0 - BETA_ONE**STEP)
    second_hat = second_new / (1.0 - BETA_TWO**STEP)
    weight_new = weight - rate * (first_hat / (jnp.sqrt(second_hat) + EPS_ADAM) + decay * weight)
    return (weight_new, first_new, second_new)


class Links:
    def __init__(self, dp_count, mp_count):
        self.dp_count = dp_count
        self.total = dp_count * mp_count
        self.cube = dp_count == BLOCKS
        self.dp = lax.axis_index("dp").astype(jnp.int32)
        mp = lax.axis_index("mp").astype(jnp.int32)
        self.side = mp // 2
        self.core = mp % 2

    def swap(self, value, bit):
        pairs = [(i, i ^ bit) for i in range(self.total)]
        return lax.ppermute(value, ("dp", "mp"), pairs)

    def places(self):
        rows = []
        for name in NAMES:
            for j in range(2 * BLOCKS):
                if self.cube:
                    bits = 0
                    for k, bit in enumerate(ORDERS[name]):
                        bits ^= bit if (j >> k) & 1 else 0
                    rows.append((bits // SIDE & 1, bits // X_BIT))
                else:
                    rows.append((j // BLOCKS, j % BLOCKS))
        flips = np.array(rows, np.int32)
        mine = self.dp if self.cube else 0
        return (self.side ^ flips[:, 0]) * BLOCKS + (mine ^ flips[:, 1])

    def spread(self, share, name):
        if not self.cube:
            near = lax.all_gather(share, "dp", axis=0, tiled=True)
            near = near.reshape(BLOCKS, BLOCK_ROWS, share.shape[1])
            return near, self.swap(near, SIDE)
        near = share[None]
        for bit in ORDERS[name][:-1]:
            near = jnp.concatenate([near, self.swap(near, bit)], axis=0)
        return near, self.swap(near, ORDERS[name][-1])

    def fold(self, near, far, name):
        if not self.cube:
            whole = near.astype(WIDE) + self.swap(far, SIDE).astype(WIDE)
            whole = whole.reshape(D, near.shape[2])
            return lax.psum_scatter(whole, "dp", scatter_dimension=0, tiled=True)
        order = ORDERS[name]
        parts = [near, self.swap(far, order[3])]
        for k in (2, 1, 0):
            half = 2**k
            send = sum(part[half : 2 * half].astype(WIDE) for part in parts)
            parts.append(self.swap(send.astype(LOW), order[k]))
        return sum(part[0].astype(WIDE) for part in parts)

    def total_over(self, value, with_side):
        if self.cube:
            for bit in (X_BIT, Z_LOW, Z_HIGH):
                value = value + self.swap(value, bit)
        else:
            value = lax.psum(value, "dp")
        if with_side:
            value = value + self.swap(value, SIDE)
        return value

    def rows_of(self, share):
        if not self.cube:
            return lax.all_gather(share, "dp", axis=0, tiled=True)
        number = self.dp * 4
        for bit in (X_BIT, Z_LOW, Z_HIGH):
            other = self.swap(share, bit)
            upper = (number & bit) != 0
            share = jnp.where(
                upper,
                jnp.concatenate([other, share], axis=0),
                jnp.concatenate([share, other], axis=0),
            )
        return share

    def both_sides(self, share):
        other = self.swap(share, SIDE)
        return jnp.where(
            self.side == 1,
            jnp.concatenate([other, share], axis=0),
            jnp.concatenate([share, other], axis=0),
        )


def call(kernel, name, grid, in_specs, out_specs, out_shape, scratch, places, args, flops, vmem=56):
    moved = sum(a.size * a.dtype.itemsize for a in args)
    moved += sum(int(np.prod(s.shape)) * np.dtype(s.dtype).itemsize for s in out_shape)
    return pl.pallas_call(
        kernel,
        out_shape=out_shape,
        grid_spec=pltpu.PrefetchScalarGridSpec(
            num_scalar_prefetch=1,
            grid=grid,
            in_specs=in_specs,
            out_specs=out_specs,
            scratch_shapes=scratch,
        ),
        compiler_params=pltpu.CompilerParams(vmem_limit_bytes=vmem * MIB),
        cost_estimate=pl.CostEstimate(
            flops=int(flops), bytes_accessed=int(moved), transcendentals=0
        ),
        name=name,
    )(places, *args)


def whole(array):
    return pl.BlockSpec(array.shape, lambda *_: (0,) * len(array.shape))


def rows(count, width):
    return pl.BlockSpec((count, width), lambda i, *_: (i, 0))


def shape(dims, kind):
    return jax.ShapeDtypeStruct(dims, kind)


def place_at(places, name, j):
    return places[1 + 2 * BLOCKS * NAMES.index(name) + j]


def gather_blocks(places, name, near, far, held):
    for j in range(2 * BLOCKS):
        source = near if j < BLOCKS else far
        held[place_at(places, name, j)] = source[j % BLOCKS]


def scatter_blocks(places, name, held, near, far):
    for j in range(2 * BLOCKS):
        target = near if j < BLOCKS else far
        target[j % BLOCKS] = held[place_at(places, name, j)]


def to_pairs(held):
    left = held[0:BLOCKS].reshape(D, held.shape[2])
    right = held[BLOCKS : 2 * BLOCKS].reshape(D, held.shape[2])
    return jnp.concatenate([left[:, :128], right[:, :128], left[:, 128:], right[:, 128:]], axis=1)


def from_pairs(value, held):
    left = jnp.concatenate([value[:, 0:128], value[:, 256:320]], axis=1)
    right = jnp.concatenate([value[:, 128:256], value[:, 320:384]], axis=1)
    held[0:BLOCKS] = left.reshape(BLOCKS, BLOCK_ROWS, 192)
    held[BLOCKS : 2 * BLOCKS] = right.reshape(BLOCKS, BLOCK_ROWS, 192)


def project_kernel(places, x, bias, qn, qf, kn, kf, vn, vf, q, k, v, w, held):
    @pl.when(pl.program_id(0) == 0)
    def _():
        for i, (name, near, far) in enumerate(
            (("query", qn, qf), ("key", kn, kf), ("value", vn, vf))
        ):
            gather_blocks(places, name, near, far, held)
            w[i] = to_pairs(held)

    left = x[...]
    q[...] = (dot(left, w[0]) + bias[0:1, :]).astype(LOW)
    k[...] = dot(left, w[1]).astype(LOW)
    v[...] = (dot(left, w[2]) + bias[1:2, :]).astype(LOW)


def project(places, tokens, bias, q_parts, k_parts, v_parts):
    step = 256
    args = (tokens, bias, *q_parts, *k_parts, *v_parts)
    return call(
        project_kernel,
        "project",
        (LEN // step,),
        [pl.BlockSpec((step, D), lambda i, places: (places[0] * (LEN // step) + i, 0))]
        + [whole(a) for a in args[1:]],
        [rows(step, 384)] * 3 + [pl.BlockSpec((3, D, 384), lambda *_: (0, 0, 0))],
        [shape((LEN, 384), LOW)] * 3 + [shape((3, D, 384), LOW)],
        [pltpu.VMEM((2 * BLOCKS, BLOCK_ROWS, 192), LOW)],
        places,
        args,
        2 * LEN * D * 1152,
    )


def first_of_pair():
    return lax.broadcasted_iota(jnp.int32, (1, 128), 1) < HD


def attend_kernel(places, q_ref, k_ref, v_ref, o_ref, inv_ref, p_ref, vx):
    first = first_of_pair()
    zero, one = jnp.zeros((), LOW), jnp.ones((), LOW)
    k = k_ref[...]
    v = v_ref[...]
    n = k.shape[0]
    vx[0:n, 0:128] = jnp.where(first, v, zero)
    vx[n : 2 * n, 0:128] = jnp.where(first, zero, v)
    vx[0:n, 128:256] = jnp.broadcast_to(jnp.where(first, one, zero), (n, 128))
    vx[n : 2 * n, 128:256] = jnp.broadcast_to(jnp.where(first, zero, one), (n, 128))
    step = 256
    for i in range(n // step):
        at = pl.ds(i * step, step)
        q = q_ref[at, :]
        result = None
        for head in range(2):
            mine = jnp.where(first, q, zero) if head == 0 else jnp.where(first, zero, q)
            score = dot_nt(mine, k)
            top = jnp.max(score, axis=1, keepdims=True)
            weight = jnp.exp2((score - top) * (HD**-0.5 * LOG2_E)).astype(LOW)
            p_ref[head, at, :] = weight
            part = dot(weight, vx[head * n : (head + 1) * n, :])
            result = part if result is None else result + part
        inv = 1.0 / result[:, 128:256]
        inv_ref[at, :] = inv
        o_ref[at, :] = (result[:, 0:128] * inv).astype(LOW)


def attend(places, q, k, v):
    pair = pl.BlockSpec((LEN, 128), lambda i, *_: (0, i))
    return call(
        attend_kernel,
        "attend_forward",
        (3,),
        [pair] * 3,
        [pair, pair, pl.BlockSpec((2, LEN, LEN), lambda i, *_: (i, 0, 0))],
        [shape((LEN, 384), LOW), shape((LEN, 384), WIDE), shape((6, LEN, LEN), LOW)],
        [pltpu.VMEM((2 * LEN, 256), LOW)],
        places,
        (q, k, v),
        4 * 6 * LEN * LEN * 256,
    )


def out_kernel(places, o, near, far, z, w, held):
    @pl.when(pl.program_id(0) == 0)
    def _():
        gather_blocks(places, "out", near, far, held)
        w[...] = to_pairs(held)

    z[...] = dot_nt(o[...], w[...]).astype(LOW)


def project_out(places, o, parts):
    step = 256
    return call(
        out_kernel,
        "project_out",
        (LEN // step,),
        [rows(step, 384)] + [whole(a) for a in parts],
        [rows(step, D), pl.BlockSpec((D, 384), lambda *_: (0, 0))],
        [shape((LEN, D), LOW), shape((D, 384), LOW)],
        [pltpu.VMEM((2 * BLOCKS, BLOCK_ROWS, 192), LOW)],
        places,
        (o, *parts),
        2 * LEN * D * 384,
    )


def normalize(hidden):
    centred = hidden - jnp.mean(hidden, axis=-1, keepdims=True)
    spread = lax.rsqrt(jnp.mean(centred * centred, axis=-1, keepdims=True) + EPS_NORM)
    return centred * spread, spread


def norm_back(grad_normed, normed, spread):
    return spread * (
        grad_normed
        - jnp.mean(grad_normed, axis=-1, keepdims=True)
        - normed * jnp.mean(grad_normed * normed, axis=-1, keepdims=True)
    )


def up_kernel(places, x, z, zp, vec, bias, near, far, m, slope, n1, rs1, low, w, held):
    @pl.when(pl.program_id(0) == 0)
    def _():
        gather_blocks(places, "up", near, far, held)
        w[:, 0:D] = held[0:BLOCKS].reshape(D, D)
        w[:, D : 2 * D] = held[BLOCKS : 2 * BLOCKS].reshape(D, D)

    total = z[...].astype(WIDE) + zp[...].astype(WIDE)
    normed, spread = normalize(x[...].astype(WIDE) + total + vec[4:5, :])
    n1[...] = normed
    rs1[...] = jnp.broadcast_to(spread, rs1.shape)
    middle = (normed * vec[0:1, :] + vec[1:2, :]).astype(LOW)
    low[...] = middle
    for c in range(4):
        at = pl.ds(c * 384, 384)
        u = dot(middle, w[:, at]) + bias[0:1, at]
        half = 0.5 * (1.0 + lax.erf(u * 0.7071067811865476))
        m[:, at] = (u * half).astype(LOW)
        slope[:, at] = (half + u * (jnp.exp(-0.5 * u * u) * 0.3989422804014327)).astype(LOW)


def feed_up(places, tokens, z, zp, vec, bias, parts):
    step = 256
    args = (tokens, z, zp, vec, bias, *parts)
    return call(
        up_kernel,
        "feed_up",
        (LEN // step,),
        [pl.BlockSpec((step, D), lambda i, places: (places[0] * (LEN // step) + i, 0))]
        + [rows(step, D)] * 2
        + [whole(a) for a in args[3:]],
        [rows(step, 2 * D)] * 2
        + [rows(step, D), rows(step, 128), rows(step, D)]
        + [pl.BlockSpec((D, 2 * D), lambda *_: (0, 0))],
        [shape((LEN, 2 * D), LOW)] * 2
        + [shape((LEN, D), WIDE), shape((LEN, 128), WIDE), shape((LEN, D), LOW)]
        + [shape((D, 2 * D), LOW)],
        [pltpu.VMEM((2 * BLOCKS, BLOCK_ROWS, D), LOW)],
        places,
        args,
        2 * LEN * D * 2 * D,
    )


def down_kernel(places, m, near, far, f, w, held):
    @pl.when(pl.program_id(0) == 0)
    def _():
        gather_blocks(places, "down", near, far, held)
        w[:, 0:D] = held[0:BLOCKS].reshape(D, D)
        w[:, D : 2 * D] = held[BLOCKS : 2 * BLOCKS].reshape(D, D)

    f[...] = dot_nt(m[...], w[...]).astype(LOW)


def feed_down(places, m, parts):
    step = 256
    return call(
        down_kernel,
        "feed_down",
        (LEN // step,),
        [rows(step, 2 * D)] + [whole(a) for a in parts],
        [rows(step, D), pl.BlockSpec((D, 2 * D), lambda *_: (0, 0))],
        [shape((LEN, D), LOW), shape((D, 2 * D), LOW)],
        [pltpu.VMEM((2 * BLOCKS, BLOCK_ROWS, D), LOW)],
        places,
        (m, *parts),
        2 * LEN * D * 2 * D,
    )


def turn_kernel(
    places, facts, n1, f, fp, cot, vec, pool_a, pool_b, classes, bias, y, dh2, low, sums, ramp, pool
):
    step = pl.program_id(0)
    middle = n1[...] * vec[0:1, :] + vec[1:2, :]
    total = f[...].astype(WIDE) + fp[...].astype(WIDE)
    normed, spread = normalize(middle + total + vec[5:6, :])
    result = normed * vec[2:3, :] + vec[3:4, :]
    y[...] = result.astype(LOW)
    grad = cot[...].astype(WIDE) * facts[2]
    dh2[...] = grad

    @pl.when(step == 0)
    def _():
        sums[...] = jnp.zeros_like(sums)
        half = D // 2
        own = places[0 + 1 + 2 * BLOCKS * len(NAMES)]

        @pl.when(own == 0)
        def _():
            pool[:, 0:half] = pool_a[...]
            pool[:, half:D] = pool_b[...]

        @pl.when(own == 1)
        def _():
            pool[:, 0:half] = pool_b[...]
            pool[:, half:D] = pool_a[...]

        count = 16
        head = result[0:count, :].astype(LOW)
        pooled = jnp.tanh(dot(head, pool[...]) + vec[6:7, :])
        pooled_low = pooled.astype(LOW)
        lane = lax.broadcasted_iota(jnp.int32, (count, 128), 1)
        row = lax.broadcasted_iota(jnp.int32, (count, 128), 0)
        valid = lane < 3
        logits = dot(pooled_low, classes[...]) + bias[0:1, :]
        top = jnp.max(jnp.where(valid, logits, -jnp.inf), axis=1, keepdims=True)
        shifted = logits - top
        log_sum = jnp.log(
            jnp.sum(jnp.where(valid, jnp.exp(shifted), 0.0), axis=1, keepdims=True)
        )
        log_probs = jnp.where(valid, shifted - log_sum, 0.0)
        probs = jnp.where(valid, jnp.exp(log_probs), 0.0)
        live = facts[1]
        entropy = -live * jnp.sum(probs * log_probs, axis=1, keepdims=True)
        label = facts[0].astype(jnp.int32)
        onehot = jnp.where(lane == label, 1.0, 0.0)
        grad_logits = live * (probs - onehot) / facts[3]
        grad_logits = jnp.where(valid & (row == 0), grad_logits, 0.0).astype(LOW)
        grad_pre = (dot_nt(grad_logits, classes[...]) * (1.0 - pooled * pooled)).astype(LOW)
        grad_head = dot_nt(grad_pre, pool[...])
        dh2[0:count, :] = dh2[0:count, :] + grad_head
        sums[3:4, :] = grad_pre[0:1, :].astype(WIDE)
        of_class = dot_tn(grad_logits, pooled_low)
        sums[4:7, :] = of_class[0:3, :]
        last = jnp.where(lane == 3, entropy, grad_logits.astype(WIDE))
        sums[7:8, 0:128] = last[0:1, :]
        wide_row = lax.broadcasted_iota(jnp.int32, (count, D), 0)
        second = jnp.broadcast_to(grad_pre[0:1, :].astype(WIDE), (count, D))
        kept = jnp.where(wide_row == 0, head.astype(WIDE), 0.0)
        ramp[...] = jnp.where(wide_row == 1, second, kept).astype(LOW)

    grad = dh2[...]
    sums[0:1, :] += jnp.sum(grad * normed, axis=0, keepdims=True)
    sums[1:2, :] += jnp.sum(grad, axis=0, keepdims=True)
    back = norm_back(grad * vec[2:3, :], normed, spread)
    sums[2:3, :] += jnp.sum(back, axis=0, keepdims=True)
    dh2[...] = back
    low[...] = back.astype(LOW)


def turn(places, facts, n1, f, fp, cotangent, vec, pool_a, pool_b, classes, bias):
    step = 256
    args = (facts, n1, f, fp, cotangent, vec, pool_a, pool_b, classes, bias)
    return call(
        turn_kernel,
        "turn",
        (LEN // step,),
        [pl.BlockSpec(memory_space=pltpu.SMEM)]
        + [rows(step, D)] * 3
        + [pl.BlockSpec((step, D), lambda i, places: (places[0] * (LEN // step) + i, 0))]
        + [whole(a) for a in args[5:]],
        [rows(step, D)] * 3
        + [pl.BlockSpec((8, D), lambda *_: (0, 0)), pl.BlockSpec((16, D), lambda *_: (0, 0))],
        [shape((LEN, D), LOW), shape((LEN, D), WIDE), shape((LEN, D), LOW)]
        + [shape((8, D), WIDE), shape((16, D), LOW)],
        [pltpu.VMEM((D, D), LOW)],
        places,
        args,
        LEN * D * 60,
    )


def feed_back_kernel(places, dh2, slope, w_down, w_up, du, dx, sums):
    grad = dot(dh2[...], w_down[...]) * slope[...].astype(WIDE)
    grad = grad.astype(LOW)
    du[...] = grad
    dx[...] = dot_nt(grad, w_up[...]).astype(LOW)

    @pl.when(pl.program_id(0) == 0)
    def _():
        sums[...] = jnp.zeros_like(sums)

    sums[0:1, :] += jnp.sum(grad.astype(WIDE), axis=0, keepdims=True)


def feed_back(places, dh2, slope, w_down, w_up):
    step = 256
    args = (dh2, slope, w_down, w_up)
    return call(
        feed_back_kernel,
        "feed_back",
        (LEN // step,),
        [rows(step, D), rows(step, 2 * D), whole(w_down), whole(w_up)],
        [rows(step, 2 * D), rows(step, D), pl.BlockSpec((8, 2 * D), lambda *_: (0, 0))],
        [shape((LEN, 2 * D), LOW), shape((LEN, D), LOW), shape((8, 2 * D), WIDE)],
        [],
        places,
        args,
        4 * LEN * D * 2 * D,
    )


def feed_grad_kernel(name, places, left, right, near, far, held, turned):
    @pl.when(pl.program_id(0) == 0)
    def _():
        turned[...] = left[...].T

    side = pl.program_id(0)
    for c in range(3):
        at = pl.ds(c * 256, 256)
        part = dot(turned[...], right[:, at]).astype(LOW)
        held[pl.ds(pl.multiple_of(side * BLOCKS, BLOCKS), BLOCKS), :, at] = part.reshape(
            BLOCKS, BLOCK_ROWS, 256
        )

    @pl.when(side == 1)
    def _():
        scatter_blocks(places, name, held, near, far)


def feed_grad(places, name, left, right):
    return call(
        functools.partial(feed_grad_kernel, name),
        "feed_grad_" + name,
        (2,),
        [whole(left), pl.BlockSpec((LEN, D), lambda i, *_: (0, i))],
        [pl.BlockSpec((BLOCKS, BLOCK_ROWS, D), lambda *_: (0, 0, 0))] * 2,
        [shape((BLOCKS, BLOCK_ROWS, D), LOW)] * 2,
        [pltpu.VMEM((2 * BLOCKS, BLOCK_ROWS, D), LOW), pltpu.VMEM((D, LEN), LOW)],
        places,
        (left, right),
        2 * LEN * D * 2 * D,
    )


def mid_kernel(places, dh2, dx, dxp, n1, rs1, vec, w_out, dh1, low, do, sums):
    @pl.when(pl.program_id(0) == 0)
    def _():
        sums[...] = jnp.zeros_like(sums)

    total = dx[...].astype(WIDE) + dxp[...].astype(WIDE)
    grad = dh2[...] + total
    normed = n1[...]
    sums[0:1, :] += jnp.sum(grad * normed, axis=0, keepdims=True)
    sums[1:2, :] += jnp.sum(grad, axis=0, keepdims=True)
    back = norm_back(grad * vec[0:1, :], normed, rs1[:, 0:1])
    sums[2:3, :] += jnp.sum(back, axis=0, keepdims=True)
    dh1[...] = back
    back_low = back.astype(LOW)
    low[...] = back_low
    do[...] = dot(back_low, w_out[...]).astype(LOW)


def mid(places, dh2, dx, dxp, n1, rs1, vec, w_out):
    step = 256
    args = (dh2, dx, dxp, n1, rs1, vec, w_out)
    return call(
        mid_kernel,
        "middle_back",
        (LEN // step,),
        [rows(step, D)] * 4 + [rows(step, 128), whole(vec), whole(w_out)],
        [rows(step, D)] * 2 + [rows(step, 384), pl.BlockSpec((8, D), lambda *_: (0, 0))],
        [shape((LEN, D), WIDE), shape((LEN, D), LOW), shape((LEN, 384), LOW), shape((8, D), WIDE)],
        [],
        places,
        args,
        2 * LEN * D * 384,
    )


def attend_back_kernel(
    places, q_ref, k_ref, v_ref, do_ref, inv_ref, p_ref, dq_ref, dk_ref, dv_ref, ds_ref, held
):
    first = first_of_pair()
    zero = jnp.zeros((), LOW)
    n = k_ref.shape[0]
    k = k_ref[...]
    v = v_ref[...]
    k_own = [jnp.where(first, k, zero), jnp.where(first, zero, k)]
    scaled = (do_ref[...].astype(WIDE) * inv_ref[...]).astype(LOW)
    held[...] = scaled
    step = 256
    for i in range(n // step):
        at = pl.ds(i * step, step)
        d = held[at, :]
        total = None
        for head in range(2):
            mine = jnp.where(first, d, zero) if head == 0 else jnp.where(first, zero, d)
            grad_weight = dot_nt(mine, v)
            weight = p_ref[head, at, :].astype(WIDE)
            product = weight * grad_weight
            inner = jnp.sum(product, axis=1, keepdims=True)
            inner = inner * inv_ref[at, pl.ds(HD * head, 1)]
            grad_score = (product - weight * inner).astype(LOW)
            ds_ref[head, at, :] = grad_score
            part = dot(grad_score, k_own[head])
            total = part if total is None else total + part
        dq_ref[at, :] = (total * HD**-0.5).astype(LOW)
    scaled_t = scaled.T
    q_t = q_ref[...].T
    grad_v = jnp.concatenate(
        [dot(scaled_t[0:HD], p_ref[0]), dot(scaled_t[HD : 2 * HD], p_ref[1])], axis=0
    )
    dv_ref[...] = grad_v.T.astype(LOW)
    grad_k = jnp.concatenate(
        [dot(q_t[0:HD], ds_ref[0]), dot(q_t[HD : 2 * HD], ds_ref[1])], axis=0
    )
    dk_ref[...] = (grad_k * HD**-0.5).T.astype(LOW)


def attend_back(places, q, k, v, do, inv, p):
    pair = pl.BlockSpec((LEN, 128), lambda i, *_: (0, i))
    return call(
        attend_back_kernel,
        "attend_backward",
        (3,),
        [pair] * 5 + [pl.BlockSpec((2, LEN, LEN), lambda i, *_: (i, 0, 0))],
        [pair] * 3,
        [shape((LEN, 384), LOW)] * 3,
        [pltpu.VMEM((2, LEN, LEN), LOW), pltpu.VMEM((LEN, 128), LOW)],
        places,
        (q, k, v, do, inv, p),
        8 * 6 * LEN * LEN * 256,
    )


def narrow_grad_kernel(names, places, left, *refs):
    count = len(names)
    rights, outs, sums = refs[:count], refs[count : 3 * count], refs[3 * count]
    held, turned = refs[3 * count + 1 :]
    turned[...] = left[...].T
    for i, name in enumerate(names):
        from_pairs(dot(turned[...], rights[i][...]).astype(LOW), held)
        scatter_blocks(places, name, held, outs[2 * i], outs[2 * i + 1])
        sums[i : i + 1, :] = jnp.sum(rights[i][...].astype(WIDE), axis=0, keepdims=True)


def narrow_grad(places, names, left, rights, from_side):
    count = len(names)
    own = pl.BlockSpec((LEN, D), (lambda i, places: (places[0], 0)) if from_side else (lambda *_: (0, 0)))
    half = pl.BlockSpec((BLOCKS, BLOCK_ROWS, 192), lambda *_: (0, 0, 0))
    return call(
        functools.partial(narrow_grad_kernel, names),
        "narrow_grad_" + names[0],
        (1,),
        [own] + [whole(a) for a in rights],
        [half] * (2 * count) + [pl.BlockSpec((8, 384), lambda *_: (0, 0))],
        [shape((BLOCKS, BLOCK_ROWS, 192), LOW)] * (2 * count) + [shape((8, 384), WIDE)],
        [pltpu.VMEM((2 * BLOCKS, BLOCK_ROWS, 192), LOW), pltpu.VMEM((D, LEN), LOW)],
        places,
        (left, *rights),
        2 * LEN * D * 384 * count,
    )


def input_kernel(places, dq, dk, dv, w, out):
    total = dot_nt(dq[...], w[0]) + dot_nt(dk[...], w[1]) + dot_nt(dv[...], w[2])
    out[...] = total.astype(LOW)


def input_grad(places, dq, dk, dv, w):
    step = 256
    return call(
        input_kernel,
        "input_grad",
        (LEN // step,),
        [rows(step, 384)] * 3 + [whole(w)],
        [rows(step, D)],
        [shape((LEN, D), LOW)],
        [],
        places,
        (dq, dk, dv, w),
        2 * LEN * D * 1152,
    )[0]


def both_sequences(links, mine):
    half = LEN // 2
    own_half = lax.dynamic_slice_in_dim(mine, links.core * half, half, 0)
    other_half = links.swap(own_half, SIDE)
    last_half = links.swap(other_half, CORE)
    other = jnp.where(
        links.core == 0,
        jnp.concatenate([other_half, last_half], axis=0),
        jnp.concatenate([last_half, other_half], axis=0),
    )
    return jnp.where(
        links.side == 0,
        jnp.concatenate([mine, other], axis=0),
        jnp.concatenate([other, mine], axis=0),
    )


def per_device(
    dp_count,
    mp_count,
    tokens,
    cotangent,
    exit_layer,
    labels,
    qkv_weight,
    qkv_first,
    qkv_second,
    out_weight,
    out_first,
    out_second,
    up_weight,
    up_first,
    up_second,
    down_weight,
    down_first,
    down_second,
    pool_weight,
    pool_first,
    pool_second,
    qv_bias,
    qv_first,
    qv_second,
    up_bias,
    upb_first,
    upb_second,
    layer_vectors,
    vector_first,
    vector_second,
    class_weight,
    class_first,
    class_second,
):
    links = Links(dp_count, mp_count)
    side, core = links.side, links.core

    places = jnp.concatenate([side[None], links.places(), core[None]]).astype(jnp.int32)

    qkv_low = qkv_weight.astype(LOW)
    q_parts = links.spread(qkv_low[:, 0], "query")
    k_parts = links.spread(qkv_low[:, 1], "key")
    v_parts = links.spread(qkv_low[:, 2], "value")
    biases = links.both_sides(
        jnp.concatenate([qv_bias.reshape(1, 384), up_bias.reshape(1, D)], axis=1)
    )
    qv_pairs = jnp.stack(
        [
            jnp.concatenate(
                [
                    biases[0, 192 * i : 192 * i + 128],
                    biases[1, 192 * i : 192 * i + 128],
                    biases[0, 192 * i + 128 : 192 * i + 192],
                    biases[1, 192 * i + 128 : 192 * i + 192],
                ]
            )
            for i in range(2)
        ]
    )
    up_bias_both = biases[:, 384:].reshape(1, 2 * D)
    live_mask = (exit_layer >= LAYER).astype(WIDE)
    carry_mask = (exit_layer > LAYER).astype(WIDE)
    live_total = links.total_over(
        jnp.broadcast_to(jnp.sum(live_mask), (8, 128)), with_side=False
    )[0, 0]
    out_parts = links.spread(out_weight.T.astype(LOW), "out")
    up_parts = links.spread(up_weight.astype(LOW), "up")
    down_parts = links.spread(down_weight.T.astype(LOW), "down")
    pool_low = lax.dynamic_slice_in_dim(pool_weight.astype(LOW), core * (D // 2), D // 2, 1)
    pool_mine = links.rows_of(pool_low)
    pool_other = links.swap(pool_mine, CORE)

    q, k, v, w_qkv = project(places, tokens, qv_pairs, q_parts, k_parts, v_parts)
    o, inv, p = attend(places, q, k, v)
    z, w_out = project_out(places, o, out_parts)
    zp = links.swap(z, CORE)
    m, slope, n1, rs1, middle_low, w_up = feed_up(
        places, tokens, z, zp, layer_vectors, up_bias_both, up_parts
    )
    f, w_down = feed_down(places, m, down_parts)
    fp = links.swap(f, CORE)
    classes = jnp.pad(class_weight[:D].astype(LOW), ((0, 0), (0, 125)))
    class_bias = jnp.pad(class_weight[D:], ((0, 0), (0, 125)))
    facts = jnp.stack(
        [
            labels.astype(WIDE)[side],
            live_mask[side],
            carry_mask[side],
            live_total,
        ]
    )
    y, dh2, dh2_low, turn_sums, ramp = turn(
        places, facts, n1, f, fp, cotangent, layer_vectors, pool_mine, pool_other, classes, class_bias
    )
    result = both_sequences(links, y)

    du, dx, up_sums = feed_back(places, dh2_low, slope, w_down, w_up)
    dxp = links.swap(dx, CORE)
    down_near, down_far = feed_grad(places, "down", dh2_low, m)
    grad_down = links.fold(down_near, down_far, "down")
    up_near, up_far = feed_grad(places, "up", middle_low, du)
    grad_up = links.fold(up_near, up_far, "up")
    dh1, dh1_low, do, mid_sums = mid(places, dh2, dx, dxp, n1, rs1, layer_vectors, w_out)
    out_near, out_far, _ = narrow_grad(places, ("out",), dh1_low, (o,), False)
    grad_out = links.fold(out_near, out_far, "out")
    sums = links.total_over(
        jnp.concatenate([turn_sums, mid_sums[0:3], up_sums[0].reshape(2, D)], axis=0),
        with_side=True,
    )
    ramps = links.rows_of(links.both_sides(ramp[None]))
    dq, dk, dv = attend_back(places, q, k, v, do, inv, p)
    token_part = input_grad(places, dq, dk, dv, w_qkv)
    token_other = links.swap(token_part, CORE)
    qn, qf, kn, kf, vn, vf, pair_sums = narrow_grad(
        places, ("query", "key", "value"), tokens, (dq, dk, dv), True
    )
    grad_q = links.fold(qn, qf, "query")
    grad_k = links.fold(kn, kf, "key")
    grad_v = links.fold(vn, vf, "value")
    pair_total = links.total_over(pair_sums, with_side=True)
    token_sum = token_part.astype(WIDE) + token_other.astype(WIDE)
    tokens_grad = both_sequences(links, (dh1 + token_sum).astype(LOW))

    own_rows = lax.dynamic_slice_in_dim(
        ramps[:, 0, :], links.dp * (D // dp_count), D // dp_count, 1
    )
    grad_pool = lax.dot_general(
        own_rows, ramps[:, 1, :], (((0,), (0,)), ((), ())), preferred_element_type=WIDE
    )
    vector_sum = jnp.stack([sums[8], sums[9], sums[0], sums[1], sums[10], sums[2], sums[3]])
    class_sum = jnp.concatenate([sums[4:7].T, sums[7:8, 0:3]], axis=0)
    upb_sum = lax.dynamic_slice_in_dim(sums, 11 + side, 1, 0)[0]
    pair_rows = jnp.stack([pair_total[0], pair_total[2]])
    bias_sum = jnp.concatenate(
        [
            lax.dynamic_slice_in_dim(pair_rows, side * 128, 128, 1),
            lax.dynamic_slice_in_dim(pair_rows, 256 + side * 64, 64, 1),
        ],
        axis=1,
    )
    grad_qkv = jnp.stack([grad_q, grad_k, grad_v], axis=1)

    qkv_new, qkv_first_new, qkv_second_new = adamw(
        qkv_weight, qkv_first, qkv_second, grad_qkv, RATE * D ** (-0.5), DECAY
    )
    out_new, out_first_new, out_second_new = adamw(
        out_weight, out_first, out_second, grad_out.T, RATE * max(1, 2 * D // LEN) ** (-0.5), DECAY
    )
    up_new, up_first_new, up_second_new = adamw(
        up_weight, up_first, up_second, grad_up, RATE * D ** (-0.5), DECAY
    )
    down_new, down_first_new, down_second_new = adamw(
        down_weight, down_first, down_second, grad_down.T, RATE * FF ** (-0.5), DECAY
    )
    pool_new, pool_first_new, pool_second_new = adamw(
        pool_weight, pool_first, pool_second, grad_pool, RATE * D ** (-0.5), DECAY
    )
    qv_new, qv_first_new, qv_second_new = adamw(
        qv_bias, qv_first, qv_second, bias_sum, VECTOR_RATE, 0.0
    )
    upb_new, upb_first_new, upb_second_new = adamw(
        up_bias, upb_first, upb_second, upb_sum, VECTOR_RATE, 0.0
    )
    vector_new, vector_first_new, vector_second_new = adamw(
        layer_vectors, vector_first, vector_second, vector_sum, VECTOR_RATE, 0.0
    )
    class_new, class_first_new, class_second_new = adamw(
        class_weight, class_first, class_second, class_sum, RATE * (D // 4) ** (-0.5), DECAY
    )
    return (
        result,
        tokens_grad,
        sums[7, 3] / live_total,
        qkv_new,
        qkv_first_new,
        qkv_second_new,
        qkv_new.astype(LOW),
        out_new,
        out_first_new,
        out_second_new,
        out_new.astype(LOW),
        up_new,
        up_first_new,
        up_second_new,
        up_new.astype(LOW),
        down_new,
        down_first_new,
        down_second_new,
        down_new.astype(LOW),
        pool_new,
        pool_first_new,
        pool_second_new,
        pool_new.astype(LOW),
        qv_new,
        qv_first_new,
        qv_second_new,
        upb_new,
        upb_first_new,
        upb_second_new,
        vector_new,
        vector_first_new,
        vector_second_new,
        class_new,
        class_first_new,
        class_second_new,
    )


def solution(mesh):
    in_specs = (
        P("dp", None),
        P("dp", None),
        P("dp"),
        P("dp"),
        P("dp", None, "mp"),
        P("dp", None, "mp"),
        P("dp", None, "mp"),
        P("mp", "dp"),
        P("mp", "dp"),
        P("mp", "dp"),
        P("dp", "mp"),
        P("dp", "mp"),
        P("dp", "mp"),
        P("mp", "dp"),
        P("mp", "dp"),
        P("mp", "dp"),
        P("dp", None),
        P("dp", None),
        P("dp", None),
        P(None, "mp"),
        P(None, "mp"),
        P(None, "mp"),
        P("mp"),
        P("mp"),
        P("mp"),
        P(),
        P(),
        P(),
        P(),
        P(),
        P(),
    )
    out_specs = (
        P("dp", None),
        P("dp", None),
        P(),
        P("dp", None, "mp"),
        P("dp", None, "mp"),
        P("dp", None, "mp"),
        P("dp", None, "mp"),
        P("mp", "dp"),
        P("mp", "dp"),
        P("mp", "dp"),
        P("mp", "dp"),
        P("dp", "mp"),
        P("dp", "mp"),
        P("dp", "mp"),
        P("dp", "mp"),
        P("mp", "dp"),
        P("mp", "dp"),
        P("mp", "dp"),
        P("mp", "dp"),
        P("dp", None),
        P("dp", None),
        P("dp", None),
        P("dp", None),
        P(None, "mp"),
        P(None, "mp"),
        P(None, "mp"),
        P("mp"),
        P("mp"),
        P("mp"),
        P(),
        P(),
        P(),
        P(),
        P(),
        P(),
    )
    one_device = functools.partial(per_device, mesh.shape["dp"], mesh.shape["mp"])
    return jax.shard_map(
        one_device, mesh=mesh, in_specs=in_specs, out_specs=out_specs, check_vma=False
    )
```

time: 872 us -> 464 us (0.53)
  waiting for transfers between devices: 382 us -> 161 us
  Pallas kernels: 0 us -> 133 us
  blocking collectives: 133 us -> 0 us
  matrix products: 135 us -> 2.59 us
  starting transfers between devices: 1.75 us -> 86.6 us
  other arithmetic: 108 us -> 48.7 us
  local copies, waits for them, and re-layouts: 62.8 us -> 22.2 us
  loops' own time: 19.9 us -> 0 us
  between operations: 19.9 us -> 4.68 us
    reduce_scatter x4 -> x0, waiting for transfers between devices: 208 us -> none  [the longest x1 69.6 us: per_device(): lax.psum_scatter(grad_pool, 'dp', scatter_dimension=0, tiled=True)]
    psum x4 -> x0, waiting for transfers between devices: 174 us -> none  [the longest x1 64.4 us: per_device(): lax.psum(jnp.dot(attended, out_full, preferred_element_type=jnp.float32)....]
    ppermute x0 -> x76, waiting for transfers between devices: none -> 161 us  [swap(): return lax.ppermute(value, ('dp', 'mp'), pairs)]
    pallas_call x0 -> x14, Pallas kernels: none -> 133 us  [call(): pl.pallas_call(kernel, out_shape=out_shape, grid_spec=pltpu.PrefetchScala...]
    dot_general x45 -> x1, matrix products: 132 us -> 2.59 us  [per_device(): lax.dot_general(own_rows, ramps[:, 1, :], (((0,), (0,)), ((), ())), prefe...]
    ppermute x0 -> x76, starting transfers between devices: none -> 86.6 us  [swap(): return lax.ppermute(value, ('dp', 'mp'), pairs)]
    all_gather x2 -> x0, blocking collectives: 72.4 us -> none  [the longest x1 39.1 us: per_device(): lax.all_gather(qkv_weight.astype(jnp.bfloat16), 'dp', axis=0, tiled=True)]
    psum x2 -> x0, blocking collectives: 61 us -> none  [per_device(): lax.psum((jnp.sum(live_mask), entropy_local), 'dp')]
  transfers between devices with their start and end apart: 12 -> 76, of which waited for: 6 -> 23; matrix products, arithmetic and copies ran while one was open for 19% -> 14% of each run, Pallas kernels for 0% -> 27%
where the time goes in v1:
time: 464 us; the launch traced here: 459 us
  waiting for transfers between devices  161 us (35%)
  Pallas kernels  133 us (29%)
  starting transfers between devices  86.6 us (19%)
  other arithmetic  48.7 us (10%)
  local copies, waits for them, and re-layouts  22.2 us (5%)
  between operations  4.68 us (1%)
    ppermute x76, waiting for transfers between devices, swap(): return lax.ppermute(value, ('dp', 'mp'), pairs)  161 us
    pallas_call x14, Pallas kernels, call(): pl.pallas_call(kernel, out_shape=out_shape, grid_spec=pltpu.PrefetchScala...  133 us
    ppermute x76, starting transfers between devices, swap(): return lax.ppermute(value, ('dp', 'mp'), pairs)  86.6 us
    convert_element_type x18, other arithmetic, fold(): parts.append(self.swap(send.astype(LOW), order[k]))  13.8 us
    unnamed x136, local copies, waits for them, and re-layouts  12 us
  transfers between devices with their start and end apart: 76, of which 23 were waited for; matrix products, arithmetic and copies ran while one was open for 14% of the time, Pallas kernels for 27%

profile of v1, /device:TPU:0, one launch (start us, length us, event | category | flops | bytes accessed | tf_op | source)
XLA Modules:
  0.0 458.9 jit_solution(15612818603240286123)
XLA Ops:
  24.9 8.0 %collective-permute-done.9 = bf16[2,96,192]{2,1,0:T(8,128)(2,1)S(1)} collective-permute-done((bf16[2,96,192]{2,1,0:T(8,128)(2,1)S(1)}, bf16[2,96,192]{2,1,0:T(8,128)(2,1)S(1)}, u32[]{:S(2)}, u32[]{:S(2)}) %collective-permute-start.9) | collective-permute-done | bytes 73760 | tf_op jit(solution)/shard_map/ppermute | solution.py:85
  39.8 6.0 %collective-permute-done.14 = bf16[4,96,192]{2,1,0:T(8,128)(2,1)S(1)} collective-permute-done((bf16[4,96,192]{2,1,0:T(8,128)(2,1)S(1)}, bf16[4,96,192]{2,1,0:T(8,128)(2,1)S(1)}, u32[]{:S(2)}, u32[]{:S(2)}) %collective-permute-start.14) | collective-permute-done | bytes 147488 | tf_op jit(solution)/shard_map/ppermute | solution.py:85
  55.6 5.5 %collective-permute-done.26 = bf16[2,96,768]{2,1,0:T(8,128)(2,1)S(1)} collective-permute-done((bf16[2,96,768]{2,1,0:T(8,128)(2,1)S(1)}, bf16[2,96,768]{2,1,0:T(8,128)(2,1)S(1)}, u32[]{:S(2)}, u32[]{:S(2)}) %collective-permute-start.26) | collective-permute-done | bytes 294944 | tf_op jit(solution)/shard_map/ppermute | solution.py:85
  63.1 6.5 %collective-permute-done.15.vf = bf16[8,96,192]{2,1,0:T(8,128)(2,1)S(1)} collective-permute-done((bf16[8,96,192]{2,1,0:T(8,128)(2,1)S(1)}, bf16[8,96,192]{2,1,0:T(8,128)(2,1)S(1)}, u32[]{:S(2)}, u32[]{:S(2)}) %collective-permute-start.15) | collective-permute-done | bytes 294944 | tf_op jit(solution)/shard_map/ppermute | solution.py:85
  72.4 8.3 %project.1 = (bf16[1024,384]{1,0:T(8,128)(2,1)}, bf16[1024,384]{1,0:T(8,128)(2,1)}, bf16[1024,384]{1,0:T(8,128)(2,1)}, bf16[3,768,384]{2,1,0:T(8,128)(2,1)}) custom-call(s32[98]{0:T(128)} %pad_add_fusion.places, bf16[2048,768]{1,0:T(8,128)(2,1)} %left.1, f32[2,384]{1,0:T(2,128)} %pad_maximum_fusion.22.bias, bf16[8,96,192]{2,1,0:T(8,128)(2,1)} %copy-done.16, ...), custom_call_target="tpu_custom_call" | custom-call | flops 1811939328 | bytes 9047040 | tf_op jit(solution)/shard_map/project/pallas_call | solution.py:161
  80.7 14.1 %attend_forward.1 = (bf16[1024,384]{1,0:T(8,128)(2,1)}, f32[1024,384]{1,0:T(8,128)}, bf16[6,1024,1024]{2,1,0:T(8,128)(2,1)}) custom-call(s32[98]{0:T(128)} %pad_add_fusion.places, bf16[1024,384]{1,0:T(8,128)(2,1)} %get-tuple-element.80.q_ref, bf16[1024,384]{1,0:T(8,128)(2,1)} %get-tuple-element.81.k_ref, bf16[1024,384]{1,0:T(8,128)(2,1)} %get-tuple-element.82.v_ref), custom_call_target="tpu_custom_call" | custom-call | flops 6442450944 | bytes 17301504 | tf_op jit(solution)/shard_map/attend_forward/pallas_call | solution.py:161
  95.5 5.4 %project_out.1 = (bf16[1024,768]{1,0:T(8,128)(2,1)}, bf16[768,384]{1,0:T(8,128)(2,1)}) custom-call(s32[98]{0:T(128)} %pad_add_fusion.places, bf16[1024,384]{1,0:T(8,128)(2,1)} %get-tuple-element.83.o.refs_0_, bf16[8,96,192]{2,1,0:T(8,128)(2,1)} %copy-done.17, bf16[8,96,192]{2,1,0:T(8,128)(2,1)} %copy-done.59), custom_call_target="tpu_custom_call" | custom-call | flops 603979776 | bytes 3538944 | tf_op jit(solution)/shard_map/project_out/pallas_call | solution.py:161
  105.8 23.8 %collective-permute-done.24.far = bf16[8,96,768]{2,1,0:T(8,128)(2,1)} collective-permute-done((bf16[8,96,768]{2,1,0:T(8,128)(2,1)S(1)}, bf16[8,96,768]{2,1,0:T(8,128)(2,1)}, u32[]{:S(2)}, u32[]{:S(2)}) %collective-permute-start.24) | collective-permute-done | bytes 1179680 | tf_op jit(solution)/shard_map/ppermute | solution.py:85
  129.6 11.9 %feed_up.1 = (bf16[1024,1536]{1,0:T(8,128)(2,1)}, bf16[1024,1536]{1,0:T(8,128)(2,1)}, f32[1024,768]{1,0:T(8,128)}, f32[1024,128]{1,0:T(8,128)}, bf16[1024,768]{1,0:T(8,128)(2,1)}, /*index=5*/bf16[768,1536]{1,0:T(8,128)(2,1)}) custom-call(s32[98]{0:T(128)} %pad_add_fusion.places, bf16[2048,768]{1,0:T(8,128)(2,1)} %left.1, ...), custom_call_target="tpu_custom_call" | custom-call | flops 2415919104 | bytes 22572032 | tf_op jit(solution)/shard_map/feed_up/pallas_call | solution.py:161
  141.5 8.1 %feed_down.1 = (bf16[1024,768]{1,0:T(8,128)(2,1)}, bf16[768,1536]{1,0:T(8,128)(2,1)}) custom-call(s32[98]{0:T(128)} %pad_add_fusion.places, bf16[1024,1536]{1,0:T(8,128)(2,1)} %get-tuple-element.86.m.right, bf16[8,96,768]{2,1,0:T(8,128)(2,1)} %copy-done.8, bf16[8,96,768]{2,1,0:T(8,128)(2,1)} %collective-permute-done.28.far), custom_call_target="tpu_custom_call" | custom-call | flops 2415919104 | bytes 9437184 | tf_op jit(solution)/shard_map/feed_down/pallas_call | solution.py:161
  151.6 5.4 %collective-permute-done.31 = bf16[192,384]{1,0:T(8,128)(2,1)S(1)} collective-permute-done((bf16[192,384]{1,0:T(8,128)(2,1)S(1)}, bf16[192,384]{1,0:T(8,128)(2,1)S(1)}, u32[]{:S(2)}, u32[]{:S(2)}) %collective-permute-start.31) | collective-permute-done | bytes 147488 | tf_op jit(solution)/shard_map/ppermute | solution.py:85
  162.0 11.0 %collective-permute-done.32 = bf16[384,384]{1,0:T(8,128)(2,1)S(1)} collective-permute-done((bf16[384,384]{1,0:T(8,128)(2,1)S(1)}, bf16[384,384]{1,0:T(8,128)(2,1)S(1)}, u32[]{:S(2)}, u32[]{:S(2)}) %collective-permute-start.32) | collective-permute-done | bytes 294944 | tf_op jit(solution)/shard_map/ppermute | solution.py:85
  190.5 10.2 %turn.1 = (bf16[1024,768]{1,0:T(8,128)(2,1)}, f32[1024,768]{1,0:T(8,128)}, bf16[1024,768]{1,0:T(8,128)(2,1)}, f32[8,768]{1,0:T(8,128)}, bf16[16,768]{1,0:T(8,128)(2,1)}) custom-call(s32[98]{0:T(128)} %pad_add_fusion.places, f32[4]{0:T(128)} %pad_maximum_fusion.26.facts, f32[1024,768]{1,0:T(8,128)} %get-tuple-element.85.n1, ...), custom_call_target="tpu_custom_call" | custom-call | flops 47185920 | bytes 17176080 | tf_op jit(solution)/shard_map/turn/pallas_call | solution.py:161
  201.3 11.3 %feed_back.1 = (bf16[1024,1536]{1,0:T(8,128)(2,1)}, bf16[1024,768]{1,0:T(8,128)(2,1)}, f32[8,1536]{1,0:T(8,128)}) custom-call(s32[98]{0:T(128)} %pad_add_fusion.places, bf16[1024,768]{1,0:T(8,128)(2,1)} %get-tuple-element.90.dh2.left, bf16[1024,1536]{1,0:T(8,128)(2,1)} %get-tuple-element.91.slope, bf16[768,1536]{1,0:T(8,128)(2,1)} %get-tuple-element.92.w_down, ...), custom_call_target="tpu_custom_call" | custom-call | flops 4831838208 | bytes 14204928 | tf_op jit(solution)/shard_map/feed_back/pallas_call | solution.py:161
  214.5 7.4 %feed_grad_down.1 = (bf16[8,96,768]{2,1,0:T(8,128)(2,1)}, bf16[8,96,768]{2,1,0:T(8,128)(2,1)}) custom-call(s32[98]{0:T(128)} %pad_add_fusion.places, bf16[1024,768]{1,0:T(8,128)(2,1)} %get-tuple-element.90.dh2.left, bf16[1024,1536]{1,0:T(8,128)(2,1)} %get-tuple-element.86.m.right), custom_call_target="tpu_custom_call" | custom-call | flops 2415919104 | bytes 7077888 | tf_op jit(solution)/shard_map/feed_grad_down/pallas_call | solution.py:161
  224.4 7.5 %feed_grad_up.1 = (bf16[8,96,768]{2,1,0:T(8,128)(2,1)}, bf16[8,96,768]{2,1,0:T(8,128)(2,1)}) custom-call(s32[98]{0:T(128)} %pad_add_fusion.places, bf16[1024,768]{1,0:T(8,128)(2,1)} %get-tuple-element.117.left, bf16[1024,1536]{1,0:T(8,128)(2,1)} %get-tuple-element.118.right), custom_call_target="tpu_custom_call" | custom-call | flops 2415919104 | bytes 7077888 | tf_op jit(solution)/shard_map/feed_grad_up/pallas_call | solution.py:161
  236.5 9.2 %collective-permute-done.71 = bf16[8,16,768]{2,1,0:T(8,128)(2,1)} collective-permute-done((bf16[8,16,768]{2,1,0:T(8,128)(2,1)}, bf16[8,16,768]{2,1,0:T(8,128)(2,1)}, u32[]{:S(2)}, u32[]{:S(2)}) %collective-permute-start.71) | collective-permute-done | bytes 196640 | tf_op jit(solution)/shard_map/ppermute | solution.py:85
  249.7 27.1 %collective-permute-done.34 = bf16[512,768]{1,0:T(8,128)(2,1)} collective-permute-done((bf16[512,768]{1,0:T(8,128)(2,1)}, bf16[512,768]{1,0:T(8,128)(2,1)}, u32[]{:S(2)}, u32[]{:S(2)}) %collective-permute-start.34) | collective-permute-done | bytes 786464 | tf_op jit(solution)/shard_map/ppermute | solution.py:85
  284.1 8.8 %middle_back.1 = (f32[1024,768]{1,0:T(8,128)}, bf16[1024,768]{1,0:T(8,128)(2,1)}, bf16[1024,384]{1,0:T(8,128)(2,1)}, f32[8,768]{1,0:T(8,128)}) custom-call(s32[98]{0:T(128)} %pad_add_fusion.places, f32[1024,768]{1,0:T(8,128)} %get-tuple-element.89.dh2, bf16[1024,768]{1,0:T(8,128)(2,1)} %get-tuple-element.94.dx, ...), custom_call_target="tpu_custom_call" | custom-call | flops 603979776 | bytes 16102400 | tf_op jit(solution)/shard_map/middle_back/pallas_call | solution.py:161
  294.0 22.0 %attend_backward.1 = (bf16[1024,384]{1,0:T(8,128)(2,1)}, bf16[1024,384]{1,0:T(8,128)(2,1)}, bf16[1024,384]{1,0:T(8,128)(2,1)}) custom-call(s32[98]{0:T(128)} %pad_add_fusion.places, bf16[1024,384]{1,0:T(8,128)(2,1)} %get-tuple-element.80.q_ref, bf16[1024,384]{1,0:T(8,128)(2,1)} %get-tuple-element.81.k_ref, bf16[1024,384]{1,0:T(8,128)(2,1)} %get-tuple-element.82.v_ref, ...), custom_call_target="tpu_custom_call" | custom-call | flops 12884901888 | bytes 19660800 | tf_op jit(solution)/shard_map/attend_backward/pallas_call | solution.py:161
  316.0 6.8 %narrow_grad_query.1 = (bf16[8,96,192]{2,1,0:T(8,128)(2,1)}, bf16[8,96,192]{2,1,0:T(8,128)(2,1)}, bf16[8,96,192]{2,1,0:T(8,128)(2,1)}, bf16[8,96,192]{2,1,0:T(8,...) custom-call(s32[98]{0:T(128)} %pad_add_fusion.places, ...), custom_call_target="tpu_custom_call" | custom-call | flops 1811939328 | bytes 7286784 | tf_op jit(solution)/shard_map/narrow_grad_query/pallas_call | solution.py:161
  339.9 7.3 %input_grad.1 = bf16[1024,768]{1,0:T(8,128)(2,1)} custom-call(s32[98]{0:T(128)} %pad_add_fusion.places, bf16[1024,384]{1,0:T(8,128)(2,1)} %get-tuple-element.101.dq.refs_0_, bf16[1024,384]{1,0:T(8,128)(2,1)} %get-tuple-element.102.dk.refs_1_, bf16[1024,384]{1,0:T(8,128)(2,1)} %get-tuple-element.103.dv.refs_2_, bf16[3,768,384]{2,1,0:T(8,128)(2,1)} %get-tuple-element.104.w), custom_call_target="tpu_custom_call" | custom-call | flops 1811939328 | bytes 5701632 | tf_op jit(solution)/shard_map/input_grad/pallas_call | solution.py:161
  349.4 8.0 %collective-permute-done.75 = f32[8,384]{1,0:T(8,128)S(1)} collective-permute-done((f32[8,384]{1,0:T(8,128)S(1)}, f32[8,384]{1,0:T(8,128)S(1)}, u32[]{:S(2)}, u32[]{:S(2)}) %collective-permute-start.75) | collective-permute-done | bytes 12320 | tf_op jit(solution)/shard_map/ppermute | solution.py:85
  386.4 12.7 %collective-permute-done.57 = bf16[4,96,192]{2,1,0:T(8,128)(2,1)S(1)} collective-permute-done((bf16[4,96,192]{2,1,0:T(8,128)(2,1)S(1)}, bf16[4,96,192]{2,1,0:T(8,128)(2,1)S(1)}, u32[]{:S(2)}, u32[]{:S(2)}) %collective-permute-start.57) | collective-permute-done | bytes 147488 | tf_op jit(solution)/shard_map/ppermute | solution.py:85
  (397 shorter events, 202.1 us)
Async XLA Ops:
  45.9 23.7 %collective-permute-start.15 = (bf16[8,96,192]{2,1,0:T(8,128)(2,1)S(1)}, bf16[8,96,192]{2,1,0:T(8,128)(2,1)S(1)}, u32[]{:S(2)}, u32[]{:S(2)}) collective-permute-start(bf16[8,96,192]{2,1,0:T(8,128)(2,1)S(1)} %pad_maximum_fusion.6.vn), channel_id=1, source_target_pairs={{0,8},{1,9},{2,10},{3,11},{4,12},{5,13},{6,14},{7,15},{8,0},{9,1},... | collective-permute-start | bytes 884744 | tf_op jit(solution)/shard_map/ppermute | solution.py:85
  48.1 22.8 %collective-permute-start.11 = (bf16[8,96,192]{2,1,0:T(8,128)(2,1)S(1)}, bf16[8,96,192]{2,1,0:T(8,128)(2,1)S(1)}, u32[]{:S(2)}, u32[]{:S(2)}) collective-permute-start(bf16[8,96,192]{2,1,0:T(8,128)(2,1)S(1)} %pad_maximum_fusion.5.kn), channel_id=1, source_target_pairs={{0,4},{1,5},{2,6},{3,7},{4,0},{5,1},{6,2},{7,3},{8,12},{9,13},{10,... | collective-permute-start | bytes 884744 | tf_op jit(solution)/shard_map/ppermute | solution.py:85
  54.8 40.0 %collective-permute-start.19 = (bf16[8,96,192]{2,1,0:T(8,128)(2,1)S(1)}, bf16[8,96,192]{2,1,0:T(8,128)(2,1)S(1)}, u32[]{:S(2)}, u32[]{:S(2)}) collective-permute-start(bf16[8,96,192]{2,1,0:T(8,128)(2,1)S(1)} %pad_maximum_fusion.7.near), channel_id=1, source_target_pairs={{0,8},{1,9},{2,10},{3,11},{4,12},{5,13},{6,14},{7,15},{8,0},{9,1},... | collective-permute-start | bytes 884744 | tf_op jit(solution)/shard_map/ppermute | solution.py:85
  61.1 39.8 %collective-permute-start.23 = (bf16[4,96,768]{2,1,0:T(8,128)(2,1)S(1)}, bf16[4,96,768]{2,1,0:T(8,128)(2,1)S(1)}, u32[]{:S(2)}, u32[]{:S(2)}) collective-permute-start(bf16[4,96,768]{2,1,0:T(8,128)(2,1)S(1)} %pad_maximum_fusion.2), channel_id=1, source_target_pairs={{0,4},{1,5},{2,6},{3,7},{4,0},{5,1},{6,2},{7,3},{8,12},{9,13},{10,... | collective-permute-start | bytes 1769480 | tf_op jit(solution)/shard_map/ppermute | solution.py:85
  69.6 32.3 %collective-permute-start.27 = (bf16[4,96,768]{2,1,0:T(8,128)(2,1)S(1)}, bf16[4,96,768]{2,1,0:T(8,128)(2,1)S(1)}, u32[]{:S(2)}, u32[]{:S(2)}) collective-permute-start(bf16[4,96,768]{2,1,0:T(8,128)(2,1)S(1)} %pad_maximum_fusion.3), channel_id=1, source_target_pairs={{0,2},{1,3},{2,0},{3,1},{4,6},{5,7},{6,4},{7,5},{8,10},{9,11},{10,... | collective-permute-start | bytes 1769480 | tf_op jit(solution)/shard_map/ppermute | solution.py:85
  101.1 28.5 %collective-permute-start.24 = (bf16[8,96,768]{2,1,0:T(8,128)(2,1)S(1)}, bf16[8,96,768]{2,1,0:T(8,128)(2,1)}, u32[]{:S(2)}, u32[]{:S(2)}) collective-permute-start(bf16[8,96,768]{2,1,0:T(8,128)(2,1)S(1)} %pad_maximum_fusion.near), channel_id=1, source_target_pairs={{0,2},{1,3},{2,0},{3,1},{4,6},{5,7},{6,4},{7,5},{8,10},{9,11},{10,... | collective-permute-start | bytes 3538952 | tf_op jit(solution)/shard_map/ppermute | solution.py:85
  102.0 39.5 %collective-permute-start.28 = (bf16[8,96,768]{2,1,0:T(8,128)(2,1)S(1)}, bf16[8,96,768]{2,1,0:T(8,128)(2,1)}, u32[]{:S(2)}, u32[]{:S(2)}) collective-permute-start(bf16[8,96,768]{2,1,0:T(8,128)(2,1)S(1)} %pad_maximum_fusion.1.near), channel_id=1, source_target_pairs={{0,4},{1,5},{2,6},{3,7},{4,0},{5,1},{6,2},{7,3},{8,12},{9,13},{10,... | collective-permute-start | bytes 3538952 | tf_op jit(solution)/shard_map/ppermute | solution.py:85
  104.8 44.9 %collective-permute-start.30 = (bf16[96,384]{1,0:T(8,128)(2,1)S(1)}, bf16[96,384]{1,0:T(8,128)(2,1)}, u32[]{:S(2)}, u32[]{:S(2)}) collective-permute-start(bf16[96,384]{1,0:T(8,128)(2,1)S(1)} %dynamic-slice_convert_fusion), channel_id=1, source_target_pairs={{0,4},{1,5},{2,6},{3,7},{4,0},{5,1},{6,2},{7,3},{8,12},{9,13},{10,... | collective-permute-start | bytes 221192 | tf_op jit(solution)/shard_map/ppermute | solution.py:85
  149.6 39.5 %collective-permute-start.29 = (bf16[1024,768]{1,0:T(8,128)(2,1)}, bf16[1024,768]{1,0:T(8,128)(2,1)S(1)}, u32[]{:S(2)}, u32[]{:S(2)}) collective-permute-start(bf16[1024,768]{1,0:T(8,128)(2,1)} %get-tuple-element.87.f), channel_id=1, source_target_pairs={{0,1},{1,0},{2,3},{3,2},{4,5},{5,4},{6,7},{7,6},{8,9},{9,8},{10,11... | collective-permute-start | bytes 4718600 | tf_op jit(solution)/shard_map/ppermute | solution.py:85
  221.9 62.2 %collective-permute-start.36 = (bf16[1024,768]{1,0:T(8,128)(2,1)S(1)}, bf16[1024,768]{1,0:T(8,128)(2,1)}, u32[]{:S(2)}, u32[]{:S(2)}) collective-permute-start(bf16[1024,768]{1,0:T(8,128)(2,1)S(1)} %copy-done.4), channel_id=1, source_target_pairs={{0,1},{1,0},{2,3},{3,2},{4,5},{5,4},{6,7},{7,6},{8,9},{9,8},{10,11... | collective-permute-start | bytes 4718600 | tf_op jit(solution)/shard_map/ppermute | solution.py:85
  221.9 55.0 %collective-permute-start.64 = (bf16[8,96,768]{2,1,0:T(8,128)(2,1)}, bf16[8,96,768]{2,1,0:T(8,128)(2,1)}, u32[]{:S(2)}, u32[]{:S(2)}) collective-permute-start(bf16[8,96,768]{2,1,0:T(8,128)(2,1)} %get-tuple-element.122), channel_id=1, source_target_pairs={{0,4},{1,5},{2,6},{3,7},{4,0},{5,1},{6,2},{7,3},{8,12},{9,13},{10,... | collective-permute-start | bytes 3538952 | tf_op jit(solution)/shard_map/ppermute | solution.py:85
  231.9 48.4 %collective-permute-start.60 = (bf16[8,96,768]{2,1,0:T(8,128)(2,1)}, bf16[8,96,768]{2,1,0:T(8,128)(2,1)}, u32[]{:S(2)}, u32[]{:S(2)}) collective-permute-start(bf16[8,96,768]{2,1,0:T(8,128)(2,1)} %get-tuple-element.120), channel_id=1, source_target_pairs={{0,2},{1,3},{2,0},{3,1},{4,6},{5,7},{6,4},{7,5},{8,10},{9,11},{10,... | collective-permute-start | bytes 3538952 | tf_op jit(solution)/shard_map/ppermute | solution.py:85
  235.1 41.8 %collective-permute-start.34 = (bf16[512,768]{1,0:T(8,128)(2,1)}, bf16[512,768]{1,0:T(8,128)(2,1)}, u32[]{:S(2)}, u32[]{:S(2)}) collective-permute-start(bf16[512,768]{1,0:T(8,128)(2,1)} %constant_dynamic-slice_fusion.2), channel_id=1, source_target_pairs={{0,2},{1,3},{2,0},{3,1},{4,6},{5,7},{6,4},{7,5},{8,10},{9,11},{10,... | collective-permute-start | bytes 2359304 | tf_op jit(solution)/shard_map/ppermute | solution.py:85
  276.9 52.0 %collective-permute-start.35 = (bf16[512,768]{1,0:T(8,128)(2,1)}, bf16[512,768]{1,0:T(8,128)(2,1)S(1)}, u32[]{:S(2)}, u32[]{:S(2)}) collective-permute-start(bf16[512,768]{1,0:T(8,128)(2,1)} %collective-permute-done.34), channel_id=1, source_target_pairs={{0,1},{1,0},{2,3},{3,2},{4,5},{5,4},{6,7},{7,6},{8,9},{9,8},{10,11... | collective-permute-start | bytes 2359304 | tf_op jit(solution)/shard_map/ppermute | solution.py:85
  278.9 96.2 %collective-permute-start.65 = (bf16[4,96,768]{2,1,0:T(8,128)(2,1)}, bf16[4,96,768]{2,1,0:T(8,128)(2,1)}, u32[]{:S(2)}, u32[]{:S(2)}) collective-permute-start(bf16[4,96,768]{2,1,0:T(8,128)(2,1)} %add_convert_fusion.1), channel_id=1, source_target_pairs={{0,2},{1,3},{2,0},{3,1},{4,6},{5,7},{6,4},{7,5},{8,10},{9,11},{10,... | collective-permute-start | bytes 1769480 | tf_op jit(solution)/shard_map/ppermute | solution.py:85
  282.4 95.6 %collective-permute-start.61 = (bf16[4,96,768]{2,1,0:T(8,128)(2,1)}, bf16[4,96,768]{2,1,0:T(8,128)(2,1)}, u32[]{:S(2)}, u32[]{:S(2)}) collective-permute-start(bf16[4,96,768]{2,1,0:T(8,128)(2,1)} %add_convert_fusion.2), channel_id=1, source_target_pairs={{0,4},{1,5},{2,6},{3,7},{4,0},{5,1},{6,2},{7,3},{8,12},{9,13},{10,... | collective-permute-start | bytes 1769480 | tf_op jit(solution)/shard_map/ppermute | solution.py:85
  293.6 54.3 %collective-permute-start.40 = (f32[13,768]{1,0:T(8,128)S(1)}, f32[13,768]{1,0:T(8,128)S(1)}, u32[]{:S(2)}, u32[]{:S(2)}) collective-permute-start(f32[13,768]{1,0:T(8,128)S(1)} %pad_maximum_fusion.19), channel_id=1, source_target_pairs={{0,4},{1,5},{2,6},{3,7},{4,0},{5,1},{6,2},{7,3},{8,12},{9,13},{10,... | collective-permute-start | bytes 119816 | tf_op jit(solution)/shard_map/ppermute | solution.py:85
  328.8 50.6 %collective-permute-start.56 = (bf16[8,96,192]{2,1,0:T(8,128)(2,1)}, bf16[8,96,192]{2,1,0:T(8,128)(2,1)}, u32[]{:S(2)}, u32[]{:S(2)}) collective-permute-start(bf16[8,96,192]{2,1,0:T(8,128)(2,1)} %get-tuple-element.116), channel_id=1, source_target_pairs={{0,8},{1,9},{2,10},{3,11},{4,12},{5,13},{6,14},{7,15},{8,0},{9,1},... | collective-permute-start | bytes 884744 | tf_op jit(solution)/shard_map/ppermute | solution.py:85
  347.3 33.5 %collective-permute-start.44 = (bf16[8,96,192]{2,1,0:T(8,128)(2,1)}, bf16[8,96,192]{2,1,0:T(8,128)(2,1)S(1)}, u32[]{:S(2)}, u32[]{:S(2)}) collective-permute-start(bf16[8,96,192]{2,1,0:T(8,128)(2,1)} %get-tuple-element.109), channel_id=1, source_target_pairs={{0,2},{1,3},{2,0},{3,1},{4,6},{5,7},{6,4},{7,5},{8,10},{9,11},{10,... | collective-permute-start | bytes 884744 | tf_op jit(solution)/shard_map/ppermute | solution.py:85
  378.0 49.3 %collective-permute-start.37 = (bf16[1024,768]{1,0:T(8,128)(2,1)S(1)}, bf16[1024,768]{1,0:T(8,128)(2,1)S(1)}, u32[]{:S(2)}, u32[]{:S(2)}) collective-permute-start(bf16[1024,768]{1,0:T(8,128)(2,1)S(1)} %copy-done.5), channel_id=1, source_target_pairs={{0,1},{1,0},{2,3},{3,2},{4,5},{5,4},{6,7},{7,6},{8,9},{9,8},{10,11... | collective-permute-start | bytes 4718600 | tf_op jit(solution)/shard_map/ppermute | solution.py:85
  379.4 34.4 %collective-permute-start.66 = (bf16[2,96,768]{2,1,0:T(8,128)(2,1)S(1)}, bf16[2,96,768]{2,1,0:T(8,128)(2,1)S(1)}, u32[]{:S(2)}, u32[]{:S(2)}) collective-permute-start(bf16[2,96,768]{2,1,0:T(8,128)(2,1)S(1)} %add_convert_fusion.3), channel_id=1, source_target_pairs={{0,8},{1,9},{2,10},{3,11},{4,12},{5,13},{6,14},{7,15},{8,0},{9,1},... | collective-permute-start | bytes 884744 | tf_op jit(solution)/shard_map/ppermute | solution.py:85
  380.8 36.7 %collective-permute-start.62 = (bf16[2,96,768]{2,1,0:T(8,128)(2,1)S(1)}, bf16[2,96,768]{2,1,0:T(8,128)(2,1)S(1)}, u32[]{:S(2)}, u32[]{:S(2)}) collective-permute-start(bf16[2,96,768]{2,1,0:T(8,128)(2,1)S(1)} %add_convert_fusion.4), channel_id=1, source_target_pairs={{0,8},{1,9},{2,10},{3,11},{4,12},{5,13},{6,14},{7,15},{8,0},{9,1},... | collective-permute-start | bytes 884744 | tf_op jit(solution)/shard_map/ppermute | solution.py:85
  419.9 28.8 %collective-permute-start.67 = (bf16[1,96,768]{2,1,0:T(8,128)(2,1)}, bf16[1,96,768]{2,1,0:T(8,128)(2,1)}, u32[]{:S(2)}, u32[]{:S(2)}) collective-permute-start(bf16[1,96,768]{2,1,0:T(8,128)(2,1)} %add_convert_fusion.9), channel_id=1, source_target_pairs={{0,16},{1,17},{2,18},{3,19},{4,20},{5,21},{6,22},{7,23},{8,24},{9,... | collective-permute-start | bytes 442376 | tf_op jit(solution)/shard_map/ppermute | solution.py:85
  421.8 29.3 %collective-permute-start.63 = (bf16[1,96,768]{2,1,0:T(8,128)(2,1)}, bf16[1,96,768]{2,1,0:T(8,128)(2,1)}, u32[]{:S(2)}, u32[]{:S(2)}) collective-permute-start(bf16[1,96,768]{2,1,0:T(8,128)(2,1)} %add_convert_fusion.10), channel_id=1, source_target_pairs={{0,16},{1,17},{2,18},{3,19},{4,20},{5,21},{6,22},{7,23},{8,24},{9,... | collective-permute-start | bytes 442376 | tf_op jit(solution)/shard_map/ppermute | solution.py:85
  (115 other events, 1726.9 us)

commit v2 on v1

v2 whole, which is shorter than its diff:
```python
import functools

import jax
import jax.numpy as jnp
import numpy as np
from jax import lax
from jax.experimental import pallas as pl
from jax.experimental.pallas import tpu as pltpu
from jax.sharding import PartitionSpec as P

D = 768
HD = 64
FF = 3072
LAYER = 6
STEP = 10
LEN = 1024


EPS_NORM = 1e-06
BETA_ONE = 0.9
BETA_TWO = 0.98
EPS_ADAM = 1e-08
DECAY = 0.01
RATE = 0.8
VECTOR_RATE = 0.3

LOW = jnp.bfloat16
WIDE = jnp.float32
LOG2_E = 1.4426950408889634
MIB = 2**20
COST_SCALE = 16

CORE, SIDE, X_BIT, Z_LOW, Z_HIGH = 1, 2, 4, 8, 16
BLOCKS = 8
BLOCK_ROWS = D // BLOCKS
PART_ROWS = BLOCK_ROWS // 2
MARKS_AT, MARKED_WIDTH = 768, 896
ACROSS = ((Z_HIGH, Z_LOW, X_BIT, SIDE), (Z_HIGH, Z_LOW, SIDE, X_BIT))
ALONG = ((Z_HIGH, Z_LOW, SIDE, X_BIT), (Z_HIGH, SIDE, X_BIT, Z_LOW))
Z_LINE = (Z_HIGH, Z_LOW, Z_HIGH | Z_LOW)
ROUTES = (ACROSS, ALONG)


def dot(left, right):
    return lax.dot_general(
        left, right, (((1,), (0,)), ((), ())), preferred_element_type=WIDE
    )


def dot_nt(left, right):
    return lax.dot_general(
        left, right, (((1,), (1,)), ((), ())), preferred_element_type=WIDE
    )


def dot_tn(left, right):
    return lax.dot_general(
        left, right, (((0,), (0,)), ((), ())), preferred_element_type=WIDE
    )


def adamw(weight, first, second, grad, rate, decay):
    first_new = BETA_ONE * first + (1.0 - BETA_ONE) * grad
    second_new = BETA_TWO * second + (1.0 - BETA_TWO) * grad * grad
    first_hat = first_new / (1.0 - BETA_ONE**STEP)
    second_hat = second_new / (1.0 - BETA_TWO**STEP)
    weight_new = weight - rate * (first_hat / (jnp.sqrt(second_hat) + EPS_ADAM) + decay * weight)
    return (weight_new, first_new, second_new)


class Links:
    def __init__(self, dp_count, mp_count):
        self.dp_count = dp_count
        self.total = dp_count * mp_count
        self.cube = dp_count == BLOCKS
        self.dp = lax.axis_index("dp").astype(jnp.int32)
        mp = lax.axis_index("mp").astype(jnp.int32)
        self.side = mp // 2
        self.core = mp % 2

    def swap(self, value, bit):
        pairs = [(i, i ^ bit) for i in range(self.total)]
        return lax.ppermute(value, ("dp", "mp"), pairs)

    def places(self):
        flips = []
        for order in sum(ROUTES, ()):
            for j in range(2 * BLOCKS):
                if self.cube:
                    bits = 0
                    for k, bit in enumerate(order):
                        bits ^= bit if (j >> k) & 1 else 0
                    flips.append((bits // SIDE & 1, bits // X_BIT))
                else:
                    flips.append((j // BLOCKS, j % BLOCKS))
        flips = np.array(flips, np.int32)
        mine = self.dp if self.cube else 0
        return (self.side ^ flips[:, 0]) * BLOCKS + (mine ^ flips[:, 1])

    def spread(self, share):
        return (Spread if self.cube else WholeSpread)(self, share)

    def fold(self, halves, route):
        return (Fold if self.cube else WholeFold)(self, halves, route)


class Spread:
    def __init__(self, links, share):
        self.links = links
        self.held = [share[None]]
        self.last = None
        self.round = 0

    def step(self, *others):
        links = self.links
        if others:
            (self.held, self.last), *_ = lax.optimization_barrier(((self.held, self.last), *others))
        if self.round == 0:
            self.last = [links.swap(self.held[0], bits) for bits in Z_LINE]
        elif self.round == 1:
            line = [self.held[0], *self.last]
            at = (slice(0, PART_ROWS), slice(PART_ROWS, BLOCK_ROWS))
            self.held = [jnp.concatenate([a[:, i] for a in line], axis=0) for i in at]
        else:
            self.held = [
                jnp.concatenate([mine, other], axis=0)
                for mine, other in zip(self.held, self.last, strict=True)
            ]
        if self.round:
            self.last = [
                links.swap(part, ACROSS[i][self.round + 1]) for i, part in enumerate(self.held)
            ]
        self.round += 1
        return tuple(self.held)

    def halves(self):
        return (self.held[0], self.last[0], self.held[1], self.last[1])


class WholeSpread:
    def __init__(self, links, share):
        self.last = ()
        near = lax.all_gather(share, "dp", axis=0, tiled=True)
        near = near.reshape(BLOCKS, BLOCK_ROWS, share.shape[1])
        far = links.swap(near, SIDE)
        self.parts = (
            near[:, :PART_ROWS],
            far[:, :PART_ROWS],
            near[:, PART_ROWS:],
            far[:, PART_ROWS:],
        )

    def step(self, *others):
        return ()

    def halves(self):
        return self.parts


class Fold:
    def __init__(self, links, halves, route):
        self.links = links
        self.route = route
        self.parts = [[halves[0]], [halves[2]]]
        self.far = [halves[1], halves[3]]
        self.joined = []
        self.round = 0

    def step(self, *others, vmem=60):
        links, k = self.links, 3 - self.round
        if others:
            (self.parts, self.joined, self.far), *_ = lax.optimization_barrier(
                ((self.parts, self.joined, self.far), *others)
            )
        if self.route is ACROSS and self.round == 2:
            sent = fold_add(self.parts, [], (1, 2, 3), False, vmem)
            self.joined = [links.swap(a, bits) for a, bits in zip(sent, Z_LINE, strict=True)]
        else:
            if self.round == 0:
                sent = self.far
            else:
                sent = fold_add(self.parts, [], range(2**k, 2 ** (k + 1)), True, vmem)
            for i, order in enumerate(self.route):
                self.parts[i].append(links.swap(sent[i], order[k]))
        self.round += 1
        return tuple(sent)

    def pieces(self):
        return (self.parts[0], self.parts[1], self.joined)


class WholeFold:
    def __init__(self, links, halves, route):
        near, far = (
            jnp.concatenate([halves[i], halves[i + 2]], axis=1).reshape(D, -1) for i in range(2)
        )
        total = near.astype(WIDE) + links.swap(far, SIDE).astype(WIDE)
        self.share = lax.psum_scatter(total, "dp", scatter_dimension=0, tiled=True)
        if self.share.shape[1] == MARKED_WIDTH:
            marks = lax.psum(total[0:8, MARKS_AT:], "dp")
            self.share = self.share.at[0:8, MARKS_AT:].set(marks)

    def step(self, *others, vmem=60):
        return ()

    def pieces(self):
        return ([], [], [self.share])


def sum_pieces(refs, counts):
    def add(group):
        return sum(ref[0].astype(WIDE) for ref in group)

    first, second, joined = counts
    if first:
        total = jnp.concatenate(
            [add_marked(refs[:first]), add_marked(refs[first : first + second])], axis=0
        )
        if joined:
            total = total + add(refs[first + second :])
        return total
    return refs[0][...]


def add_marked(refs):
    total = sum(ref[0].astype(WIDE) for ref in refs)
    if total.shape[1] != MARKED_WIDTH:
        return total
    marks = refs[0][0][:, MARKS_AT:].astype(WIDE)
    for ref in refs[1:]:
        marks = marks.astype(LOW).astype(WIDE) + ref[0][:, MARKS_AT:].astype(WIDE)
    return jnp.concatenate([total[:, :MARKS_AT], marks], axis=1)


def fold_add_kernel(counts, apart, *refs):
    first = counts[0]
    total = sum(counts)
    ins, outs = refs[:total], refs[total:]
    if apart:
        outs[0][0] = add_marked(ins[:first]).astype(LOW)
        outs[1][0] = add_marked(ins[first:]).astype(LOW)
    else:
        block = sum_pieces(ins, counts).astype(LOW)
        for i, out in enumerate(outs):

            @pl.when(pl.program_id(0) == i)
            def _(out=out):
                out[0] = block


def fold_add(parts, joined, blocks, apart, vmem):
    counts = (len(parts[0]), len(parts[1]), len(joined))
    args = [*parts[0], *parts[1], *joined]
    width = args[0].shape[2]
    low, count = blocks[0], len(blocks)
    if apart:
        outs = [shape((count, PART_ROWS, width), LOW)] * 2
        out_specs = [pl.BlockSpec((1, PART_ROWS, width), lambda i: (i, 0, 0))] * 2
    else:
        outs = [shape((1, BLOCK_ROWS, width), LOW)] * count
        out_specs = [pl.BlockSpec((1, BLOCK_ROWS, width), lambda i: (0, 0, 0))] * count
    return pl.pallas_call(
        functools.partial(fold_add_kernel, counts, apart),
        grid=(count,),
        in_specs=[pl.BlockSpec((1, a.shape[1], width), lambda i: (low + i, 0, 0)) for a in args],
        out_specs=out_specs,
        out_shape=outs,
        compiler_params=pltpu.CompilerParams(vmem_limit_bytes=vmem * MIB),
        cost_estimate=pl.CostEstimate(
            flops=count * BLOCK_ROWS * width, bytes_accessed=count * width, transcendentals=0
        ),
        name="fold_add",
    )(*args)


class Total:
    def __init__(self, links, value):
        self.links = links
        self.value = value
        self.bits = [Z_LOW, Z_HIGH, X_BIT, SIDE]
        self.last = None

    def step(self, *others):
        links = self.links
        if others:
            (self.value, self.last), *_ = lax.optimization_barrier(
                ((self.value, self.last), *others)
            )
        self.value = self.result()
        if not links.cube and len(self.bits) == 4:
            self.bits = [SIDE]
            self.value = lax.psum(self.value, "dp")
        if not self.bits:
            return ()
        self.last = links.swap(self.value, self.bits.pop(0))
        return (self.value,)

    def result(self):
        return self.value if self.last is None else self.value + self.last


def after(value, *others):
    return lax.optimization_barrier((value, *others))[0]


def call(kernel, name, grid, in_specs, out_specs, out_shape, scratch, places, args, flops, vmem=24, aliases=None):
    moved = sum(a.size * a.dtype.itemsize for a in args)
    moved += sum(int(np.prod(s.shape)) * np.dtype(s.dtype).itemsize for s in out_shape)
    return pl.pallas_call(
        kernel,
        out_shape=out_shape,
        grid_spec=pltpu.PrefetchScalarGridSpec(
            num_scalar_prefetch=1,
            grid=grid,
            in_specs=in_specs,
            out_specs=out_specs,
            scratch_shapes=scratch,
        ),
        input_output_aliases=aliases or {},
        compiler_params=pltpu.CompilerParams(vmem_limit_bytes=vmem * MIB),
        cost_estimate=pl.CostEstimate(
            flops=int(flops) // COST_SCALE, bytes_accessed=int(moved) // COST_SCALE, transcendentals=0
        ),
        name=name,
    )(places, *args)


def whole(array):
    return pl.BlockSpec(array.shape, lambda *_: (0,) * len(array.shape))


def rows(count, width):
    return pl.BlockSpec((count, width), lambda i, *_: (i, 0))


def shape(dims, kind):
    return jax.ShapeDtypeStruct(dims, kind)


def gather_blocks(places, halves, held, route=ACROSS):
    for i in range(2):
        for j in range(2 * BLOCKS):
            source = halves[2 * i + j // BLOCKS]
            target = places[1 + 2 * BLOCKS * (2 * ROUTES.index(route) + i) + j]
            held[target, i * PART_ROWS : (i + 1) * PART_ROWS, :] = source[j % BLOCKS]


def scatter_blocks(places, held, halves, route=ACROSS):
    for i in range(2):
        for j in range(2 * BLOCKS):
            target = halves[2 * i + j // BLOCKS]
            source = places[1 + 2 * BLOCKS * (2 * ROUTES.index(route) + i) + j]
            target[j % BLOCKS] = held[source, i * PART_ROWS : (i + 1) * PART_ROWS, :]


CORE_AT = 1 + 4 * BLOCKS * len(ROUTES)
SLOT_AT = CORE_AT + 1


def side_of(held, side, at, width):
    return held[side * BLOCKS : (side + 1) * BLOCKS, :, at : at + width].reshape(D, width)


def to_pairs(held, wide_at, narrow_at):
    return jnp.concatenate(
        [side_of(held, side, wide_at, 128) for side in range(2)]
        + [side_of(held, side, narrow_at, 64) for side in range(2)],
        axis=1,
    )


def from_pairs(value, held, wide_at, narrow_at):
    for side in range(2):
        at = slice(side * BLOCKS, (side + 1) * BLOCKS)
        wide = value[:, 128 * side : 128 * (side + 1)]
        held[at, :, wide_at : wide_at + 128] = wide.reshape(BLOCKS, BLOCK_ROWS, 128)
        narrow = value[:, 256 + 64 * side : 320 + 64 * side]
        held[at, :, narrow_at : narrow_at + 64] = narrow.reshape(BLOCKS, BLOCK_ROWS, 64)


def half_shapes(width):
    return [shape((BLOCKS, PART_ROWS, width), LOW)] * 4


def half_specs(width):
    return [pl.BlockSpec((BLOCKS, PART_ROWS, width), lambda *_: (0, 0, 0))] * 4


def held_blocks(width):
    return pltpu.VMEM((2 * BLOCKS, BLOCK_ROWS, width), LOW)


def pack_first_kernel(w, out):
    wide = [w[i][:, :128] for i in range(3)]
    narrow = [w[i][:, 128:] for i in range(3)]
    out[...] = jnp.concatenate(wide + narrow, axis=1).astype(LOW)


def pack_first(qkv):
    return pl.pallas_call(
        pack_first_kernel,
        out_shape=shape((qkv.shape[1], 576), LOW),
        name="pack_first",
    )(qkv)


def pack_kernel(places, exit_layer, up, out, down, pool, qv, upb, up_out, down_pool, biases):
    up_out[:, 0:D] = up[...].astype(LOW)
    up_out[:, D : D + 192] = out[...].T.astype(LOW)
    down_pool[:, 0:D] = down[...].astype(LOW)
    quarter = 2 * places[CORE_AT] + places[0]
    mine = jnp.zeros((pool.shape[0], 192), WIDE)
    for i in range(4):
        mine = jnp.where(quarter == i, pool[:, 192 * i : 192 * (i + 1)], mine)
    live = jnp.float32(0.0)
    for i in range(exit_layer.shape[0]):
        live += jnp.where(exit_layer[i] >= LAYER, 1.0, 0.0)
    row = lax.broadcasted_iota(jnp.int32, (pool.shape[0], 64), 0)
    marks = jnp.where(row == 0, live, 0.0)
    down_pool[:, D : D + 256] = jnp.concatenate([mine, marks], axis=1).astype(LOW)
    biases[...] = jnp.zeros_like(biases)
    biases[0:1, :] = upb[...].reshape(1, D)
    biases[1:2, 0:192] = qv[0:1, :]
    biases[2:3, 0:192] = qv[1:2, :]


def pack(places, exit_layer, up, out, down, pool, qv, upb):
    share = up.shape[0]
    args = (exit_layer, up, out, down, pool, qv, upb)
    return call(
        pack_kernel,
        "pack",
        (1,),
        [pl.BlockSpec(memory_space=pltpu.SMEM)] + [whole(a) for a in args[1:]],
        [pl.BlockSpec((share, 960), lambda *_: (0, 0)), pl.BlockSpec((share, 1024), lambda *_: (0, 0))]
        + [pl.BlockSpec((8, D), lambda *_: (0, 0))],
        [shape((share, 960), LOW), shape((share, 1024), LOW), shape((8, D), WIDE)],
        [],
        places,
        args,
        1,
        vmem=60,
    )


def by_side(places, mine, other):
    upper = places[0] == 1
    return jnp.where(upper, other, mine), jnp.where(upper, mine, other)


def project_kernel(places, x, bias, bias_other, h0, h1, h2, h3, q, k, v, w, held, pairs):
    @pl.when(pl.program_id(0) == 0)
    def _():
        gather_blocks(places, (h0, h1, h2, h3), held)
        for i in range(3):
            w[i] = to_pairs(held, 128 * i, 512 + 64 * i - 128)
        left, right = by_side(places, bias[...], bias_other[...])
        pairs[...] = jnp.concatenate(
            [left[:, :128], right[:, :128], left[:, 128:192], right[:, 128:192]], axis=1
        )

    left = x[...]
    q[...] = (dot(left, w[0]) + pairs[1:2, :]).astype(LOW)
    k[...] = dot(left, w[1]).astype(LOW)
    v[...] = (dot(left, w[2]) + pairs[2:3, :]).astype(LOW)


def project(places, tokens, bias, bias_other, halves):
    step = 256
    args = (tokens, bias, bias_other, *halves)
    return call(
        project_kernel,
        "project",
        (LEN // step,),
        [pl.BlockSpec((step, D), lambda i, places: (places[0] * (LEN // step) + i, 0))]
        + [whole(a) for a in args[1:]],
        [rows(step, 384)] * 3 + [pl.BlockSpec((3, D, 384), lambda *_: (0, 0, 0))],
        [shape((LEN, 384), LOW)] * 3 + [shape((3, D, 384), LOW)],
        [held_blocks(576), pltpu.VMEM((8, 384), WIDE)],
        places,
        args,
        2 * LEN * D * 1152,
    )


def first_of_pair():
    return lax.broadcasted_iota(jnp.int32, (1, 128), 1) < HD


def attend_kernel(places, q_ref, k_ref, v_ref, o_ref, inv_ref, p_ref, vx):
    first = first_of_pair()
    zero, one = jnp.zeros((), LOW), jnp.ones((), LOW)
    k = k_ref[...]
    v = v_ref[...]
    n = k.shape[0]
    vx[0:n, 0:128] = jnp.where(first, v, zero)
    vx[n : 2 * n, 0:128] = jnp.where(first, zero, v)
    vx[0:n, 128:256] = jnp.broadcast_to(jnp.where(first, one, zero), (n, 128))
    vx[n : 2 * n, 128:256] = jnp.broadcast_to(jnp.where(first, zero, one), (n, 128))
    step = 256
    for i in range(n // step):
        at = pl.ds(i * step, step)
        q = q_ref[at, :]
        result = None
        for head in range(2):
            mine = jnp.where(first, q, zero) if head == 0 else jnp.where(first, zero, q)
            score = dot_nt(mine, k)
            top = jnp.max(score, axis=1, keepdims=True)
            weight = jnp.exp2((score - top) * (HD**-0.5 * LOG2_E)).astype(LOW)
            p_ref[head, at, :] = weight
            part = dot(weight, vx[head * n : (head + 1) * n, :])
            result = part if result is None else result + part
        inv = 1.0 / result[:, 128:256]
        inv_ref[at, :] = inv
        o_ref[at, :] = (result[:, 0:128] * inv).astype(LOW)


def attend(places, q, k, v):
    pair = pl.BlockSpec((LEN, 128), lambda i, *_: (0, i))
    return call(
        attend_kernel,
        "attend_forward",
        (3,),
        [pair] * 3,
        [pair, pair, pl.BlockSpec((2, LEN, LEN), lambda i, *_: (i, 0, 0))],
        [shape((LEN, 384), LOW), shape((LEN, 384), WIDE), shape((6, LEN, LEN), LOW)],
        [pltpu.VMEM((2 * LEN, 256), LOW)],
        places,
        (q, k, v),
        4 * 6 * LEN * LEN * 256,
        vmem=50,
    )


def out_kernel(places, o, h0, h1, h2, h3, z, w_out, w_up, held):
    @pl.when(pl.program_id(0) == 0)
    def _():
        gather_blocks(places, (h0, h1, h2, h3), held)
        w_out[...] = to_pairs(held, D, D + 128)
        w_up[:, 0:D] = side_of(held, 0, 0, D)
        w_up[:, D : 2 * D] = side_of(held, 1, 0, D)

    z[...] = dot_nt(o[...], w_out[...]).astype(LOW)


def project_out(places, o, halves):
    step = 256
    return call(
        out_kernel,
        "project_out",
        (LEN // step,),
        [rows(step, 384)] + [whole(a) for a in halves],
        [rows(step, D), pl.BlockSpec((D, 384), lambda *_: (0, 0))]
        + [pl.BlockSpec((D, 2 * D), lambda *_: (0, 0))],
        [shape((LEN, D), LOW), shape((D, 384), LOW), shape((D, 2 * D), LOW)],
        [held_blocks(960)],
        places,
        (o, *halves),
        2 * LEN * D * 384,
    )


def normalize(hidden):
    centred = hidden - jnp.mean(hidden, axis=-1, keepdims=True)
    spread = lax.rsqrt(jnp.mean(centred * centred, axis=-1, keepdims=True) + EPS_NORM)
    return centred * spread, spread


def norm_back(grad_normed, normed, spread):
    return spread * (
        grad_normed
        - jnp.mean(grad_normed, axis=-1, keepdims=True)
        - normed * jnp.mean(grad_normed * normed, axis=-1, keepdims=True)
    )


def up_kernel(places, x, z, zp, vec, bias_mine, bias_other, w, m, slope, n1, rs1, low, bias):
    @pl.when(pl.program_id(0) == 0)
    def _():
        left, right = by_side(places, bias_mine[0:1, :], bias_other[0:1, :])
        bias[:, 0:D] = left
        bias[:, D : 2 * D] = right

    total = z[...].astype(WIDE) + zp[...].astype(WIDE)
    normed, spread = normalize(x[...].astype(WIDE) + total + vec[4:5, :])
    n1[...] = normed
    rs1[...] = jnp.broadcast_to(spread, rs1.shape)
    middle = (normed * vec[0:1, :] + vec[1:2, :]).astype(LOW)
    low[...] = middle
    for c in range(4):
        at = pl.ds(c * 384, 384)
        u = dot(middle, w[:, at]) + bias[0:1, at]
        half = 0.5 * (1.0 + lax.erf(u * 0.7071067811865476))
        m[:, at] = (u * half).astype(LOW)
        slope[:, at] = (half + u * (jnp.exp(-0.5 * u * u) * 0.3989422804014327)).astype(LOW)


def feed_up(places, tokens, z, zp, vec, bias, bias_other, w_up):
    step = 256
    args = (tokens, z, zp, vec, bias, bias_other, w_up)
    return call(
        up_kernel,
        "feed_up",
        (LEN // step,),
        [pl.BlockSpec((step, D), lambda i, places: (places[0] * (LEN // step) + i, 0))]
        + [rows(step, D)] * 2
        + [whole(a) for a in args[3:]],
        [rows(step, 2 * D)] * 2
        + [rows(step, D), rows(step, 128), rows(step, D)],
        [shape((LEN, 2 * D), LOW)] * 2
        + [shape((LEN, D), WIDE), shape((LEN, 128), WIDE), shape((LEN, D), LOW)],
        [pltpu.VMEM((1, 2 * D), WIDE)],
        places,
        args,
        2 * LEN * D * 2 * D,
    )


def down_kernel(places, m, h0, h1, h2, h3, f, w, pool, count, held):
    @pl.when(pl.program_id(0) == 0)
    def _():
        gather_blocks(places, (h0, h1, h2, h3), held)
        for side in range(2):
            w[:, D * side : D * (side + 1)] = side_of(held, side, 0, D)
        pool[...] = jnp.concatenate([side_of(held, side, D, 192) for side in range(2)], axis=1)
        live = jnp.sum(side_of(held, 0, D + 192, 64).astype(WIDE), axis=0, keepdims=True)
        count[...] = jnp.broadcast_to(live[:, 0:1], count.shape)

    f[...] = dot_nt(m[...], w[...]).astype(LOW)


def feed_down(places, m, halves):
    step = 256
    return call(
        down_kernel,
        "feed_down",
        (LEN // step,),
        [rows(step, 2 * D)] + [whole(a) for a in halves],
        [rows(step, D), pl.BlockSpec((D, 2 * D), lambda *_: (0, 0))]
        + [pl.BlockSpec((D, 384), lambda *_: (0, 0)), pl.BlockSpec((8, 128), lambda *_: (0, 0))],
        [shape((LEN, D), LOW), shape((D, 2 * D), LOW), shape((D, 384), LOW), shape((8, 128), WIDE)],
        [held_blocks(1024)],
        places,
        (m, *halves),
        2 * LEN * D * 2 * D,
    )


def turn_kernel(
    places, exit_layer, labels, n1, f, fp, cot, vec, pool_a, pool_b, classes, bias, live_count,
    y, half, dh2, low, sums, ramp, pool
):
    step = pl.program_id(0)
    middle = n1[...] * vec[0:1, :] + vec[1:2, :]
    total = f[...].astype(WIDE) + fp[...].astype(WIDE)
    normed, spread = normalize(middle + total + vec[5:6, :])
    result = normed * vec[2:3, :] + vec[3:4, :]
    low_result = result.astype(LOW)
    y[...] = low_result

    @pl.when(step // 2 == places[CORE_AT])
    def _():
        half[...] = low_result

    leaves = exit_layer[places[0]]
    grad = cot[...].astype(WIDE) * jnp.where(leaves > LAYER, 1.0, 0.0)
    dh2[...] = grad

    @pl.when(step == 0)
    def _():
        sums[...] = jnp.zeros_like(sums)
        own = places[CORE_AT]

        @pl.when(own == 0)
        def _():
            pool[:, 0:384] = pool_a[...]
            pool[:, 384:D] = pool_b[...]

        @pl.when(own == 1)
        def _():
            pool[:, 0:384] = pool_b[...]
            pool[:, 384:D] = pool_a[...]

        count = 16
        head = result[0:count, :].astype(LOW)
        pooled = jnp.tanh(dot(head, pool[...]) + vec[6:7, :])
        pooled_low = pooled.astype(LOW)
        lane = lax.broadcasted_iota(jnp.int32, (count, 128), 1)
        row = lax.broadcasted_iota(jnp.int32, (count, 128), 0)
        valid = lane < 3
        logits = dot(pooled_low, classes[...]) + bias[0:1, :]
        top = jnp.max(jnp.where(valid, logits, -jnp.inf), axis=1, keepdims=True)
        shifted = logits - top
        log_sum = jnp.log(
            jnp.sum(jnp.where(valid, jnp.exp(shifted), 0.0), axis=1, keepdims=True)
        )
        log_probs = jnp.where(valid, shifted - log_sum, 0.0)
        probs = jnp.where(valid, jnp.exp(log_probs), 0.0)
        live = jnp.where(leaves >= LAYER, 1.0, 0.0)
        entropy = -live * jnp.sum(probs * log_probs, axis=1, keepdims=True)
        onehot = jnp.where(lane == labels[places[0]], 1.0, 0.0)
        grad_logits = live * (probs - onehot) / live_count[0:1, 0:1]
        grad_logits = jnp.where(valid & (row == 0), grad_logits, 0.0).astype(LOW)
        grad_pre = (dot_nt(grad_logits, classes[...]) * (1.0 - pooled * pooled)).astype(LOW)
        grad_head = dot_nt(grad_pre, pool[...])
        dh2[0:count, :] = dh2[0:count, :] + grad_head
        sums[3:4, :] = grad_pre[0:1, :].astype(WIDE)
        of_class = dot_tn(grad_logits, pooled_low)
        sums[4:7, :] = of_class[0:3, :]
        last = jnp.where(lane == 3, entropy, grad_logits.astype(WIDE))
        sums[7:8, 0:128] = last[0:1, :]
        ramp[0:1, :] = head[0:1, :].astype(WIDE)
        ramp[1:2, :] = grad_pre[0:1, :].astype(WIDE)

    grad = dh2[...]
    sums[0:1, :] += jnp.sum(grad * normed, axis=0, keepdims=True)
    sums[1:2, :] += jnp.sum(grad, axis=0, keepdims=True)
    back = norm_back(grad * vec[2:3, :], normed, spread)
    sums[2:3, :] += jnp.sum(back, axis=0, keepdims=True)
    dh2[...] = back
    low[...] = back.astype(LOW)


def own_rows(step):
    return pl.BlockSpec((step, D), lambda i, places: (places[0] * (LEN // step) + i, 0))


def half_rows(step, sibling=False):
    count = LEN // step // 2

    def at(i, places):
        core = 1 - places[CORE_AT] if sibling else places[CORE_AT]
        return jnp.clip(i - count * core, 0, count - 1), 0

    return pl.BlockSpec((step, D), at)


def turn(places, exit_layer, labels, n1, f, fp, cotangent, vec, pool_a, pool_b, classes, bias, live_count):
    step = 256
    args = (exit_layer, labels, n1, f, fp, cotangent, vec, pool_a, pool_b, classes, bias, live_count)
    return call(
        turn_kernel,
        "turn",
        (LEN // step,),
        [pl.BlockSpec(memory_space=pltpu.SMEM)] * 2
        + [rows(step, D)] * 3
        + [own_rows(step)]
        + [whole(a) for a in args[6:]],
        [own_rows(step), half_rows(step)]
        + [rows(step, D)] * 2
        + [pl.BlockSpec((8, D), lambda *_: (0, 0))] * 2,
        [shape((2 * LEN, D), LOW), shape((LEN // 2, D), LOW)]
        + [shape((LEN, D), WIDE), shape((LEN, D), LOW)]
        + [shape((8, D), WIDE)] * 2,
        [pltpu.VMEM((D, D), LOW)],
        places,
        args,
        LEN * D * 60,
    )


def feed_back_kernel(places, dh2, slope, w_down, w_up, du, dx, sums):
    grad = dot(dh2[...], w_down[...]) * slope[...].astype(WIDE)
    grad = grad.astype(LOW)
    du[...] = grad
    dx[...] = dot_nt(grad, w_up[...]).astype(LOW)

    @pl.when(pl.program_id(0) == 0)
    def _():
        sums[...] = jnp.zeros_like(sums)

    sums[0:1, :] += jnp.sum(grad.astype(WIDE), axis=0, keepdims=True)


def feed_back(places, dh2, slope, w_down, w_up):
    step = 256
    args = (dh2, slope, w_down, w_up)
    return call(
        feed_back_kernel,
        "feed_back",
        (LEN // step,),
        [rows(step, D), rows(step, 2 * D), whole(w_down), whole(w_up)],
        [rows(step, 2 * D), rows(step, D), pl.BlockSpec((8, 2 * D), lambda *_: (0, 0))],
        [shape((LEN, 2 * D), LOW), shape((LEN, D), LOW), shape((8, 2 * D), WIDE)],
        [],
        places,
        args,
        4 * LEN * D * 2 * D,
    )


def feed_grad_kernel(places, dh2, m, middle, du, h0, h1, h2, h3, held, turned):
    for at, left, right in ((0, dh2, m), (D, middle, du)):
        turned[...] = left[...].T
        for side in range(2):
            for c in range(0, D, 256):
                part = dot(turned[...], right[:, D * side + c : D * side + c + 256]).astype(LOW)
                held[side * BLOCKS : (side + 1) * BLOCKS, :, at + c : at + c + 256] = part.reshape(
                    BLOCKS, BLOCK_ROWS, 256
                )
    scatter_blocks(places, held, (h0, h1, h2, h3))


def feed_grad(places, dh2, m, middle, du):
    args = (dh2, m, middle, du)
    return call(
        feed_grad_kernel,
        "feed_grad",
        (1,),
        [whole(a) for a in args],
        half_specs(2 * D),
        half_shapes(2 * D),
        [held_blocks(2 * D), pltpu.VMEM((D, LEN), LOW)],
        places,
        args,
        4 * LEN * D * 2 * D,
        vmem=40,
    )


def mid_kernel(
    places, dh2, dx, dxp, n1, rs1, vec, w_out, turn_sums, up_sums, ramp, dh1, low, do, sums
):
    @pl.when(pl.program_id(0) == 0)
    def _():
        row = lax.broadcasted_iota(jnp.int32, sums.shape, 0)
        at = 16 + 2 * places[SLOT_AT]
        slots = jnp.where(row == at, ramp[0:1, :], jnp.where(row == at + 1, ramp[1:2, :], 0.0))
        sums[...] = slots
        sums[0:8, :] = turn_sums[...]
        sums[11:12, :] = up_sums[0:1, 0:D]
        sums[12:13, :] = up_sums[0:1, D : 2 * D]

    total = dx[...].astype(WIDE) + dxp[...].astype(WIDE)
    grad = dh2[...] + total
    normed = n1[...]
    sums[8:9, :] += jnp.sum(grad * normed, axis=0, keepdims=True)
    sums[9:10, :] += jnp.sum(grad, axis=0, keepdims=True)
    back = norm_back(grad * vec[0:1, :], normed, rs1[:, 0:1])
    sums[10:11, :] += jnp.sum(back, axis=0, keepdims=True)
    dh1[...] = back
    back_low = back.astype(LOW)
    low[...] = back_low
    do[...] = dot(back_low, w_out[...]).astype(LOW)


def mid(places, dh2, dx, dxp, n1, rs1, vec, w_out, turn_sums, up_sums, ramp, slots):
    step = 256
    args = (dh2, dx, dxp, n1, rs1, vec, w_out, turn_sums, up_sums, ramp)
    count = 16 + 2 * slots
    return call(
        mid_kernel,
        "middle_back",
        (LEN // step,),
        [rows(step, D)] * 4 + [rows(step, 128)] + [whole(a) for a in args[5:]],
        [rows(step, D)] * 2 + [rows(step, 384), pl.BlockSpec((count, D), lambda *_: (0, 0))],
        [shape((LEN, D), WIDE), shape((LEN, D), LOW), shape((LEN, 384), LOW), shape((count, D), WIDE)],
        [],
        places,
        args,
        2 * LEN * D * 384,
    )


def attend_back_kernel(
    places, q_ref, k_ref, v_ref, do_ref, inv_ref, p_ref, dq_ref, dk_ref, dv_ref, ds_ref, held
):
    first = first_of_pair()
    zero = jnp.zeros((), LOW)
    n = k_ref.shape[0]
    k = k_ref[...]
    v = v_ref[...]
    k_own = [jnp.where(first, k, zero), jnp.where(first, zero, k)]
    scaled = (do_ref[...].astype(WIDE) * inv_ref[...]).astype(LOW)
    held[...] = scaled
    step = 256
    for i in range(n // step):
        at = pl.ds(i * step, step)
        d = held[at, :]
        total = None
        for head in range(2):
            mine = jnp.where(first, d, zero) if head == 0 else jnp.where(first, zero, d)
            grad_weight = dot_nt(mine, v)
            weight = p_ref[head, at, :].astype(WIDE)
            product = weight * grad_weight
            inner = jnp.sum(product, axis=1, keepdims=True)
            inner = inner * inv_ref[at, pl.ds(HD * head, 1)]
            grad_score = (product - weight * inner).astype(LOW)
            ds_ref[head, at, :] = grad_score
            part = dot(grad_score, k_own[head])
            total = part if total is None else total + part
        dq_ref[at, :] = (total * HD**-0.5).astype(LOW)
    scaled_t = scaled.T
    q_t = q_ref[...].T
    grad_v = jnp.concatenate(
        [dot(scaled_t[0:HD], p_ref[0]), dot(scaled_t[HD : 2 * HD], p_ref[1])], axis=0
    )
    dv_ref[...] = grad_v.T.astype(LOW)
    grad_k = jnp.concatenate(
        [dot(q_t[0:HD], ds_ref[0]), dot(q_t[HD : 2 * HD], ds_ref[1])], axis=0
    )
    dk_ref[...] = (grad_k * HD**-0.5).T.astype(LOW)


def attend_back(places, q, k, v, do, inv, p):
    at = pl.BlockSpec((LEN, 128), lambda i, *_: (0, i))
    return call(
        attend_back_kernel,
        "attend_backward",
        (3,),
        [at] * 5 + [pl.BlockSpec((2, LEN, LEN), lambda i, *_: (i, 0, 0))],
        [at] * 3,
        [shape((LEN, 384), LOW)] * 3,
        [pltpu.VMEM((2, LEN, LEN), LOW), pltpu.VMEM((LEN, 128), LOW)],
        places,
        (q, k, v, do, inv, p),
        8 * 6 * LEN * LEN * 256,
        vmem=36,
    )


def narrow_grad_kernel(share, places, left, dh1, o, *refs):
    grads, halves, (held, turned) = refs[:3], refs[3:7], refs[7:]
    turned[...] = left[...].T
    marks = []
    for i in range(3):
        right = grads[i][...]
        from_pairs(dot(turned[...], right).astype(LOW), held, 128 * i, 512 + 64 * i)
        if i != 1:
            marks.append(jnp.sum(right.astype(WIDE), axis=0, keepdims=True))
    turned[...] = dh1[...].T
    from_pairs(dot(turned[...], o[...]).astype(LOW), held, 384, 704)
    row = lax.rem(lax.broadcasted_iota(jnp.int32, (BLOCK_ROWS, 128), 0), share)
    for side in range(2):
        block = jnp.zeros((BLOCK_ROWS, 128), WIDE)
        for i, mark in enumerate(marks):
            narrow = mark[:, 256 + 64 * side : 320 + 64 * side]
            pieces = (mark[:, 128 * side : 128 * (side + 1)], jnp.concatenate([narrow, narrow], axis=1))
            for j, piece in enumerate(pieces):
                block = jnp.where(row == 2 * i + j, piece, block)
        for p in range(BLOCKS):
            held[side * BLOCKS + p, :, MARKS_AT:MARKED_WIDTH] = block.astype(LOW)
    scatter_blocks(places, held, halves, ALONG)


def narrow_grad(places, share, tokens, dh1, o, grads):
    args = (tokens, dh1, o, *grads)
    return call(
        functools.partial(narrow_grad_kernel, share),
        "narrow_grad",
        (1,),
        [own_rows(LEN)] + [whole(a) for a in args[1:]],
        half_specs(MARKED_WIDTH),
        half_shapes(MARKED_WIDTH),
        [held_blocks(MARKED_WIDTH), pltpu.VMEM((D, LEN), LOW)],
        places,
        args,
        2 * LEN * D * 1536,
    )


def input_kernel(places, *refs):
    grads, w, (keep, send) = refs[:3], refs[3], refs[4:]
    total = None
    for i in range(3):
        part = dot_nt(grads[i][...], w[i])
        total = part if total is None else total + part
    total = total.astype(LOW)
    mine = pl.program_id(0) // 2 == places[CORE_AT]

    @pl.when(mine)
    def _():
        keep[...] = total

    @pl.when(jnp.logical_not(mine))
    def _():
        send[...] = total


def input_grad(places, grads, w):
    step = 256
    return call(
        input_kernel,
        "input_grad",
        (LEN // step,),
        [rows(step, 384)] * 3 + [whole(w)],
        [half_rows(step), half_rows(step, True)],
        [shape((LEN // 2, D), LOW)] * 2,
        [],
        places,
        (*grads, w),
        2 * LEN * D * 1152,
    )


def finish_kernel(places, dh1, keep, other, half):
    total = keep[...].astype(WIDE) + other[...].astype(WIDE)
    half[...] = (dh1[...] + total).astype(LOW)


def finish(places, dh1, keep, other):
    step = 128
    count = LEN // 2 // step
    return call(
        finish_kernel,
        "finish",
        (count,),
        [pl.BlockSpec((step, D), lambda i, places: (count * places[CORE_AT] + i, 0))]
        + [rows(step, D)] * 2,
        [rows(step, D)],
        [shape((LEN // 2, D), LOW)],
        [],
        places,
        (dh1, keep, other),
        LEN * D * 3,
    )[0]


def place_kernel(count, places, *refs):
    half = LEN // 2
    ins, out, sems = refs[-2 - count : -2], refs[-2], refs[-1]
    side, core = places[0], places[CORE_AT]
    at = [(1 - side, core), (1 - side, 1 - core), (side, core), (side, 1 - core)]
    copies = []
    for i, ref in enumerate(ins):
        first = pl.multiple_of((2 * at[i][0] + at[i][1]) * half, half)
        copies.append(pltpu.make_async_copy(ref, out.at[pl.ds(first, half)], sems.at[i]))
        copies[-1].start()
    for copy in copies:
        copy.wait()


def place(places, kept, quarters):
    first = [] if kept is None else [kept]
    return call(
        functools.partial(place_kernel, len(quarters)),
        "place",
        (1,),
        [pl.BlockSpec(memory_space=pl.ANY)] * len(first) + [whole(a) for a in quarters],
        [pl.BlockSpec(memory_space=pl.ANY)],
        [shape((2 * LEN, D), LOW)],
        [pltpu.SemaphoreType.DMA((len(quarters),))],
        places,
        (*first, *quarters),
        1,
        vmem=12,
        aliases={} if kept is None else {1: 0},
    )[0]


def update(places, name, pieces, width, masters, kernel, extra):
    counts = tuple(len(group) for group in pieces)
    args = [a for group in pieces for a in group]
    specs = [
        pl.BlockSpec((1, a.shape[1], width), lambda *_: (0, 0, 0))
        if a.ndim == 3
        else pl.BlockSpec(a.shape, lambda *_: (0, 0))
        for a in args
    ]
    flat = [a for triple in masters for a in triple]
    outs = []
    for weight, first, second in masters:
        outs += [shape(weight.shape, WIDE)] * 3 + [shape(weight.shape, LOW)]
    outs += extra
    return call(
        functools.partial(kernel, counts),
        name,
        (1,),
        specs + [whole(a) for a in flat],
        [whole(o) for o in outs],
        outs,
        [],
        places,
        (*args, *flat),
        1,
        vmem=60,
    )


def step_matrix(ins, outs, at, grad, rate):
    new, first, second = adamw(ins[0][at], ins[1][at], ins[2][at], grad, rate, DECAY)
    outs[0][at] = new
    outs[1][at] = first
    outs[2][at] = second
    outs[3][at] = new.astype(LOW)


def update_feed_kernel(counts, places, *refs):
    total = sum(counts)
    grad = sum_pieces(refs[:total], counts)
    ins, outs = refs[total : total + 6], refs[total + 6 :]
    step_matrix(ins[0:3], outs[0:4], ..., grad[:, 0:D], RATE * FF ** (-0.5))
    step_matrix(ins[3:6], outs[4:8], ..., grad[:, D : 2 * D], RATE * D ** (-0.5))


def update_narrow_kernel(counts, places, *refs):
    total = sum(counts)
    grad = sum_pieces(refs[:total], counts)
    ins, outs = refs[total : total + 6], refs[total + 6 :]

    def columns(i):
        return jnp.concatenate(
            [grad[:, 128 * i : 128 * (i + 1)], grad[:, 512 + 64 * i : 576 + 64 * i]], axis=1
        )

    for i in range(3):
        step_matrix(ins[0:3], outs[0:4], i, columns(i), RATE * D ** (-0.5))
    step_matrix(ins[3:6], outs[4:8], ..., columns(3).T, RATE * max(1, 2 * D // LEN) ** (-0.5))
    outs[8][...] = grad[0:8, MARKS_AT:MARKED_WIDTH]


def per_device(
    dp_count,
    mp_count,
    tokens,
    cotangent,
    exit_layer,
    labels,
    qkv_weight,
    qkv_first,
    qkv_second,
    out_weight,
    out_first,
    out_second,
    up_weight,
    up_first,
    up_second,
    down_weight,
    down_first,
    down_second,
    pool_weight,
    pool_first,
    pool_second,
    qv_bias,
    qv_first,
    qv_second,
    up_bias,
    upb_first,
    upb_second,
    layer_vectors,
    vector_first,
    vector_second,
    class_weight,
    class_first,
    class_second,
):
    links = Links(dp_count, mp_count)
    side, core = links.side, links.core

    slot = 2 * links.dp + side
    places = jnp.concatenate([side[None], links.places(), core[None], slot[None]]).astype(jnp.int32)
    share = D // dp_count

    by_kind = [a.transpose(1, 0, 2) for a in (qkv_weight, qkv_first, qkv_second)]
    down_turned = [a.T for a in (down_weight, down_first, down_second)]
    qkv_spread = links.spread(pack_first(by_kind[0]))
    sent = qkv_spread.step()
    up_out, down_pool, biases = pack(
        places,
        exit_layer,
        after(up_weight, *sent),
        out_weight,
        down_turned[0],
        pool_weight,
        qv_bias,
        up_bias,
    )
    other_biases = links.swap(biases, SIDE)
    qkv_z = tuple(qkv_spread.last)
    sent = qkv_spread.step(up_out, other_biases)
    up_out_spread = links.spread(up_out)
    up_out_spread.step(*qkv_z)
    class_low = after(class_weight, *sent)
    classes = jnp.pad(class_low[:D].astype(LOW), ((0, 0), (0, 125)))
    class_bias = jnp.pad(class_low[D:], ((0, 0), (0, 125)))
    sent = qkv_spread.step(classes, class_bias)
    sent = up_out_spread.step(*sent)
    down_spread = links.spread(down_pool)
    sent = down_spread.step(*sent)

    biases = after(biases, *sent)
    q, k, v, w_qkv = project(places, tokens, biases, other_biases, qkv_spread.halves())
    sent = up_out_spread.step(q)
    q = after(q, *sent)
    o, inv, p = attend(places, q, k, v)
    sent = down_spread.step(o)
    o = after(o, *sent)
    z, w_out, w_up = project_out(places, o, up_out_spread.halves())
    zp = links.swap(z, CORE)
    sent = down_spread.step(z)
    z = after(z, *sent)
    m, slope, n1, rs1, middle_low = feed_up(
        places, tokens, z, zp, layer_vectors, biases, other_biases, w_up
    )
    f, w_down, pool_mine, live_count = feed_down(places, m, down_spread.halves())
    fp = links.swap(f, CORE)
    pool_other = links.swap(pool_mine, CORE)
    y, y_half, dh2, dh2_low, turn_sums, ramp = turn(
        places, exit_layer, labels, n1, f, fp, cotangent, layer_vectors, pool_mine, pool_other,
        classes, class_bias, live_count,
    )

    y_first = links.swap(y_half, SIDE)
    du, dx, up_sums = feed_back(places, dh2_low, slope, w_down, w_up)
    dxp = links.swap(dx, CORE)
    m, dh2_low = after((m, dh2_low), dx)
    feed_halves = feed_grad(places, dh2_low, m, middle_low, du)
    feed_fold = links.fold(feed_halves, ACROSS)
    feed_fold.step(y_first)
    dx = after(dx, *feed_halves)
    slots = 2 * dp_count
    dh1, dh1_low, do, sums = mid(
        places, dh2, dx, dxp, n1, rs1, layer_vectors, w_out, turn_sums, up_sums, ramp, slots
    )
    total = Total(links, sums)
    total.step()
    grads = attend_back(places, q, k, v, do, inv, p)
    sent = feed_fold.step(grads[0], vmem=12)
    grads = after(grads, *sent)
    token_keep, token_send = input_grad(places, grads, w_qkv)
    token_other = links.swap(token_send, CORE)
    grads = after(grads, token_keep)
    narrow_halves = narrow_grad(places, share, tokens, dh1_low, o, grads)
    narrow_fold = links.fold(narrow_halves, ALONG)
    narrow_fold.step()
    token_keep = after(token_keep, *narrow_halves)
    grad_half = finish(places, dh1, token_keep, token_other)
    first = links.swap(grad_half, SIDE)
    second_own = links.swap(grad_half, CORE)
    sent = total.step(grad_half)
    sent = feed_fold.step(*sent)
    y_second = links.swap(after(y_first, *sent), CORE)
    sent = narrow_fold.step(*sent)
    first = after(first, *sent)
    second = links.swap(first, CORE)
    sent = total.step(*sent)
    y = after(y, *sent)
    result = place(places, y, [y_first, y_second])
    feed_pieces = after(feed_fold.pieces(), result)
    feed_new = update(
        places,
        "update_feed",
        feed_pieces,
        2 * D,
        [down_turned, (up_weight, up_first, up_second)],
        update_feed_kernel,
        [],
    )
    sent = narrow_fold.step(feed_new[0])
    sent = total.step(*sent)
    tokens_grad = place(
        places, None, [first, after(second, *sent), grad_half, second_own]
    )
    sent = narrow_fold.step(tokens_grad)
    total.value, total.last = after((total.value, total.last), *sent)
    sums = total.result()
    down_new, down_first_new, down_second_new, down_copy = (a.T for a in feed_new[0:4])
    up_new, up_first_new, up_second_new, up_copy = feed_new[4:8]
    *narrow_new, marks = update(
        places,
        "update_narrow",
        narrow_fold.pieces(),
        MARKED_WIDTH,
        [by_kind, (out_weight, out_first, out_second)],
        update_narrow_kernel,
        [shape((8, 128), WIDE)],
    )
    qkv_new, qkv_first_new, qkv_second_new, qkv_copy = (
        a.transpose(1, 0, 2) for a in narrow_new[0:4]
    )
    out_new, out_first_new, out_second_new, out_copy = narrow_new[4:8]

    ramps = sums[16:].reshape(slots, 2, D)

    head_rows = lax.dynamic_slice_in_dim(ramps[:, 0], links.dp * share, share, 1)
    grad_pool = lax.dot_general(
        head_rows.astype(LOW),
        ramps[:, 1].astype(LOW),
        (((0,), (0,)), ((), ())),
        preferred_element_type=WIDE,
    )
    vector_sum = jnp.concatenate([sums[8:10], sums[0:2], sums[10:11], sums[2:4]], axis=0)
    class_sum = jnp.concatenate([sums[4:7].T, sums[7:8, 0:3]], axis=0)
    upb_sum = lax.dynamic_slice_in_dim(sums, 11 + side, 1, 0)[0]
    bias_sum = jnp.concatenate([marks[0:4:2], marks[1:4:2, 0:64]], axis=1)

    pool_new, pool_first_new, pool_second_new = adamw(
        pool_weight, pool_first, pool_second, grad_pool, RATE * D ** (-0.5), DECAY
    )
    qv_new, qv_first_new, qv_second_new = adamw(
        qv_bias, qv_first, qv_second, bias_sum, VECTOR_RATE, 0.0
    )
    upb_new, upb_first_new, upb_second_new = adamw(
        up_bias, upb_first, upb_second, upb_sum, VECTOR_RATE, 0.0
    )
    vector_new, vector_first_new, vector_second_new = adamw(
        layer_vectors, vector_first, vector_second, vector_sum, VECTOR_RATE, 0.0
    )
    class_new, class_first_new, class_second_new = adamw(
        class_weight, class_first, class_second, class_sum, RATE * (D // 4) ** (-0.5), DECAY
    )
    return (
        result,
        tokens_grad,
        sums[7, 3] / live_count[0, 0],
        qkv_new,
        qkv_first_new,
        qkv_second_new,
        qkv_copy,
        out_new,
        out_first_new,
        out_second_new,
        out_copy,
        up_new,
        up_first_new,
        up_second_new,
        up_copy,
        down_new,
        down_first_new,
        down_second_new,
        down_copy,
        pool_new,
        pool_first_new,
        pool_second_new,
        pool_new.astype(LOW),
        qv_new,
        qv_first_new,
        qv_second_new,
        upb_new,
        upb_first_new,
        upb_second_new,
        vector_new,
        vector_first_new,
        vector_second_new,
        class_new,
        class_first_new,
        class_second_new,
    )


def solution(mesh):
    in_specs = (
        P("dp", None),
        P("dp", None),
        P("dp"),
        P("dp"),
        P("dp", None, "mp"),
        P("dp", None, "mp"),
        P("dp", None, "mp"),
        P("mp", "dp"),
        P("mp", "dp"),
        P("mp", "dp"),
        P("dp", "mp"),
        P("dp", "mp"),
        P("dp", "mp"),
        P("mp", "dp"),
        P("mp", "dp"),
        P("mp", "dp"),
        P("dp", None),
        P("dp", None),
        P("dp", None),
        P(None, "mp"),
        P(None, "mp"),
        P(None, "mp"),
        P("mp"),
        P("mp"),
        P("mp"),
        P(),
        P(),
        P(),
        P(),
        P(),
        P(),
    )
    out_specs = (
        P("dp", None),
        P("dp", None),
        P(),
        P("dp", None, "mp"),
        P("dp", None, "mp"),
        P("dp", None, "mp"),
        P("dp", None, "mp"),
        P("mp", "dp"),
        P("mp", "dp"),
        P("mp", "dp"),
        P("mp", "dp"),
        P("dp", "mp"),
        P("dp", "mp"),
        P("dp", "mp"),
        P("dp", "mp"),
        P("mp", "dp"),
        P("mp", "dp"),
        P("mp", "dp"),
        P("mp", "dp"),
        P("dp", None),
        P("dp", None),
        P("dp", None),
        P("dp", None),
        P(None, "mp"),
        P(None, "mp"),
        P(None, "mp"),
        P("mp"),
        P("mp"),
        P("mp"),
        P(),
        P(),
        P(),
        P(),
        P(),
        P(),
    )
    one_device = functools.partial(per_device, mesh.shape["dp"], mesh.shape["mp"])
    return jax.shard_map(
        one_device, mesh=mesh, in_specs=in_specs, out_specs=out_specs, check_vma=False
    )
```

time: 464 us -> 271 us (0.58)
  waiting for transfers between devices: 161 us -> 56.5 us
  other arithmetic: 48.7 us -> 7.43 us
  starting transfers between devices: 86.6 us -> 59.6 us
  Pallas kernels: 133 us -> 119 us
    ppermute x76 -> x51, waiting for transfers between devices: 161 us -> 56.5 us  [swap(): return lax.ppermute(value, ('dp', 'mp'), pairs)]
    pallas_call x14 -> x18, Pallas kernels: 133 us -> 106 us  [call(): pl.pallas_call(kernel, out_shape=out_shape, grid_spec=pltpu.PrefetchScala...]
    ppermute x76 -> x51, starting transfers between devices: 86.6 us -> 59.6 us  [swap(): return lax.ppermute(value, ('dp', 'mp'), pairs)]
    convert_element_type x26 -> x0, other arithmetic: 23.7 us -> none  [the longest x18 13.8 us: fold(): parts.append(self.swap(send.astype(LOW), order[k]))]
    pallas_call x0 -> x6, Pallas kernels: none -> 13.1 us  [the longest x5 11.5 us: fold_add(): pl.pallas_call(functools.partial(fold_add_kernel, counts, apart), grid=(c...]
    select_n x12 -> x0, other arithmetic: 11.3 us -> none  [the longest x2 4.17 us: both_sequences(): jnp.where(links.side == 0, jnp.concatenate([mine, other], axis=0), jnp.co...]
    unnamed x136 -> x117, local copies, waits for them, and re-layouts: 12 us -> 17.7 us
  transfers between devices with their start and end apart: 76 -> 51, of which waited for: 23 -> 18; matrix products, arithmetic and copies ran while one was open for 14% -> 3% of each run, Pallas kernels for 27% -> 36%
where the time goes in v2:
time: 271 us; the launch traced here: 270 us
  Pallas kernels  119 us (44%)
  starting transfers between devices  59.6 us (22%)
  waiting for transfers between devices  56.5 us (21%)
  local copies, waits for them, and re-layouts  22 us (8%)
  other arithmetic  7.43 us (3%)
  between operations  4.01 us (1%)
    pallas_call x18, Pallas kernels, call(): pl.pallas_call(kernel, out_shape=out_shape, grid_spec=pltpu.PrefetchScala...  106 us
    ppermute x51, starting transfers between devices, swap(): return lax.ppermute(value, ('dp', 'mp'), pairs)  59.6 us
    ppermute x51, waiting for transfers between devices, swap(): return lax.ppermute(value, ('dp', 'mp'), pairs)  56.5 us
    unnamed x117, local copies, waits for them, and re-layouts  17.7 us
    pallas_call x5, Pallas kernels, fold_add(): pl.pallas_call(functools.partial(fold_add_kernel, counts, apart), grid=(c...  11.5 us
  transfers between devices with their start and end apart: 51, of which 18 were waited for; matrix products, arithmetic and copies ran while one was open for 3% of the time, Pallas kernels for 36%

profile of v2, /device:TPU:0, one launch (start us, length us, event | category | flops | bytes accessed | tf_op | source)
XLA Modules:
  0.0 270.0 jit_solution(15727613657562546384)
XLA Ops:
  2.4 5.0 %collective-permute-start.2 = (bf16[1,96,576]{2,1,0:T(8,128)(2,1)}, bf16[1,96,576]{2,1,0:T(8,128)(2,1)S(1)}, u32[]{:S(2)}, u32[]{:S(2)}) collective-permute-start(bf16[1,96,576]{2,1,0:T(8,128)(2,1)} %bitcast.37), channel_id=1, source_target_pairs={{0,24},{1,25},{2,26},{3,27},{4,28},{5,29},{6,30},{7,31},{8,16},{9,... | collective-permute-start | bytes 331784 | tf_op jit(solution)/shard_map/ppermute | solution.py:83
  31.8 4.2 %collective-permute-done.4 = bf16[1,96,960]{2,1,0:T(8,128)(2,1)S(1)} collective-permute-done((bf16[1,96,960]{2,1,0:T(8,128)(2,1)S(1)}, bf16[1,96,960]{2,1,0:T(8,128)(2,1)S(1)}, u32[]{:S(2)}, u32[]{:S(2)}) %collective-permute-start.4) | collective-permute-done | bytes 184352 | tf_op jit(solution)/shard_map/ppermute | solution.py:83
  36.1 3.7 %collective-permute-done.3 = bf16[1,96,960]{2,1,0:T(8,128)(2,1)S(1)} collective-permute-done((bf16[1,96,960]{2,1,0:T(8,128)(2,1)S(1)}, bf16[1,96,960]{2,1,0:T(8,128)(2,1)S(1)}, u32[]{:S(2)}, u32[]{:S(2)}) %collective-permute-start.3) | collective-permute-done | bytes 184352 | tf_op jit(solution)/shard_map/ppermute | solution.py:83
  45.5 4.4 %project.1 = (bf16[1024,384]{1,0:T(8,128)(2,1)S(1)}, bf16[1024,384]{1,0:T(8,128)(2,1)S(1)}, bf16[1024,384]{1,0:T(8,128)(2,1)S(1)}, bf16[3,768,384]{2,1,0:T(8,128)(2,1)S(1)}) custom-call(s32[67]{0:T(128)S(1)} %copy-done.28, bf16[2048,768]{1,0:T(8,128)(2,1)S(1)} %copy-done, f32[8,768]{1,0:T(8,128)S(1)} %copy-done.30, ...), custom_call_target="tpu_custom_call" | custom-call | flops 113246208 | bytes 568320 | tf_op jit(solution)/shard_map/project/pallas_call | solution.py:309
  54.5 13.3 %attend_forward.1 = (bf16[1024,384]{1,0:T(8,128)(2,1)S(1)}, f32[1024,384]{1,0:T(8,128)}, bf16[6,1024,1024]{2,1,0:T(8,128)(2,1)}) custom-call(s32[67]{0:T(128)S(1)} %copy-done.28, bf16[1024,384]{1,0:T(8,128)(2,1)S(1)} %get-tuple-element.231.q_ref, bf16[1024,384]{1,0:T(8,128)(2,1)S(1)} %get-tuple-element.232.k_ref, bf16[1024,384]{1,0:T(8,128)(2,1)S(1)} %get-tuple-element.233.v_ref), custom_call_target="tpu_custom_call" | custom-call | flops 402653184 | bytes 1081344 | tf_op jit(solution)/shard_map/attend_forward/pallas_call | solution.py:309
  79.7 7.6 %feed_up.1 = (bf16[1024,1536]{1,0:T(8,128)(2,1)S(1)}, bf16[1024,1536]{1,0:T(8,128)(2,1)S(1)}, f32[1024,768]{1,0:T(8,128)S(1)}, f32[1024,128]{1,0:T(8,128)S(1)}, bf16[1024,768]{1,0:T(8,128)(2,1)S(1)}) custom-call(s32[67]{0:T(128)S(1)} %copy-done.28, bf16[2048,768]{1,0:T(8,128)(2,1)S(1)} %copy-done, bf16[1024,768]{1,0:T(8,128)(2,1)S(1)} %get-tuple-element.245.z, ...), custom_call_target="tpu_custom_call" | custom-call | flops 150994944 | bytes 1265984 | tf_op jit(solution)/shard_map/feed_up/pallas_call | solution.py:309
  88.9 4.9 %collective-permute-done.22.h3 = bf16[8,48,1024]{2,1,0:T(8,128)(2,1)S(1)} collective-permute-done((bf16[8,48,1024]{2,1,0:T(8,128)(2,1)S(1)}, bf16[8,48,1024]{2,1,0:T(8,128)(2,1)S(1)}, u32[]{:S(2)}, u32[]{:S(2)}) %collective-permute-start.22) | collective-permute-done | bytes 786464 | tf_op jit(solution)/shard_map/ppermute | solution.py:83
  94.8 4.3 %feed_down.1 = (bf16[1024,768]{1,0:T(8,128)(2,1)S(1)}, bf16[768,1536]{1,0:T(8,128)(2,1)S(1)}, bf16[768,384]{1,0:T(8,128)(2,1)S(1)}, f32[8,128]{1,0:T(8,128)S(1)}) custom-call(s32[67]{0:T(128)S(1)} %copy-done.28, bf16[1024,1536]{1,0:T(8,128)(2,1)S(1)} %get-tuple-element.259.m, bf16[8,48,1024]{2,1,0:T(8,128)(2,1)S(1)} %constant_dynamic-update-slice_fusion.8.h0, ...), custom_call_target="tpu_custom_call" | custom-call | flops 150994944 | bytes 676096 | tf_op jit(solution)/shard_map/feed_down/pallas_call | solution.py:309
  99.7 3.7 %collective-permute-done.24.pool_b = bf16[768,384]{1,0:T(8,128)(2,1)S(1)} collective-permute-done((bf16[768,384]{1,0:T(8,128)(2,1)S(1)}, bf16[768,384]{1,0:T(8,128)(2,1)S(1)}, u32[]{:S(2)}, u32[]{:S(2)}) %collective-permute-start.24) | collective-permute-done | bytes 589856 | tf_op jit(solution)/shard_map/ppermute | solution.py:83
  103.5 6.7 %turn.1 = (bf16[2048,768]{1,0:T(8,128)(2,1)}, bf16[512,768]{1,0:T(8,128)(2,1)}, f32[1024,768]{1,0:T(8,128)S(1)}, bf16[1024,768]{1,0:T(8,128)(2,1)S(1)}, f32[8,768]{1,0:T(8,128)S(1)}, /*index=5*/f32[8,768]{1,0:T(8,128)S(1)}) custom-call(s32[67]{0:T(128)S(1)} %copy-done.28, s32[2]{0:T(128)S(1)} %copy-done.31, s32[2]{0:T(128)S(1)} %copy-done.32, ...), custom_call_target="tpu_custom_call" | custom-call | flops 2949120 | bytes 1221217 | tf_op jit(solution)/shard_map/turn/pallas_call | solution.py:309
  115.4 8.0 %feed_back.1 = (bf16[1024,1536]{1,0:T(8,128)(2,1)S(1)}, bf16[1024,768]{1,0:T(8,128)(2,1)}, f32[8,1536]{1,0:T(8,128)S(1)}) custom-call(s32[67]{0:T(128)S(1)} %copy-done.28, bf16[1024,768]{1,0:T(8,128)(2,1)S(1)} %get-tuple-element.258.dh2, bf16[1024,1536]{1,0:T(8,128)(2,1)S(1)} %copy-done.15, bf16[768,1536]{1,0:T(8,128)(2,1)S(1)} %get-tuple-element.256.w_down, ...), custom_call_target="tpu_custom_call" | custom-call | flops 301989888 | bytes 887808 | tf_op jit(solution)/shard_map/feed_back/pallas_call | solution.py:309
  123.4 7.0 %feed_grad.1 = (bf16[8,48,1536]{2,1,0:T(8,128)(2,1)S(1)}, bf16[8,48,1536]{2,1,0:T(8,128)(2,1)}, bf16[8,48,1536]{2,1,0:T(8,128)(2,1)S(1)}, bf16[8,48,1536]{2,1,0:T(8,128)(2,1)S(1)}) custom-call(s32[67]{0:T(128)S(1)} %copy-done.28, bf16[1024,768]{1,0:T(8,128)(2,1)S(1)} %get-tuple-element.258.dh2, bf16[1024,1536]{1,0:T(8,128)(2,1)S(1)} %get-tuple-element.259.m, ...), custom_call_target="tpu_custom_call" | custom-call | flops 301989888 | bytes 884736 | tf_op jit(solution)/shard_map/feed_grad/pallas_call | solution.py:309
  141.7 5.5 %middle_back.1 = (f32[1024,768]{1,0:T(8,128)S(1)}, bf16[1024,768]{1,0:T(8,128)(2,1)S(1)}, bf16[1024,384]{1,0:T(8,128)(2,1)S(1)}, f32[48,768]{1,0:T(8,128)S(1)}) custom-call(s32[67]{0:T(128)S(1)} %copy-done.28, f32[1024,768]{1,0:T(8,128)S(1)} %copy-done.13, bf16[1024,768]{1,0:T(8,128)(2,1)} %get-tuple-element.266.dx, bf16[1024,768]{1,0:T(8,128)(2,1)S(1)} %copy-done.22, ...), custom_call_target="tpu_custom_call" | custom-call | flops 37748736 | bytes 1020224 | tf_op jit(solution)/shard_map/middle_back/pallas_call | solution.py:309
  147.2 21.0 %attend_backward.1 = (bf16[1024,384]{1,0:T(8,128)(2,1)S(1)}, bf16[1024,384]{1,0:T(8,128)(2,1)S(1)}, bf16[1024,384]{1,0:T(8,128)(2,1)S(1)}) custom-call(s32[67]{0:T(128)S(1)} %copy-done.28, bf16[1024,384]{1,0:T(8,128)(2,1)S(1)} %copy-done.8, bf16[1024,384]{1,0:T(8,128)(2,1)S(1)} %copy-done.10, bf16[1024,384]{1,0:T(8,128)(2,1)S(1)} %get-tuple-element.233.v_ref, ...), custom_call_target="tpu_custom_call" | custom-call | flops 805306368 | bytes 1228800 | tf_op jit(solution)/shard_map/attend_backward/pallas_call | solution.py:309
  170.7 4.1 %input_grad.1 = (bf16[512,768]{1,0:T(8,128)(2,1)S(1)}, bf16[512,768]{1,0:T(8,128)(2,1)S(1)}) custom-call(s32[67]{0:T(128)S(1)} %copy-done.28, bf16[1024,384]{1,0:T(8,128)(2,1)S(1)} %get-tuple-element.297.refs_0_, bf16[1024,384]{1,0:T(8,128)(2,1)S(1)} %get-tuple-element.298.refs_1_, bf16[1024,384]{1,0:T(8,128)(2,1)S(1)} %get-tuple-element.299.refs_2_, ...), custom_call_target="tpu_custom_call" | custom-call | flops 113246208 | bytes 356352 | tf_op jit(solution)/shard_map/input_grad/pallas_call | solution.py:309
  176.3 4.3 %narrow_grad.1 = (bf16[8,48,896]{2,1,0:T(8,128)(2,1)S(1)}, bf16[8,48,896]{2,1,0:T(8,128)(2,1)S(1)}, bf16[8,48,896]{2,1,0:T(8,128)(2,1)S(1)}, bf16[8,48,896]{2,1,0:T(8,128)(2,1)S(1)}) custom-call(s32[67]{0:T(128)S(1)} %copy-done.28, bf16[2048,768]{1,0:T(8,128)(2,1)S(1)} %copy-done, bf16[1024,768]{1,0:T(8,128)(2,1)S(1)} %get-tuple-element.296.dh1, ...), custom_call_target="tpu_custom_call" | custom-call | flops 150994944 | bytes 663552 | tf_op jit(solution)/shard_map/narrow_grad/pallas_call | solution.py:309
  186.4 4.7 %collective-permute-done.34.refs_2_ = bf16[4,48,1536]{2,1,0:T(8,128)(2,1)S(1)} collective-permute-done((bf16[4,48,1536]{2,1,0:T(8,128)(2,1)S(1)}, bf16[4,48,1536]{2,1,0:T(8,128)(2,1)S(1)}, u32[]{:S(2)}, u32[]{:S(2)}) %collective-permute-start.34) | collective-permute-done | bytes 589856 | tf_op jit(solution)/shard_map/ppermute | solution.py:83
  191.9 3.7 %fold_add.6 = (bf16[1,96,1536]{2,1,0:T(8,128)(2,1)}, bf16[1,96,1536]{2,1,0:T(8,128)(2,1)}, bf16[1,96,1536]{2,1,0:T(8,128)(2,1)}) custom-call(bf16[8,48,1536]{2,1,0:T(8,128)(2,1)} %copy-done.3, bf16[8,48,1536]{2,1,0:T(8,128)(2,1)} %copy-done.5, bf16[4,48,1536]{2,1,0:T(8,128)(2,1)} %copy-done.34, bf16[8,48,1536]{2,1,0:T(8,128)(2,1)} %copy-done.4, ...), custom_call_target="tpu_custom_call" | custom-call | flops 442368 | bytes 4608 | tf_op jit(solution)/shard_map/fold_add/pallas_call | solution.py:262
  197.3 8.2 %collective-permute-done.32.refs_1_ = bf16[8,48,896]{2,1,0:T(8,128)(2,1)} collective-permute-done((bf16[8,48,896]{2,1,0:T(8,128)(2,1)S(1)}, bf16[8,48,896]{2,1,0:T(8,128)(2,1)}, u32[]{:S(2)}, u32[]{:S(2)}) %collective-permute-start.32) | collective-permute-done | bytes 688160 | tf_op jit(solution)/shard_map/ppermute | solution.py:83
  213.8 5.9 %collective-permute-done.31 = f32[48,768]{1,0:T(8,128)S(1)} collective-permute-done((f32[48,768]{1,0:T(8,128)S(1)}, f32[48,768]{1,0:T(8,128)S(1)}, u32[]{:S(2)}, u32[]{:S(2)}) %collective-permute-start.31) | collective-permute-done | bytes 147488 | tf_op jit(solution)/shard_map/ppermute | solution.py:83
  220.3 6.3 %collective-permute-done.43.refs_7_ = bf16[1,96,1536]{2,1,0:T(8,128)(2,1)} collective-permute-done((bf16[1,96,1536]{2,1,0:T(8,128)(2,1)}, bf16[1,96,1536]{2,1,0:T(8,128)(2,1)}, u32[]{:S(2)}, u32[]{:S(2)}) %collective-permute-start.43) | collective-permute-done | bytes 294944 | tf_op jit(solution)/shard_map/ppermute | solution.py:83
  232.6 4.3 %update_feed.1 = (f32[96,768]{1,0:T(8,128)}, f32[96,768]{1,0:T(8,128)}, f32[96,768]{1,0:T(8,128)}, bf16[96,768]{1,0:T(8,128)(2,1)}, f32[96,768]{1,0:T(8,128)}, /...) custom-call(s32[67]{0:T(128)} %pad_add_fusion.places, bf16[8,48,1536]{2,1,0:T(8,128)(2,1)} %copy-done.3, ...), custom_call_target="tpu_custom_call" | custom-call | bytes 663552 | tf_op jit(solution)/shard_map/update_feed/pallas_call | solution.py:309
  239.6 4.2 %collective-permute-start.47 = (bf16[2,48,896]{2,1,0:T(8,128)(2,1)}, bf16[2,48,896]{2,1,0:T(8,128)(2,1)S(1)}, u32[]{:S(2)}, u32[]{:S(2)}) collective-permute-start(bf16[2,48,896]{2,1,0:T(8,128)(2,1)} %get-tuple-element.344), channel_id=1, source_target_pairs={{0,8},{1,9},{2,10},{3,11},{4,12},{5,13},{6,14},{7,15},{8,0},{9,1},... | collective-permute-start | bytes 516104 | tf_op jit(solution)/shard_map/ppermute | solution.py:83
  263.2 3.7 %update_narrow.1 = (f32[3,96,192]{2,1,0:T(8,128)}, f32[3,96,192]{2,1,0:T(8,128)}, f32[3,96,192]{2,1,0:T(8,128)}, bf16[3,96,192]{2,1,0:T(8,128)(2,1)}, f32[192,96...) custom-call(s32[67]{0:T(128)} %pad_add_fusion.places, ...), custom_call_target="tpu_custom_call" | custom-call | bytes 367360 | tf_op jit(solution)/shard_map/update_narrow/pallas_call | solution.py:309
  (270 shorter events, 117.3 us)
Async XLA Ops:
  27.5 16.2 %collective-permute-start.10 = (bf16[8,48,576]{2,1,0:T(8,128)(2,1)S(1)}, bf16[8,48,576]{2,1,0:T(8,128)(2,1)S(1)}, u32[]{:S(2)}, u32[]{:S(2)}) collective-permute-start(bf16[8,48,576]{2,1,0:T(8,128)(2,1)S(1)} %constant_dynamic-update-slice_fusion.2.h2), channel_id=1, source_target_pairs={{0,4},{1,5},{2,6},{3,7},{4,0},{5,1},{6,2},{7,3},{8,12},{9,13},{10,... | collective-permute-start | bytes 1327112 | tf_op jit(solution)/shard_map/ppermute | solution.py:83
  28.2 15.5 %collective-permute-start.9 = (bf16[8,48,576]{2,1,0:T(8,128)(2,1)S(1)}, bf16[8,48,576]{2,1,0:T(8,128)(2,1)S(1)}, u32[]{:S(2)}, u32[]{:S(2)}) collective-permute-start(bf16[8,48,576]{2,1,0:T(8,128)(2,1)S(1)} %constant_dynamic-update-slice_fusion.h0), channel_id=1, source_target_pairs={{0,2},{1,3},{2,0},{3,1},{4,6},{5,7},{6,4},{7,5},{8,10},{9,11},{10,... | collective-permute-start | bytes 1327112 | tf_op jit(solution)/shard_map/ppermute | solution.py:83
  41.1 26.7 %collective-permute-start.15 = (bf16[1,96,1024]{2,1,0:T(8,128)(2,1)S(1)}, bf16[1,96,1024]{2,1,0:T(8,128)(2,1)S(1)}, u32[]{:S(2)}, u32[]{:S(2)}) collective-permute-start(bf16[1,96,1024]{2,1,0:T(8,128)(2,1)S(1)} %bitcast.45), channel_id=1, source_target_pairs={{0,24},{1,25},{2,26},{3,27},{4,28},{5,29},{6,30},{7,31},{8,16},{9,... | collective-permute-start | bytes 589832 | tf_op jit(solution)/shard_map/ppermute | solution.py:83
  43.7 24.1 %collective-permute-start.14 = (bf16[1,96,1024]{2,1,0:T(8,128)(2,1)S(1)}, bf16[1,96,1024]{2,1,0:T(8,128)(2,1)S(1)}, u32[]{:S(2)}, u32[]{:S(2)}) collective-permute-start(bf16[1,96,1024]{2,1,0:T(8,128)(2,1)S(1)} %bitcast.46), channel_id=1, source_target_pairs={{0,8},{1,9},{2,10},{3,11},{4,12},{5,13},{6,14},{7,15},{8,0},{9,1},... | collective-permute-start | bytes 589832 | tf_op jit(solution)/shard_map/ppermute | solution.py:83
  43.7 24.1 %collective-permute-start.13 = (bf16[1,96,1024]{2,1,0:T(8,128)(2,1)S(1)}, bf16[1,96,1024]{2,1,0:T(8,128)(2,1)S(1)}, u32[]{:S(2)}, u32[]{:S(2)}) collective-permute-start(bf16[1,96,1024]{2,1,0:T(8,128)(2,1)S(1)} %bitcast.47), channel_id=1, source_target_pairs={{0,16},{1,17},{2,18},{3,19},{4,20},{5,21},{6,22},{7,23},{8,24},{9,... | collective-permute-start | bytes 589832 | tf_op jit(solution)/shard_map/ppermute | solution.py:83
  51.2 17.9 %collective-permute-start.17 = (bf16[8,48,960]{2,1,0:T(8,128)(2,1)S(1)}, bf16[8,48,960]{2,1,0:T(8,128)(2,1)S(1)}, u32[]{:S(2)}, u32[]{:S(2)}) collective-permute-start(bf16[8,48,960]{2,1,0:T(8,128)(2,1)S(1)} %constant_dynamic-update-slice_fusion.6.h2), channel_id=1, source_target_pairs={{0,4},{1,5},{2,6},{3,7},{4,0},{5,1},{6,2},{7,3},{8,12},{9,13},{10,... | collective-permute-start | bytes 2211848 | tf_op jit(solution)/shard_map/ppermute | solution.py:83
  52.8 17.8 %collective-permute-start.16 = (bf16[8,48,960]{2,1,0:T(8,128)(2,1)S(1)}, bf16[8,48,960]{2,1,0:T(8,128)(2,1)S(1)}, u32[]{:S(2)}, u32[]{:S(2)}) collective-permute-start(bf16[8,48,960]{2,1,0:T(8,128)(2,1)S(1)} %constant_dynamic-update-slice_fusion.4.h0), channel_id=1, source_target_pairs={{0,2},{1,3},{2,0},{3,1},{4,6},{5,7},{6,4},{7,5},{8,10},{9,11},{10,... | collective-permute-start | bytes 2211848 | tf_op jit(solution)/shard_map/ppermute | solution.py:83
  77.5 16.4 %collective-permute-start.22 = (bf16[8,48,1024]{2,1,0:T(8,128)(2,1)S(1)}, bf16[8,48,1024]{2,1,0:T(8,128)(2,1)S(1)}, u32[]{:S(2)}, u32[]{:S(2)}) collective-permute-start(bf16[8,48,1024]{2,1,0:T(8,128)(2,1)S(1)} %constant_dynamic-update-slice_fusion.10.h2), channel_id=1, source_target_pairs={{0,4},{1,5},{2,6},{3,7},{4,0},{5,1},{6,2},{7,3},{8,12},{9,13},{10,... | collective-permute-start | bytes 2359304 | tf_op jit(solution)/shard_map/ppermute | solution.py:83
  78.2 16.6 %collective-permute-start.21 = (bf16[8,48,1024]{2,1,0:T(8,128)(2,1)S(1)}, bf16[8,48,1024]{2,1,0:T(8,128)(2,1)S(1)}, u32[]{:S(2)}, u32[]{:S(2)}) collective-permute-start(bf16[8,48,1024]{2,1,0:T(8,128)(2,1)S(1)} %constant_dynamic-update-slice_fusion.8.h0), channel_id=1, source_target_pairs={{0,2},{1,3},{2,0},{3,1},{4,6},{5,7},{6,4},{7,5},{8,10},{9,11},{10,... | collective-permute-start | bytes 2359304 | tf_op jit(solution)/shard_map/ppermute | solution.py:83
  111.8 19.9 %collective-permute-start.27 = (bf16[512,768]{1,0:T(8,128)(2,1)}, bf16[512,768]{1,0:T(8,128)(2,1)}, u32[]{:S(2)}, u32[]{:S(2)}) collective-permute-start(bf16[512,768]{1,0:T(8,128)(2,1)} %get-tuple-element.280), channel_id=1, source_target_pairs={{0,2},{1,3},{2,0},{3,1},{4,6},{5,7},{6,4},{7,5},{8,10},{9,11},{10,... | collective-permute-start | bytes 2359304 | tf_op jit(solution)/shard_map/ppermute | solution.py:83
  131.7 36.6 %collective-permute-start.28 = (bf16[8,48,1536]{2,1,0:T(8,128)(2,1)}, bf16[8,48,1536]{2,1,0:T(8,128)(2,1)S(1)}, u32[]{:S(2)}, u32[]{:S(2)}) collective-permute-start(bf16[8,48,1536]{2,1,0:T(8,128)(2,1)} %get-tuple-element.282), channel_id=1, source_target_pairs={{0,2},{1,3},{2,0},{3,1},{4,6},{5,7},{6,4},{7,5},{8,10},{9,11},{10,... | collective-permute-start | bytes 3538952 | tf_op jit(solution)/shard_map/ppermute | solution.py:83
  133.4 34.9 %collective-permute-start.29 = (bf16[8,48,1536]{2,1,0:T(8,128)(2,1)S(1)}, bf16[8,48,1536]{2,1,0:T(8,128)(2,1)S(1)}, u32[]{:S(2)}, u32[]{:S(2)}) collective-permute-start(bf16[8,48,1536]{2,1,0:T(8,128)(2,1)S(1)} %get-tuple-element.284), channel_id=1, source_target_pairs={{0,4},{1,5},{2,6},{3,7},{4,0},{5,1},{6,2},{7,3},{8,12},{9,13},{10,... | collective-permute-start | bytes 3538952 | tf_op jit(solution)/shard_map/ppermute | solution.py:83
  174.9 16.2 %collective-permute-start.34 = (bf16[4,48,1536]{2,1,0:T(8,128)(2,1)S(1)}, bf16[4,48,1536]{2,1,0:T(8,128)(2,1)S(1)}, u32[]{:S(2)}, u32[]{:S(2)}) collective-permute-start(bf16[4,48,1536]{2,1,0:T(8,128)(2,1)S(1)} %get-tuple-element.289), channel_id=1, source_target_pairs={{0,4},{1,5},{2,6},{3,7},{4,0},{5,1},{6,2},{7,3},{8,12},{9,13},{10,... | collective-permute-start | bytes 1769480 | tf_op jit(solution)/shard_map/ppermute | solution.py:83
  175.2 16.7 %collective-permute-start.35 = (bf16[4,48,1536]{2,1,0:T(8,128)(2,1)S(1)}, bf16[4,48,1536]{2,1,0:T(8,128)(2,1)}, u32[]{:S(2)}, u32[]{:S(2)}) collective-permute-start(bf16[4,48,1536]{2,1,0:T(8,128)(2,1)S(1)} %get-tuple-element.290), channel_id=1, source_target_pairs={{0,2},{1,3},{2,0},{3,1},{4,6},{5,7},{6,4},{7,5},{8,10},{9,11},{10,... | collective-permute-start | bytes 1769480 | tf_op jit(solution)/shard_map/ppermute | solution.py:83
  180.6 24.9 %collective-permute-start.32 = (bf16[8,48,896]{2,1,0:T(8,128)(2,1)S(1)}, bf16[8,48,896]{2,1,0:T(8,128)(2,1)}, u32[]{:S(2)}, u32[]{:S(2)}) collective-permute-start(bf16[8,48,896]{2,1,0:T(8,128)(2,1)S(1)} %get-tuple-element.301), channel_id=1, source_target_pairs={{0,4},{1,5},{2,6},{3,7},{4,0},{5,1},{6,2},{7,3},{8,12},{9,13},{10,... | collective-permute-start | bytes 2064392 | tf_op jit(solution)/shard_map/ppermute | solution.py:83
  183.3 25.5 %collective-permute-start.37 = (bf16[512,768]{1,0:T(8,128)(2,1)S(1)}, bf16[512,768]{1,0:T(8,128)(2,1)S(1)}, u32[]{:S(2)}, u32[]{:S(2)}) collective-permute-start(bf16[512,768]{1,0:T(8,128)(2,1)S(1)} %finish.1.refs_2_), channel_id=1, source_target_pairs={{0,2},{1,3},{2,0},{3,1},{4,6},{5,7},{6,4},{7,5},{8,10},{9,11},{10,... | collective-permute-start | bytes 2359304 | tf_op jit(solution)/shard_map/ppermute | solution.py:83
  185.1 22.1 %collective-permute-start.33 = (bf16[8,48,896]{2,1,0:T(8,128)(2,1)S(1)}, bf16[8,48,896]{2,1,0:T(8,128)(2,1)}, u32[]{:S(2)}, u32[]{:S(2)}) collective-permute-start(bf16[8,48,896]{2,1,0:T(8,128)(2,1)S(1)} %get-tuple-element.303), channel_id=1, source_target_pairs={{0,8},{1,9},{2,10},{3,11},{4,12},{5,13},{6,14},{7,15},{8,0},{9,1},... | collective-permute-start | bytes 2064392 | tf_op jit(solution)/shard_map/ppermute | solution.py:83
  195.6 24.0 %collective-permute-start.42 = (bf16[1,96,1536]{2,1,0:T(8,128)(2,1)}, bf16[1,96,1536]{2,1,0:T(8,128)(2,1)S(1)}, u32[]{:S(2)}, u32[]{:S(2)}) collective-permute-start(bf16[1,96,1536]{2,1,0:T(8,128)(2,1)} %get-tuple-element.314), channel_id=1, source_target_pairs={{0,16},{1,17},{2,18},{3,19},{4,20},{5,21},{6,22},{7,23},{8,24},{9,... | collective-permute-start | bytes 884744 | tf_op jit(solution)/shard_map/ppermute | solution.py:83
  197.3 30.8 %collective-permute-start.36 = (bf16[512,768]{1,0:T(8,128)(2,1)}, bf16[512,768]{1,0:T(8,128)(2,1)}, u32[]{:S(2)}, u32[]{:S(2)}) collective-permute-start(bf16[512,768]{1,0:T(8,128)(2,1)} %collective-permute-done.27.refs_1_), channel_id=1, source_target_pairs={{0,1},{1,0},{2,3},{3,2},{4,5},{5,4},{6,7},{7,6},{8,9},{9,8},{10,11... | collective-permute-start | bytes 2359304 | tf_op jit(solution)/shard_map/ppermute | solution.py:83
  207.1 19.4 %collective-permute-start.43 = (bf16[1,96,1536]{2,1,0:T(8,128)(2,1)}, bf16[1,96,1536]{2,1,0:T(8,128)(2,1)}, u32[]{:S(2)}, u32[]{:S(2)}) collective-permute-start(bf16[1,96,1536]{2,1,0:T(8,128)(2,1)} %get-tuple-element.315), channel_id=1, source_target_pairs={{0,8},{1,9},{2,10},{3,11},{4,12},{5,13},{6,14},{7,15},{8,0},{9,1},... | collective-permute-start | bytes 884744 | tf_op jit(solution)/shard_map/ppermute | solution.py:83
  208.8 18.0 %collective-permute-start.44 = (bf16[1,96,1536]{2,1,0:T(8,128)(2,1)}, bf16[1,96,1536]{2,1,0:T(8,128)(2,1)}, u32[]{:S(2)}, u32[]{:S(2)}) collective-permute-start(bf16[1,96,1536]{2,1,0:T(8,128)(2,1)} %get-tuple-element.316), channel_id=1, source_target_pairs={{0,24},{1,25},{2,26},{3,27},{4,28},{5,29},{6,30},{7,31},{8,16},{9,... | collective-permute-start | bytes 884744 | tf_op jit(solution)/shard_map/ppermute | solution.py:83
  219.6 28.3 %collective-permute-start.38 = (bf16[512,768]{1,0:T(8,128)(2,1)S(1)}, bf16[512,768]{1,0:T(8,128)(2,1)S(1)}, u32[]{:S(2)}, u32[]{:S(2)}) collective-permute-start(bf16[512,768]{1,0:T(8,128)(2,1)S(1)} %collective-permute-done.37.refs_0_), channel_id=1, source_target_pairs={{0,1},{1,0},{2,3},{3,2},{4,5},{5,4},{6,7},{7,6},{8,9},{9,8},{10,11... | collective-permute-start | bytes 2359304 | tf_op jit(solution)/shard_map/ppermute | solution.py:83
  219.6 28.3 %collective-permute-start.45 = (bf16[512,768]{1,0:T(8,128)(2,1)S(1)}, bf16[512,768]{1,0:T(8,128)(2,1)S(1)}, u32[]{:S(2)}, u32[]{:S(2)}) collective-permute-start(bf16[512,768]{1,0:T(8,128)(2,1)S(1)} %finish.1.refs_2_), channel_id=1, source_target_pairs={{0,1},{1,0},{2,3},{3,2},{4,5},{5,4},{6,7},{7,6},{8,9},{9,8},{10,11... | collective-permute-start | bytes 2359304 | tf_op jit(solution)/shard_map/ppermute | solution.py:83
  228.1 16.0 %collective-permute-start.39 = (f32[48,768]{1,0:T(8,128)}, f32[48,768]{1,0:T(8,128)S(1)}, u32[]{:S(2)}, u32[]{:S(2)}) collective-permute-start(f32[48,768]{1,0:T(8,128)} %add.114), channel_id=1, source_target_pairs={{0,4},{1,5},{2,6},{3,7},{4,0},{5,1},{6,2},{7,3},{8,12},{9,13},{10,... | collective-permute-start | bytes 442376 | tf_op jit(solution)/shard_map/ppermute | solution.py:83
  (82 other events, 625.1 us)

commit v3 on v2

--- a/solution.py
+++ b/solution.py
@@ -34,9 +34,8 @@
 BLOCKS = 8
 BLOCK_ROWS = D // BLOCKS
 PART_ROWS = BLOCK_ROWS // 2
-MARKS_AT, MARKED_WIDTH = 768, 896
 ACROSS = ((Z_HIGH, Z_LOW, X_BIT, SIDE), (Z_HIGH, Z_LOW, SIDE, X_BIT))
-ALONG = ((Z_HIGH, Z_LOW, SIDE, X_BIT), (Z_HIGH, SIDE, X_BIT, Z_LOW))
+ALONG = ((Z_HIGH, Z_LOW, SIDE, X_BIT), (SIDE, Z_HIGH, X_BIT, Z_LOW))
 Z_LINE = (Z_HIGH, Z_LOW, Z_HIGH | Z_LOW)
 ROUTES = (ACROSS, ALONG)
 
@@ -100,8 +99,8 @@
     def spread(self, share):
         return (Spread if self.cube else WholeSpread)(self, share)
 
-    def fold(self, halves, route):
-        return (Fold if self.cube else WholeFold)(self, halves, route)
+    def fold(self, halves, route, base):
+        return (Fold if self.cube else WholeFold)(self, halves, route, base)
 
 
 class Spread:
@@ -158,28 +157,29 @@
 
 
 class Fold:
-    def __init__(self, links, halves, route):
+    def __init__(self, links, halves, route, base):
         self.links = links
         self.route = route
+        self.base = base
         self.parts = [[halves[0]], [halves[2]]]
         self.far = [halves[1], halves[3]]
         self.joined = []
         self.round = 0
 
-    def step(self, *others, vmem=60):
+    def step(self, *others, vmem=16):
         links, k = self.links, 3 - self.round
         if others:
             (self.parts, self.joined, self.far), *_ = lax.optimization_barrier(
                 ((self.parts, self.joined, self.far), *others)
             )
         if self.route is ACROSS and self.round == 2:
-            sent = fold_add(self.parts, [], (1, 2, 3), False, vmem)
+            sent = fold_add(self.parts, 2, False, self.base, vmem)
             self.joined = [links.swap(a, bits) for a, bits in zip(sent, Z_LINE, strict=True)]
         else:
             if self.round == 0:
                 sent = self.far
             else:
-                sent = fold_add(self.parts, [], range(2**k, 2 ** (k + 1)), True, vmem)
+                sent = fold_add(self.parts, 2**k, True, self.base, vmem)
             for i, order in enumerate(self.route):
                 self.parts[i].append(links.swap(sent[i], order[k]))
         self.round += 1
@@ -190,120 +190,88 @@
 
 
 class WholeFold:
-    def __init__(self, links, halves, route):
+    def __init__(self, links, halves, route, base):
         near, far = (
             jnp.concatenate([halves[i], halves[i + 2]], axis=1).reshape(D, -1) for i in range(2)
         )
         total = near.astype(WIDE) + links.swap(far, SIDE).astype(WIDE)
-        self.share = lax.psum_scatter(total, "dp", scatter_dimension=0, tiled=True)
-        if self.share.shape[1] == MARKED_WIDTH:
-            marks = lax.psum(total[0:8, MARKS_AT:], "dp")
-            self.share = self.share.at[0:8, MARKS_AT:].set(marks)
-
-    def step(self, *others, vmem=60):
+        share = lax.psum_scatter(total[:, :base], "dp", scatter_dimension=0, tiled=True)
+        self.parts = [share, lax.psum(total[:BLOCK_ROWS, base:], "dp")]
+
+    def step(self, *others, vmem=16):
         return ()
 
     def pieces(self):
-        return ([], [], [self.share])
-
-
-def sum_pieces(refs, counts):
-    def add(group):
-        return sum(ref[0].astype(WIDE) for ref in group)
-
+        return ([], [], self.parts)
+
+
+def add_marked(refs, at, base):
+    total = sum(ref[at, :, 0:base].astype(WIDE) for ref in refs)
+    marks = refs[0][at, :, base:].astype(WIDE)
+    for ref in refs[1:]:
+        marks = marks.astype(LOW).astype(WIDE) + ref[at, :, base:].astype(WIDE)
+    return total, marks
+
+
+def sum_pieces(refs, counts, base, at=0):
     first, second, joined = counts
-    if first:
-        total = jnp.concatenate(
-            [add_marked(refs[:first]), add_marked(refs[first : first + second])], axis=0
-        )
-        if joined:
-            total = total + add(refs[first + second :])
-        return total
-    return refs[0][...]
-
-
-def add_marked(refs):
-    total = sum(ref[0].astype(WIDE) for ref in refs)
-    if total.shape[1] != MARKED_WIDTH:
-        return total
-    marks = refs[0][0][:, MARKS_AT:].astype(WIDE)
-    for ref in refs[1:]:
-        marks = marks.astype(LOW).astype(WIDE) + ref[0][:, MARKS_AT:].astype(WIDE)
-    return jnp.concatenate([total[:, :MARKS_AT], marks], axis=1)
-
-
-def fold_add_kernel(counts, apart, *refs):
-    first = counts[0]
-    total = sum(counts)
-    ins, outs = refs[:total], refs[total:]
+    if not first:
+        return refs[0][...], refs[1][...]
+    tops = add_marked(refs[:first], at, base)
+    ends = add_marked(refs[first : first + second], at, base)
+    total, marks = (jnp.concatenate(pair, axis=0) for pair in zip(tops, ends, strict=True))
+    joints = refs[first + second :]
+    for ref in joints:
+        total = total + ref[at, :, 0:base].astype(WIDE)
+    if joints:
+        high, low, both = (ref[at, :, base:].astype(WIDE) for ref in joints)
+        marks = (marks.astype(LOW).astype(WIDE) + high) + (low + both)
+    return total, marks
+
+
+def fold_add_kernel(count, half, apart, base, *refs):
+    ins, outs = refs[: 2 * count], refs[2 * count :]
     if apart:
-        outs[0][0] = add_marked(ins[:first]).astype(LOW)
-        outs[1][0] = add_marked(ins[first:]).astype(LOW)
+        for i in range(half):
+            for j in range(2):
+                total, marks = add_marked(ins[j * count : (j + 1) * count], i, base)
+                outs[j][i, :, 0:base] = total.astype(LOW)
+                outs[j][i, :, base:] = marks.astype(LOW)
     else:
-        block = sum_pieces(ins, counts).astype(LOW)
         for i, out in enumerate(outs):
-
-            @pl.when(pl.program_id(0) == i)
-            def _(out=out):
-                out[0] = block
-
-
-def fold_add(parts, joined, blocks, apart, vmem):
-    counts = (len(parts[0]), len(parts[1]), len(joined))
-    args = [*parts[0], *parts[1], *joined]
+            total, marks = sum_pieces(ins, (count, count, 0), base, i + 1)
+            out[0, :, 0:base] = total.astype(LOW)
+            out[0, :, base:] = marks.astype(LOW)
+
+
+def fold_add(parts, half, apart, base, vmem):
+    args = [*parts[0], *parts[1]]
     width = args[0].shape[2]
-    low, count = blocks[0], len(blocks)
     if apart:
-        outs = [shape((count, PART_ROWS, width), LOW)] * 2
-        out_specs = [pl.BlockSpec((1, PART_ROWS, width), lambda i: (i, 0, 0))] * 2
+        outs = [shape((half, PART_ROWS, width), LOW)] * 2
+        specs = [pl.BlockSpec((half, PART_ROWS, width), lambda i: (1, 0, 0))] * len(args)
     else:
-        outs = [shape((1, BLOCK_ROWS, width), LOW)] * count
-        out_specs = [pl.BlockSpec((1, BLOCK_ROWS, width), lambda i: (0, 0, 0))] * count
+        outs = [shape((1, BLOCK_ROWS, width), LOW)] * 3
+        specs = [pl.BlockSpec((4, PART_ROWS, width), lambda i: (0, 0, 0))] * len(args)
     return pl.pallas_call(
-        functools.partial(fold_add_kernel, counts, apart),
-        grid=(count,),
-        in_specs=[pl.BlockSpec((1, a.shape[1], width), lambda i: (low + i, 0, 0)) for a in args],
-        out_specs=out_specs,
+        functools.partial(fold_add_kernel, len(parts[0]), half, apart, base),
+        grid=(1,),
+        in_specs=specs,
+        out_specs=[pl.BlockSpec(o.shape, lambda i: (0, 0, 0)) for o in outs],
         out_shape=outs,
         compiler_params=pltpu.CompilerParams(vmem_limit_bytes=vmem * MIB),
         cost_estimate=pl.CostEstimate(
-            flops=count * BLOCK_ROWS * width, bytes_accessed=count * width, transcendentals=0
+            flops=half * BLOCK_ROWS * width, bytes_accessed=half * width, transcendentals=0
         ),
         name="fold_add",
     )(*args)
 
 
-class Total:
-    def __init__(self, links, value):
-        self.links = links
-        self.value = value
-        self.bits = [Z_LOW, Z_HIGH, X_BIT, SIDE]
-        self.last = None
-
-    def step(self, *others):
-        links = self.links
-        if others:
-            (self.value, self.last), *_ = lax.optimization_barrier(
-                ((self.value, self.last), *others)
-            )
-        self.value = self.result()
-        if not links.cube and len(self.bits) == 4:
-            self.bits = [SIDE]
-            self.value = lax.psum(self.value, "dp")
-        if not self.bits:
-            return ()
-        self.last = links.swap(self.value, self.bits.pop(0))
-        return (self.value,)
-
-    def result(self):
-        return self.value if self.last is None else self.value + self.last
-
-
 def after(value, *others):
     return lax.optimization_barrier((value, *others))[0]
 
 
-def call(kernel, name, grid, in_specs, out_specs, out_shape, scratch, places, args, flops, vmem=24, aliases=None):
+def call(kernel, name, grid, in_specs, out_specs, out_shape, scratch, places, args, flops, vmem=6, aliases=None):
     moved = sum(a.size * a.dtype.itemsize for a in args)
     moved += sum(int(np.prod(s.shape)) * np.dtype(s.dtype).itemsize for s in out_shape)
     return pl.pallas_call(
@@ -355,6 +323,7 @@
 
 CORE_AT = 1 + 4 * BLOCKS * len(ROUTES)
 SLOT_AT = CORE_AT + 1
+DP_AT = CORE_AT + 2
 
 
 def side_of(held, side, at, width):
@@ -528,7 +497,7 @@
         places,
         (q, k, v),
         4 * 6 * LEN * LEN * 256,
-        vmem=50,
+        vmem=12,
     )
 
 
@@ -789,7 +758,7 @@
     )
 
 
-def feed_grad_kernel(places, dh2, m, middle, du, h0, h1, h2, h3, held, turned):
+def feed_grad_kernel(places, dh2, m, middle, du, ramp, h0, h1, h2, h3, held, turned):
     for at, left, right in ((0, dh2, m), (D, middle, du)):
         turned[...] = left[...].T
         for side in range(2):
@@ -798,35 +767,43 @@
                 held[side * BLOCKS : (side + 1) * BLOCKS, :, at + c : at + c + 256] = part.reshape(
                     BLOCKS, BLOCK_ROWS, 256
                 )
-    scatter_blocks(places, held, (h0, h1, h2, h3))
-
-
-def feed_grad(places, dh2, m, middle, du):
-    args = (dh2, m, middle, du)
+    row = lax.broadcasted_iota(jnp.int32, (BLOCK_ROWS, 256), 0)
+    for group in range((held.shape[2] - 2 * D) // 256):
+        slot = places[SLOT_AT] - 16 * group
+        block = jnp.zeros((BLOCK_ROWS, 256), WIDE)
+        for i in range(6):
+            values = ramp[i // 3 : i // 3 + 1, 256 * (i % 3) : 256 * (i % 3 + 1)]
+            mine = (row == 6 * slot + i) & (slot >= 0) & (slot < 16)
+            block = jnp.where(mine, values, block)
+        block = block.astype(LOW)
+        at = 2 * D + 256 * group
+        for p in range(2 * BLOCKS):
+            held[p, :, at : at + 256] = block
+    scatter_blocks(places, held, (h0, h1, h2, h3), ALONG)
+
+
+def feed_grad(places, slots, dh2, m, middle, du, ramp):
+    args = (dh2, m, middle, du, ramp)
+    width = 2 * D + 16 * slots
     return call(
         feed_grad_kernel,
         "feed_grad",
         (1,),
         [whole(a) for a in args],
-        half_specs(2 * D),
-        half_shapes(2 * D),
-        [held_blocks(2 * D), pltpu.VMEM((D, LEN), LOW)],
+        half_specs(width),
+        half_shapes(width),
+        [held_blocks(width), pltpu.VMEM((D, LEN), LOW)],
         places,
         args,
         4 * LEN * D * 2 * D,
-        vmem=40,
-    )
-
-
-def mid_kernel(
-    places, dh2, dx, dxp, n1, rs1, vec, w_out, turn_sums, up_sums, ramp, dh1, low, do, sums
-):
+        vmem=12 if slots == 16 else 56,
+    )
+
+
+def mid_kernel(places, dh2, dx, dxp, n1, rs1, vec, w_out, turn_sums, up_sums, dh1, low, do, sums):
     @pl.when(pl.program_id(0) == 0)
     def _():
-        row = lax.broadcasted_iota(jnp.int32, sums.shape, 0)
-        at = 16 + 2 * places[SLOT_AT]
-        slots = jnp.where(row == at, ramp[0:1, :], jnp.where(row == at + 1, ramp[1:2, :], 0.0))
-        sums[...] = slots
+        sums[...] = jnp.zeros_like(sums)
         sums[0:8, :] = turn_sums[...]
         sums[11:12, :] = up_sums[0:1, 0:D]
         sums[12:13, :] = up_sums[0:1, D : 2 * D]
@@ -844,10 +821,10 @@
     do[...] = dot(back_low, w_out[...]).astype(LOW)
 
 
-def mid(places, dh2, dx, dxp, n1, rs1, vec, w_out, turn_sums, up_sums, ramp, slots):
+def mid(places, dh2, dx, dxp, n1, rs1, vec, w_out, turn_sums, up_sums):
     step = 256
-    args = (dh2, dx, dxp, n1, rs1, vec, w_out, turn_sums, up_sums, ramp)
-    count = 16 + 2 * slots
+    args = (dh2, dx, dxp, n1, rs1, vec, w_out, turn_sums, up_sums)
+    count = 16
     return call(
         mid_kernel,
         "middle_back",
@@ -915,47 +892,51 @@
         places,
         (q, k, v, do, inv, p),
         8 * 6 * LEN * LEN * 256,
-        vmem=36,
-    )
-
-
-def narrow_grad_kernel(share, places, left, dh1, o, *refs):
-    grads, halves, (held, turned) = refs[:3], refs[3:7], refs[7:]
+        vmem=18,
+    )
+
+
+MARK_ROWS = 6
+
+
+def narrow_grad_kernel(places, left, dh1, o, dq, dk, dv, sums, h0, h1, h2, h3, held, turned, marks):
     turned[...] = left[...].T
-    marks = []
-    for i in range(3):
-        right = grads[i][...]
-        from_pairs(dot(turned[...], right).astype(LOW), held, 128 * i, 512 + 64 * i)
+    marks[...] = jnp.zeros_like(marks)
+    for i, right in enumerate((dq, dk, dv)):
+        value = right[...]
+        from_pairs(dot(turned[...], value).astype(LOW), held, 128 * i, 512 + 64 * i)
         if i != 1:
-            marks.append(jnp.sum(right.astype(WIDE), axis=0, keepdims=True))
+            total = jnp.sum(value.astype(WIDE), axis=0, keepdims=True)
+            for k in range(3):
+                at = 13 * MARK_ROWS + 3 * (i // 2) + k
+                marks[at : at + 1, :] = total[:, 128 * k : 128 * (k + 1)]
     turned[...] = dh1[...].T
     from_pairs(dot(turned[...], o[...]).astype(LOW), held, 384, 704)
-    row = lax.rem(lax.broadcasted_iota(jnp.int32, (BLOCK_ROWS, 128), 0), share)
-    for side in range(2):
-        block = jnp.zeros((BLOCK_ROWS, 128), WIDE)
-        for i, mark in enumerate(marks):
-            narrow = mark[:, 256 + 64 * side : 320 + 64 * side]
-            pieces = (mark[:, 128 * side : 128 * (side + 1)], jnp.concatenate([narrow, narrow], axis=1))
-            for j, piece in enumerate(pieces):
-                block = jnp.where(row == 2 * i + j, piece, block)
-        for p in range(BLOCKS):
-            held[side * BLOCKS + p, :, MARKS_AT:MARKED_WIDTH] = block.astype(LOW)
-    scatter_blocks(places, held, halves, ALONG)
-
-
-def narrow_grad(places, share, tokens, dh1, o, grads):
-    args = (tokens, dh1, o, *grads)
-    return call(
-        functools.partial(narrow_grad_kernel, share),
+    for i in range(13):
+        for k in range(MARK_ROWS):
+            at = i * MARK_ROWS + k
+            marks[at : at + 1, :] = sums[i : i + 1, 128 * k : 128 * (k + 1)]
+    block = marks[...].astype(LOW)
+    for p in range(2 * BLOCKS):
+        held[p, :, D : D + 128] = block
+    scatter_blocks(places, held, (h0, h1, h2, h3), ALONG)
+
+
+def narrow_grad(places, tokens, dh1, o, grads, sums):
+    args = (tokens, dh1, o, *grads, sums)
+    width = D + 128
+    return call(
+        narrow_grad_kernel,
         "narrow_grad",
         (1,),
         [own_rows(LEN)] + [whole(a) for a in args[1:]],
-        half_specs(MARKED_WIDTH),
-        half_shapes(MARKED_WIDTH),
-        [held_blocks(MARKED_WIDTH), pltpu.VMEM((D, LEN), LOW)],
+        half_specs(width),
+        half_shapes(width),
+        [held_blocks(width), pltpu.VMEM((D, LEN), LOW), pltpu.VMEM((BLOCK_ROWS, 128), WIDE)],
         places,
         args,
         2 * LEN * D * 1536,
+        vmem=9,
     )
 
 
@@ -1048,33 +1029,30 @@
     )[0]
 
 
-def update(places, name, pieces, width, masters, kernel, extra):
+def update(places, name, pieces, width, ins, kernel, outs, scratch):
     counts = tuple(len(group) for group in pieces)
     args = [a for group in pieces for a in group]
     specs = [
-        pl.BlockSpec((1, a.shape[1], width), lambda *_: (0, 0, 0))
-        if a.ndim == 3
-        else pl.BlockSpec(a.shape, lambda *_: (0, 0))
+        pl.BlockSpec((1, a.shape[1], width), lambda *_: (0, 0, 0)) if a.ndim == 3 else whole(a)
         for a in args
     ]
-    flat = [a for triple in masters for a in triple]
-    outs = []
-    for weight, first, second in masters:
-        outs += [shape(weight.shape, WIDE)] * 3 + [shape(weight.shape, LOW)]
-    outs += extra
     return call(
         functools.partial(kernel, counts),
         name,
         (1,),
-        specs + [whole(a) for a in flat],
+        specs + [whole(a) for a in ins],
         [whole(o) for o in outs],
         outs,
-        [],
-        places,
-        (*args, *flat),
+        scratch,
+        places,
+        (*args, *ins),
         1,
         vmem=60,
     )
+
+
+def matrix_outs(weight):
+    return [shape(weight.shape, WIDE)] * 3 + [shape(weight.shape, LOW)]
 
 
 def step_matrix(ins, outs, at, grad, rate):
@@ -1085,18 +1063,38 @@
     outs[3][at] = new.astype(LOW)
 
 
+def step_vector(ins, outs, at, grad, rate=VECTOR_RATE, decay=0.0):
+    results = adamw(ins[0][at], ins[1][at], ins[2][at], grad, rate, decay)
+    for out, result in zip(outs, results, strict=True):
+        out[at] = result
+
+
 def update_feed_kernel(counts, places, *refs):
     total = sum(counts)
-    grad = sum_pieces(refs[:total], counts)
-    ins, outs = refs[total : total + 6], refs[total + 6 :]
+    grad, marks = sum_pieces(refs[:total], counts, 2 * D)
+    ins, outs = refs[total : total + 9], refs[total + 9 : total + 21]
+    heads, slopes = refs[total + 21 :]
     step_matrix(ins[0:3], outs[0:4], ..., grad[:, 0:D], RATE * FF ** (-0.5))
     step_matrix(ins[3:6], outs[4:8], ..., grad[:, D : 2 * D], RATE * D ** (-0.5))
+    for s in range(heads.shape[0]):
+        at = 256 * (s // 16)
+        for i, target in enumerate((heads, slopes)):
+            for k in range(3):
+                row = 6 * (s % 16) + 3 * i + k
+                target[s : s + 1, 256 * k : 256 * (k + 1)] = marks[row : row + 1, at : at + 256]
+    share = ins[6].shape[0]
+    column = lax.broadcasted_iota(jnp.int32, (D, share), 0)
+    own = column == lax.broadcasted_iota(jnp.int32, (D, share), 1) + places[DP_AT] * share
+    picked = dot(heads[...].astype(LOW), jnp.where(own, 1.0, 0.0).astype(LOW)).astype(LOW)
+    pool = dot_tn(picked, slopes[...].astype(LOW))
+    step_matrix(ins[6:9], outs[8:12], ..., pool, RATE * D ** (-0.5))
 
 
 def update_narrow_kernel(counts, places, *refs):
     total = sum(counts)
-    grad = sum_pieces(refs[:total], counts)
-    ins, outs = refs[total : total + 6], refs[total + 6 :]
+    grad, marks = sum_pieces(refs[:total], counts, D)
+    ins, outs = refs[total : total + 19], refs[total + 19 : total + 40]
+    rows_of = refs[total + 40]
 
     def columns(i):
         return jnp.concatenate(
@@ -1106,7 +1104,28 @@
     for i in range(3):
         step_matrix(ins[0:3], outs[0:4], i, columns(i), RATE * D ** (-0.5))
     step_matrix(ins[3:6], outs[4:8], ..., columns(3).T, RATE * max(1, 2 * D // LEN) ** (-0.5))
-    outs[8][...] = grad[0:8, MARKS_AT:MARKED_WIDTH]
+    for i in range(14):
+        for k in range(MARK_ROWS):
+            at = i * MARK_ROWS + k
+            rows_of[i : i + 1, 128 * k : 128 * (k + 1)] = marks[at : at + 1, :]
+    side = places[0]
+    pairs = rows_of[13:14, :]
+    for i in range(2):
+        pair = pairs[:, 384 * i : 384 * (i + 1)]
+        wide = jnp.where(side == 0, pair[:, 0:128], pair[:, 128:256])
+        narrow = jnp.where(side == 0, pair[:, 256:320], pair[:, 320:384])
+        own = jnp.concatenate([wide, narrow], axis=1)
+        step_vector(ins[6:9], outs[8:11], pl.ds(i, 1), own)
+    hidden = jnp.where(side == 0, rows_of[11:12, :], rows_of[12:13, :])
+    step_vector(ins[9:12], outs[11:14], ..., hidden.reshape(D))
+    for i, at in enumerate((8, 9, 0, 1, 10, 2, 3)):
+        step_vector(ins[12:15], outs[14:17], pl.ds(i, 1), rows_of[at : at + 1, :])
+    for i in range(3):
+        one = jnp.concatenate([rows_of[4 + i : 5 + i, :], rows_of[7:8, i : i + 1]], axis=1)
+        step_vector(
+            ins[15:18], outs[17:20], pl.ds(i, 1), one, RATE * (D // 4) ** (-0.5), DECAY
+        )
+    outs[20][...] = rows_of[7:8, 3:4] / ins[18][0:1, 0:1]
 
 
 def per_device(
@@ -1148,7 +1167,9 @@
     side, core = links.side, links.core
 
     slot = 2 * links.dp + side
-    places = jnp.concatenate([side[None], links.places(), core[None], slot[None]]).astype(jnp.int32)
+    places = jnp.concatenate(
+        [side[None], links.places(), core[None], slot[None], links.dp[None]]
+    ).astype(jnp.int32)
     share = D // dp_count
 
     by_kind = [a.transpose(1, 0, 2) for a in (qkv_weight, qkv_first, qkv_second)]
@@ -1204,105 +1225,78 @@
     du, dx, up_sums = feed_back(places, dh2_low, slope, w_down, w_up)
     dxp = links.swap(dx, CORE)
     m, dh2_low = after((m, dh2_low), dx)
-    feed_halves = feed_grad(places, dh2_low, m, middle_low, du)
-    feed_fold = links.fold(feed_halves, ACROSS)
-    feed_fold.step(y_first)
+    slots = 2 * dp_count
+    feed_halves = feed_grad(places, slots, dh2_low, m, middle_low, du, ramp)
+    feed_fold = links.fold(feed_halves, ALONG, 2 * D)
+    feed_fold.step()
     dx = after(dx, *feed_halves)
-    slots = 2 * dp_count
     dh1, dh1_low, do, sums = mid(
-        places, dh2, dx, dxp, n1, rs1, layer_vectors, w_out, turn_sums, up_sums, ramp, slots
-    )
-    total = Total(links, sums)
-    total.step()
+        places, dh2, dx, dxp, n1, rs1, layer_vectors, w_out, turn_sums, up_sums
+    )
     grads = attend_back(places, q, k, v, do, inv, p)
-    sent = feed_fold.step(grads[0], vmem=12)
-    grads = after(grads, *sent)
     token_keep, token_send = input_grad(places, grads, w_qkv)
     token_other = links.swap(token_send, CORE)
-    grads = after(grads, token_keep)
-    narrow_halves = narrow_grad(places, share, tokens, dh1_low, o, grads)
-    narrow_fold = links.fold(narrow_halves, ALONG)
+    sent = feed_fold.step(token_keep, y_first)
+    grads = after(grads, *sent)
+    narrow_halves = narrow_grad(places, tokens, dh1_low, o, grads, sums)
+    narrow_fold = links.fold(narrow_halves, ALONG, D)
     narrow_fold.step()
     token_keep = after(token_keep, *narrow_halves)
     grad_half = finish(places, dh1, token_keep, token_other)
     first = links.swap(grad_half, SIDE)
     second_own = links.swap(grad_half, CORE)
-    sent = total.step(grad_half)
+    sent = feed_fold.step(grad_half)
+    sent = narrow_fold.step(*sent)
     sent = feed_fold.step(*sent)
-    y_second = links.swap(after(y_first, *sent), CORE)
     sent = narrow_fold.step(*sent)
-    first = after(first, *sent)
-    second = links.swap(first, CORE)
-    sent = total.step(*sent)
-    y = after(y, *sent)
-    result = place(places, y, [y_first, y_second])
-    feed_pieces = after(feed_fold.pieces(), result)
+    first, y_first = after((first, y_first), *sent)
+    second, y_second = links.swap(first, CORE), links.swap(y_first, CORE)
+    tokens_grad = place(places, None, [first, second, grad_half, second_own])
+    result = place(places, y, [y_first, after(y_second, tokens_grad)])
+    sent = narrow_fold.step(result)
+    by_class = [a.T for a in (class_weight, class_first, class_second)]
+    masters = [*by_kind, out_weight, out_first, out_second]
+    vectors = [qv_bias, qv_first, qv_second, up_bias, upb_first, upb_second]
+    vectors += [layer_vectors, vector_first, vector_second, *by_class]
+    narrow_new = update(
+        places,
+        "update_narrow",
+        narrow_fold.pieces(),
+        D + 128,
+        [*masters, *vectors, live_count],
+        update_narrow_kernel,
+        [o for a in masters[0::3] for o in matrix_outs(a)]
+        + [shape(a.shape, WIDE) for a in vectors]
+        + [shape((1, 1), WIDE)],
+        [pltpu.VMEM((16, D), WIDE)],
+    )
+    masters = [*down_turned, up_weight, up_first, up_second, pool_weight, pool_first, pool_second]
     feed_new = update(
         places,
         "update_feed",
-        feed_pieces,
-        2 * D,
-        [down_turned, (up_weight, up_first, up_second)],
+        after(feed_fold.pieces(), narrow_new[0]),
+        2 * D + 16 * slots,
+        masters,
         update_feed_kernel,
-        [],
-    )
-    sent = narrow_fold.step(feed_new[0])
-    sent = total.step(*sent)
-    tokens_grad = place(
-        places, None, [first, after(second, *sent), grad_half, second_own]
-    )
-    sent = narrow_fold.step(tokens_grad)
-    total.value, total.last = after((total.value, total.last), *sent)
-    sums = total.result()
+        [o for a in masters[0::3] for o in matrix_outs(a)],
+        [pltpu.VMEM((slots, D), WIDE)] * 2,
+    )
     down_new, down_first_new, down_second_new, down_copy = (a.T for a in feed_new[0:4])
     up_new, up_first_new, up_second_new, up_copy = feed_new[4:8]
-    *narrow_new, marks = update(
-        places,
-        "update_narrow",
-        narrow_fold.pieces(),
-        MARKED_WIDTH,
-        [by_kind, (out_weight, out_first, out_second)],
-        update_narrow_kernel,
-        [shape((8, 128), WIDE)],
-    )
+    pool_new, pool_first_new, pool_second_new, pool_copy = feed_new[8:12]
     qkv_new, qkv_first_new, qkv_second_new, qkv_copy = (
         a.transpose(1, 0, 2) for a in narrow_new[0:4]
     )
     out_new, out_first_new, out_second_new, out_copy = narrow_new[4:8]
-
-    ramps = sums[16:].reshape(slots, 2, D)
-
-    head_rows = lax.dynamic_slice_in_dim(ramps[:, 0], links.dp * share, share, 1)
-    grad_pool = lax.dot_general(
-        head_rows.astype(LOW),
-        ramps[:, 1].astype(LOW),
-        (((0,), (0,)), ((), ())),
-        preferred_element_type=WIDE,
-    )
-    vector_sum = jnp.concatenate([sums[8:10], sums[0:2], sums[10:11], sums[2:4]], axis=0)
-    class_sum = jnp.concatenate([sums[4:7].T, sums[7:8, 0:3]], axis=0)
-    upb_sum = lax.dynamic_slice_in_dim(sums, 11 + side, 1, 0)[0]
-    bias_sum = jnp.concatenate([marks[0:4:2], marks[1:4:2, 0:64]], axis=1)
-
-    pool_new, pool_first_new, pool_second_new = adamw(
-        pool_weight, pool_first, pool_second, grad_pool, RATE * D ** (-0.5), DECAY
-    )
-    qv_new, qv_first_new, qv_second_new = adamw(
-        qv_bias, qv_first, qv_second, bias_sum, VECTOR_RATE, 0.0
-    )
-    upb_new, upb_first_new, upb_second_new = adamw(
-        up_bias, upb_first, upb_second, upb_sum, VECTOR_RATE, 0.0
-    )
-    vector_new, vector_first_new, vector_second_new = adamw(
-        layer_vectors, vector_first, vector_second, vector_sum, VECTOR_RATE, 0.0
-    )
-    class_new, class_first_new, class_second_new = adamw(
-        class_weight, class_first, class_second, class_sum, RATE * (D // 4) ** (-0.5), DECAY
-    )
+    qv_new, qv_first_new, qv_second_new = narrow_new[8:11]
+    upb_new, upb_first_new, upb_second_new = narrow_new[11:14]
+    vector_new, vector_first_new, vector_second_new = narrow_new[14:17]
+    class_new, class_first_new, class_second_new = (a.T for a in narrow_new[17:20])
+    entropy = narrow_new[20].reshape(())
     return (
         result,
         tokens_grad,
-        sums[7, 3] / live_count[0, 0],
+        entropy,
         qkv_new,
         qkv_first_new,
         qkv_second_new,
@@ -1322,7 +1316,7 @@
         pool_new,
         pool_first_new,
         pool_second_new,
-        pool_new.astype(LOW),
+        pool_copy,
         qv_new,
         qv_first_new,
         qv_second_new,

time: 271 us -> 241 us (0.89)
  waiting for transfers between devices: 56.5 us -> 71.4 us
  Pallas kernels: 119 us -> 105 us
  local copies, waits for them, and re-layouts: 22 us -> 10.6 us
  starting transfers between devices: 59.6 us -> 50.5 us
  other arithmetic: 7.43 us -> 1 us
    ppermute x51 -> x48, waiting for transfers between devices: 56.5 us -> 71.4 us  [swap(): return lax.ppermute(value, ('dp', 'mp'), pairs)]
    pallas_call x5 -> x6, Pallas kernels: 11.5 us -> 1.94 us  [fold_add(): pl.pallas_call(functools.partial(fold_add_kernel, len(parts[0]), half, ap...]
    unnamed x117 -> x93, local copies, waits for them, and re-layouts: 17.7 us -> 8.49 us
    ppermute x51 -> x48, starting transfers between devices: 59.6 us -> 50.5 us  [swap(): return lax.ppermute(value, ('dp', 'mp'), pairs)]
    pallas_call x18, Pallas kernels: 106 us -> 101 us  [call(): pl.pallas_call(kernel, out_shape=out_shape, grid_spec=pltpu.PrefetchScala...]
    add x4 -> x0, other arithmetic: 3.32 us -> none  [result(): return self.value if self.last is None else self.value + self.last]
  transfers between devices with their start and end apart: 51 -> 48, of which waited for: 18 -> 25; matrix products, arithmetic and copies ran while one was open for 3% -> 1% of each run, Pallas kernels for 36% -> 33%
where the time goes in v3:
time: 241 us; the launch traced here: 240 us
  Pallas kernels  105 us (44%)
  waiting for transfers between devices  71.4 us (30%)
  starting transfers between devices  50.5 us (21%)
  local copies, waits for them, and re-layouts  10.6 us (4%)
    pallas_call x18, Pallas kernels, call(): pl.pallas_call(kernel, out_shape=out_shape, grid_spec=pltpu.PrefetchScala...  101 us
    ppermute x48, waiting for transfers between devices, swap(): return lax.ppermute(value, ('dp', 'mp'), pairs)  71.4 us
    ppermute x48, starting transfers between devices, swap(): return lax.ppermute(value, ('dp', 'mp'), pairs)  50.5 us
    unnamed x93, local copies, waits for them, and re-layouts  8.49 us
  transfers between devices with their start and end apart: 48, of which 25 were waited for; matrix products, arithmetic and copies ran while one was open for 1% of the time, Pallas kernels for 33%

profile of v3, /device:TPU:0, one launch (start us, length us, event | category | flops | bytes accessed | tf_op | source)
XLA Modules:
  0.0 240.3 jit_solution(7097583942108436370)
XLA Ops:
  2.4 5.0 %collective-permute-start.2 = (bf16[1,96,576]{2,1,0:T(8,128)(2,1)}, bf16[1,96,576]{2,1,0:T(8,128)(2,1)S(1)}, u32[]{:S(2)}, u32[]{:S(2)}) collective-permute-start(bf16[1,96,576]{2,1,0:T(8,128)(2,1)} %bitcast.32), channel_id=1, source_target_pairs={{0,24},{1,25},{2,26},{3,27},{4,28},{5,29},{6,30},{7,31},{8,16},{9,... | collective-permute-start | bytes 331784 | tf_op jit(solution)/shard_map/ppermute | solution.py:82
  31.8 4.2 %collective-permute-done.4 = bf16[1,96,960]{2,1,0:T(8,128)(2,1)S(1)} collective-permute-done((bf16[1,96,960]{2,1,0:T(8,128)(2,1)S(1)}, bf16[1,96,960]{2,1,0:T(8,128)(2,1)S(1)}, u32[]{:S(2)}, u32[]{:S(2)}) %collective-permute-start.4) | collective-permute-done | bytes 184352 | tf_op jit(solution)/shard_map/ppermute | solution.py:82
  36.1 3.7 %collective-permute-done.3 = bf16[1,96,960]{2,1,0:T(8,128)(2,1)S(1)} collective-permute-done((bf16[1,96,960]{2,1,0:T(8,128)(2,1)S(1)}, bf16[1,96,960]{2,1,0:T(8,128)(2,1)S(1)}, u32[]{:S(2)}, u32[]{:S(2)}) %collective-permute-start.3) | collective-permute-done | bytes 184352 | tf_op jit(solution)/shard_map/ppermute | solution.py:82
  45.5 4.4 %project.1 = (bf16[1024,384]{1,0:T(8,128)(2,1)S(1)}, bf16[1024,384]{1,0:T(8,128)(2,1)S(1)}, bf16[1024,384]{1,0:T(8,128)(2,1)S(1)}, bf16[3,768,384]{2,1,0:T(8,128)(2,1)S(1)}) custom-call(s32[68]{0:T(128)S(1)} %copy-done.31, bf16[2048,768]{1,0:T(8,128)(2,1)S(1)} %copy-done, f32[8,768]{1,0:T(8,128)S(1)} %copy-done.32, ...), custom_call_target="tpu_custom_call" | custom-call | flops 113246208 | bytes 568320 | tf_op jit(solution)/shard_map/project/pallas_call | solution.py:277
  54.5 11.8 %attend_forward.1 = (bf16[1024,384]{1,0:T(8,128)(2,1)S(1)}, f32[1024,384]{1,0:T(8,128)S(1)}, bf16[6,1024,1024]{2,1,0:T(8,128)(2,1)S(1)}) custom-call(s32[68]{0:T(128)S(1)} %copy-done.31, bf16[1024,384]{1,0:T(8,128)(2,1)S(1)} %get-tuple-element.241.q_ref, bf16[1024,384]{1,0:T(8,128)(2,1)S(1)} %get-tuple-element.242.k_ref, ...), custom_call_target="tpu_custom_call" | custom-call | flops 402653184 | bytes 1081344 | tf_op jit(solution)/shard_map/attend_forward/pallas_call | solution.py:277
  79.7 7.6 %feed_up.1 = (bf16[1024,1536]{1,0:T(8,128)(2,1)S(1)}, bf16[1024,1536]{1,0:T(8,128)(2,1)S(1)}, f32[1024,768]{1,0:T(8,128)S(1)}, f32[1024,128]{1,0:T(8,128)S(1)}, bf16[1024,768]{1,0:T(8,128)(2,1)S(1)}) custom-call(s32[68]{0:T(128)S(1)} %copy-done.31, bf16[2048,768]{1,0:T(8,128)(2,1)S(1)} %copy-done, bf16[1024,768]{1,0:T(8,128)(2,1)S(1)} %get-tuple-element.255.z, ...), custom_call_target="tpu_custom_call" | custom-call | flops 150994944 | bytes 1265984 | tf_op jit(solution)/shard_map/feed_up/pallas_call | solution.py:277
  88.1 6.5 %collective-permute-done.22.h3 = bf16[8,48,1024]{2,1,0:T(8,128)(2,1)S(1)} collective-permute-done((bf16[8,48,1024]{2,1,0:T(8,128)(2,1)S(1)}, bf16[8,48,1024]{2,1,0:T(8,128)(2,1)S(1)}, u32[]{:S(2)}, u32[]{:S(2)}) %collective-permute-start.22) | collective-permute-done | bytes 786464 | tf_op jit(solution)/shard_map/ppermute | solution.py:82
  95.8 4.4 %feed_down.1 = (bf16[1024,768]{1,0:T(8,128)(2,1)S(1)}, bf16[768,1536]{1,0:T(8,128)(2,1)S(1)}, bf16[768,384]{1,0:T(8,128)(2,1)S(1)}, f32[8,128]{1,0:T(8,128)S(1)}) custom-call(s32[68]{0:T(128)S(1)} %copy-done.31, bf16[1024,1536]{1,0:T(8,128)(2,1)S(1)} %get-tuple-element.269.m, bf16[8,48,1024]{2,1,0:T(8,128)(2,1)S(1)} %constant_dynamic-update-slice_fusion.8.h0, ...), custom_call_target="tpu_custom_call" | custom-call | flops 150994944 | bytes 676096 | tf_op jit(solution)/shard_map/feed_down/pallas_call | solution.py:277
  100.8 3.7 %collective-permute-done.24.pool_b = bf16[768,384]{1,0:T(8,128)(2,1)S(1)} collective-permute-done((bf16[768,384]{1,0:T(8,128)(2,1)S(1)}, bf16[768,384]{1,0:T(8,128)(2,1)S(1)}, u32[]{:S(2)}, u32[]{:S(2)}) %collective-permute-start.24) | collective-permute-done | bytes 589856 | tf_op jit(solution)/shard_map/ppermute | solution.py:82
  104.5 6.7 %turn.1 = (bf16[2048,768]{1,0:T(8,128)(2,1)}, bf16[512,768]{1,0:T(8,128)(2,1)}, f32[1024,768]{1,0:T(8,128)S(1)}, bf16[1024,768]{1,0:T(8,128)(2,1)S(1)}, f32[8,768]{1,0:T(8,128)S(1)}, /*index=5*/f32[8,768]{1,0:T(8,128)S(1)}) custom-call(s32[68]{0:T(128)S(1)} %copy-done.31, s32[2]{0:T(128)S(1)} %copy-done.34, s32[2]{0:T(128)S(1)} %copy-done.35, ...), custom_call_target="tpu_custom_call" | custom-call | flops 2949120 | bytes 1221217 | tf_op jit(solution)/shard_map/turn/pallas_call | solution.py:277
  111.2 7.4 %feed_back.1 = (bf16[1024,1536]{1,0:T(8,128)(2,1)S(1)}, bf16[1024,768]{1,0:T(8,128)(2,1)S(1)}, f32[8,1536]{1,0:T(8,128)S(1)}) custom-call(s32[68]{0:T(128)S(1)} %copy-done.31, bf16[1024,768]{1,0:T(8,128)(2,1)S(1)} %get-tuple-element.268.dh2, bf16[1024,1536]{1,0:T(8,128)(2,1)S(1)} %get-tuple-element.265.slope, ...), custom_call_target="tpu_custom_call" | custom-call | flops 301989888 | bytes 887808 | tf_op jit(solution)/shard_map/feed_back/pallas_call | solution.py:277
  122.3 7.6 %feed_grad.1 = (bf16[8,48,1792]{2,1,0:T(8,128)(2,1)S(1)}, bf16[8,48,1792]{2,1,0:T(8,128)(2,1)}, bf16[8,48,1792]{2,1,0:T(8,128)(2,1)S(1)}, bf16[8,48,1792]{2,1,0:T(8,128)(2,1)}) custom-call(s32[68]{0:T(128)S(1)} %copy-done.31, bf16[1024,768]{1,0:T(8,128)(2,1)S(1)} %get-tuple-element.268.dh2, bf16[1024,1536]{1,0:T(8,128)(2,1)S(1)} %get-tuple-element.269.m, ...), custom_call_target="tpu_custom_call" | custom-call | flops 301989888 | bytes 935424 | tf_op jit(solution)/shard_map/feed_grad/pallas_call | solution.py:277
  133.6 4.1 %middle_back.1 = (f32[1024,768]{1,0:T(8,128)S(1)}, bf16[1024,768]{1,0:T(8,128)(2,1)S(1)}, bf16[1024,384]{1,0:T(8,128)(2,1)S(1)}, f32[16,768]{1,0:T(8,128)S(1)}) custom-call(s32[68]{0:T(128)S(1)} %copy-done.31, f32[1024,768]{1,0:T(8,128)S(1)} %get-tuple-element.263.dh2, bf16[1024,768]{1,0:T(8,128)(2,1)S(1)} %get-tuple-element.277.dx, ...), custom_call_target="tpu_custom_call" | custom-call | flops 37748736 | bytes 1012544 | tf_op jit(solution)/shard_map/middle_back/pallas_call | solution.py:277
  137.7 19.4 %attend_backward.1 = (bf16[1024,384]{1,0:T(8,128)(2,1)S(1)}, bf16[1024,384]{1,0:T(8,128)(2,1)S(1)}, bf16[1024,384]{1,0:T(8,128)(2,1)S(1)}) custom-call(s32[68]{0:T(128)S(1)} %copy-done.31, bf16[1024,384]{1,0:T(8,128)(2,1)S(1)} %get-tuple-element.241.q_ref, bf16[1024,384]{1,0:T(8,128)(2,1)S(1)} %get-tuple-element.242.k_ref, ...), custom_call_target="tpu_custom_call" | custom-call | flops 805306368 | bytes 1228800 | tf_op jit(solution)/shard_map/attend_backward/pallas_call | solution.py:277
  157.1 4.1 %input_grad.1 = (bf16[512,768]{1,0:T(8,128)(2,1)S(1)}, bf16[512,768]{1,0:T(8,128)(2,1)S(1)}) custom-call(s32[68]{0:T(128)S(1)} %copy-done.31, bf16[1024,384]{1,0:T(8,128)(2,1)S(1)} %get-tuple-element.299.refs_0_.dq, bf16[1024,384]{1,0:T(8,128)(2,1)S(1)} %get-tuple-element.300.refs_1_.dk, bf16[1024,384]{1,0:T(8,128)(2,1)S(1)} %get-tuple-element.301.refs_2_.dv, ...), custom_call_target="tpu_custom_call" | custom-call | flops 113246208 | bytes 356352 | tf_op jit(solution)/shard_map/input_grad/pallas_call | solution.py:277
  166.5 4.4 %narrow_grad.1 = (bf16[8,48,896]{2,1,0:T(8,128)(2,1)S(1)}, bf16[8,48,896]{2,1,0:T(8,128)(2,1)S(1)}, bf16[8,48,896]{2,1,0:T(8,128)(2,1)S(1)}, bf16[8,48,896]{2,1,0:T(8,128)(2,1)S(1)}) custom-call(s32[68]{0:T(128)S(1)} %copy-done.31, bf16[2048,768]{1,0:T(8,128)(2,1)S(1)} %copy-done, bf16[1024,768]{1,0:T(8,128)(2,1)S(1)} %get-tuple-element.291.dh1, ...), custom_call_target="tpu_custom_call" | custom-call | flops 150994944 | bytes 666624 | tf_op jit(solution)/shard_map/narrow_grad/pallas_call | solution.py:277
  174.1 8.2 %collective-permute-done.33.refs_2_ = bf16[4,48,1792]{2,1,0:T(8,128)(2,1)S(1)} collective-permute-done((bf16[4,48,1792]{2,1,0:T(8,128)(2,1)S(1)}, bf16[4,48,1792]{2,1,0:T(8,128)(2,1)S(1)}, u32[]{:S(2)}, u32[]{:S(2)}) %collective-permute-start.33) | collective-permute-done | bytes 688160 | tf_op jit(solution)/shard_map/ppermute | solution.py:82
  187.7 9.0 %collective-permute-done.31.refs_1_ = bf16[8,48,896]{2,1,0:T(8,128)(2,1)S(1)} collective-permute-done((bf16[8,48,896]{2,1,0:T(8,128)(2,1)S(1)}, bf16[8,48,896]{2,1,0:T(8,128)(2,1)S(1)}, u32[]{:S(2)}, u32[]{:S(2)}) %collective-permute-start.31) | collective-permute-done | bytes 688160 | tf_op jit(solution)/shard_map/ppermute | solution.py:82
  199.4 3.3 %collective-permute-done.37.refs_3_ = bf16[2,48,1792]{2,1,0:T(8,128)(2,1)S(1)} collective-permute-done((bf16[2,48,1792]{2,1,0:T(8,128)(2,1)S(1)}, bf16[2,48,1792]{2,1,0:T(8,128)(2,1)S(1)}, u32[]{:S(2)}, u32[]{:S(2)}) %collective-permute-start.37) | collective-permute-done | bytes 344096 | tf_op jit(solution)/shard_map/ppermute | solution.py:82
  206.5 3.2 %collective-permute-start.43 = (bf16[2,48,896]{2,1,0:T(8,128)(2,1)S(1)}, bf16[2,48,896]{2,1,0:T(8,128)(2,1)S(1)}, u32[]{:S(2)}, u32[]{:S(2)}) collective-permute-start(bf16[2,48,896]{2,1,0:T(8,128)(2,1)S(1)} %get-tuple-element.340), channel_id=1, source_target_pairs={{0,16},{1,17},{2,18},{3,19},{4,20},{5,21},{6,22},{7,23},{8,24},{9,... | collective-permute-start | bytes 516104 | tf_op jit(solution)/shard_map/ppermute | solution.py:82
  216.2 6.1 %collective-permute-done.43.refs_7_.refs_8_ = bf16[2,48,896]{2,1,0:T(8,128)(2,1)S(1)} collective-permute-done((bf16[2,48,896]{2,1,0:T(8,128)(2,1)S(1)}, bf16[2,48,896]{2,1,0:T(8,128)(2,1)S(1)}, u32[]{:S(2)}, u32[]{:S(2)}) %collective-permute-start.43) | collective-permute-done | bytes 172064 | tf_op jit(solution)/shard_map/ppermute | solution.py:82
  224.8 4.6 %collective-permute-done.44.refs_4_ = bf16[1,48,896]{2,1,0:T(8,128)(2,1)S(1)} collective-permute-done((bf16[1,48,896]{2,1,0:T(8,128)(2,1)S(1)}, bf16[1,48,896]{2,1,0:T(8,128)(2,1)S(1)}, u32[]{:S(2)}, u32[]{:S(2)}) %collective-permute-start.44) | collective-permute-done | bytes 86048 | tf_op jit(solution)/shard_map/ppermute | solution.py:82
  230.0 3.7 %update_narrow.1 = (f32[3,96,192]{2,1,0:T(8,128)}, f32[3,96,192]{2,1,0:T(8,128)}, f32[3,96,192]{2,1,0:T(8,128)}, bf16[3,96,192]{2,1,0:T(8,128)(2,1)}, f32[192,96...) custom-call(s32[68]{0:T(128)} %concatenate.39.places, ...), custom_call_target="tpu_custom_call" | custom-call | bytes 380612 | tf_op jit(solution)/shard_map/update_narrow/pallas_call | solution.py:277
  234.5 5.6 %update_feed.1 = (f32[96,768]{1,0:T(8,128)}, f32[96,768]{1,0:T(8,128)}, f32[96,768]{1,0:T(8,128)}, bf16[96,768]{1,0:T(8,128)(2,1)}, f32[96,768]{1,0:T(8,128)}, /...) custom-call(s32[68]{0:T(128)} %concatenate.39.places, ...), custom_call_target="tpu_custom_call" | custom-call | bytes 854016 | tf_op jit(solution)/shard_map/update_feed/pallas_call | solution.py:277
  (219 shorter events, 89.9 us)
Async XLA Ops:
  2.4 13.9 %collective-permute-start.2 = (bf16[1,96,576]{2,1,0:T(8,128)(2,1)}, bf16[1,96,576]{2,1,0:T(8,128)(2,1)S(1)}, u32[]{:S(2)}, u32[]{:S(2)}) collective-permute-start(bf16[1,96,576]{2,1,0:T(8,128)(2,1)} %bitcast.32), channel_id=1, source_target_pairs={{0,24},{1,25},{2,26},{3,27},{4,28},{5,29},{6,30},{7,31},{8,16},{9,... | collective-permute-start | bytes 331784 | tf_op jit(solution)/shard_map/ppermute | solution.py:82
  24.7 15.1 %collective-permute-start.3 = (bf16[1,96,960]{2,1,0:T(8,128)(2,1)S(1)}, bf16[1,96,960]{2,1,0:T(8,128)(2,1)S(1)}, u32[]{:S(2)}, u32[]{:S(2)}) collective-permute-start(bf16[1,96,960]{2,1,0:T(8,128)(2,1)S(1)} %bitcast.46), channel_id=1, source_target_pairs={{0,16},{1,17},{2,18},{3,19},{4,20},{5,21},{6,22},{7,23},{8,24},{9,... | collective-permute-start | bytes 552968 | tf_op jit(solution)/shard_map/ppermute | solution.py:82
  27.5 16.2 %collective-permute-start.10 = (bf16[8,48,576]{2,1,0:T(8,128)(2,1)S(1)}, bf16[8,48,576]{2,1,0:T(8,128)(2,1)S(1)}, u32[]{:S(2)}, u32[]{:S(2)}) collective-permute-start(bf16[8,48,576]{2,1,0:T(8,128)(2,1)S(1)} %constant_dynamic-update-slice_fusion.2.h2), channel_id=1, source_target_pairs={{0,4},{1,5},{2,6},{3,7},{4,0},{5,1},{6,2},{7,3},{8,12},{9,13},{10,... | collective-permute-start | bytes 1327112 | tf_op jit(solution)/shard_map/ppermute | solution.py:82
  28.2 15.5 %collective-permute-start.9 = (bf16[8,48,576]{2,1,0:T(8,128)(2,1)S(1)}, bf16[8,48,576]{2,1,0:T(8,128)(2,1)S(1)}, u32[]{:S(2)}, u32[]{:S(2)}) collective-permute-start(bf16[8,48,576]{2,1,0:T(8,128)(2,1)S(1)} %constant_dynamic-update-slice_fusion.h0), channel_id=1, source_target_pairs={{0,2},{1,3},{2,0},{3,1},{4,6},{5,7},{6,4},{7,5},{8,10},{9,11},{10,... | collective-permute-start | bytes 1327112 | tf_op jit(solution)/shard_map/ppermute | solution.py:82
  41.1 25.3 %collective-permute-start.15 = (bf16[1,96,1024]{2,1,0:T(8,128)(2,1)S(1)}, bf16[1,96,1024]{2,1,0:T(8,128)(2,1)S(1)}, u32[]{:S(2)}, u32[]{:S(2)}) collective-permute-start(bf16[1,96,1024]{2,1,0:T(8,128)(2,1)S(1)} %bitcast.40), channel_id=1, source_target_pairs={{0,24},{1,25},{2,26},{3,27},{4,28},{5,29},{6,30},{7,31},{8,16},{9,... | collective-permute-start | bytes 589832 | tf_op jit(solution)/shard_map/ppermute | solution.py:82
  43.7 22.7 %collective-permute-start.14 = (bf16[1,96,1024]{2,1,0:T(8,128)(2,1)S(1)}, bf16[1,96,1024]{2,1,0:T(8,128)(2,1)S(1)}, u32[]{:S(2)}, u32[]{:S(2)}) collective-permute-start(bf16[1,96,1024]{2,1,0:T(8,128)(2,1)S(1)} %bitcast.41), channel_id=1, source_target_pairs={{0,8},{1,9},{2,10},{3,11},{4,12},{5,13},{6,14},{7,15},{8,0},{9,1},... | collective-permute-start | bytes 589832 | tf_op jit(solution)/shard_map/ppermute | solution.py:82
  43.7 22.7 %collective-permute-start.13 = (bf16[1,96,1024]{2,1,0:T(8,128)(2,1)S(1)}, bf16[1,96,1024]{2,1,0:T(8,128)(2,1)S(1)}, u32[]{:S(2)}, u32[]{:S(2)}) collective-permute-start(bf16[1,96,1024]{2,1,0:T(8,128)(2,1)S(1)} %bitcast.42), channel_id=1, source_target_pairs={{0,16},{1,17},{2,18},{3,19},{4,20},{5,21},{6,22},{7,23},{8,24},{9,... | collective-permute-start | bytes 589832 | tf_op jit(solution)/shard_map/ppermute | solution.py:82
  51.2 18.6 %collective-permute-start.17 = (bf16[8,48,960]{2,1,0:T(8,128)(2,1)S(1)}, bf16[8,48,960]{2,1,0:T(8,128)(2,1)S(1)}, u32[]{:S(2)}, u32[]{:S(2)}) collective-permute-start(bf16[8,48,960]{2,1,0:T(8,128)(2,1)S(1)} %constant_dynamic-update-slice_fusion.6.h2), channel_id=1, source_target_pairs={{0,4},{1,5},{2,6},{3,7},{4,0},{5,1},{6,2},{7,3},{8,12},{9,13},{10,... | collective-permute-start | bytes 2211848 | tf_op jit(solution)/shard_map/ppermute | solution.py:82
  52.8 18.7 %collective-permute-start.16 = (bf16[8,48,960]{2,1,0:T(8,128)(2,1)S(1)}, bf16[8,48,960]{2,1,0:T(8,128)(2,1)S(1)}, u32[]{:S(2)}, u32[]{:S(2)}) collective-permute-start(bf16[8,48,960]{2,1,0:T(8,128)(2,1)S(1)} %constant_dynamic-update-slice_fusion.4.h0), channel_id=1, source_target_pairs={{0,2},{1,3},{2,0},{3,1},{4,6},{5,7},{6,4},{7,5},{8,10},{9,11},{10,... | collective-permute-start | bytes 2211848 | tf_op jit(solution)/shard_map/ppermute | solution.py:82
  77.4 17.2 %collective-permute-start.22 = (bf16[8,48,1024]{2,1,0:T(8,128)(2,1)S(1)}, bf16[8,48,1024]{2,1,0:T(8,128)(2,1)S(1)}, u32[]{:S(2)}, u32[]{:S(2)}) collective-permute-start(bf16[8,48,1024]{2,1,0:T(8,128)(2,1)S(1)} %constant_dynamic-update-slice_fusion.10.h2), channel_id=1, source_target_pairs={{0,4},{1,5},{2,6},{3,7},{4,0},{5,1},{6,2},{7,3},{8,12},{9,13},{10,... | collective-permute-start | bytes 2359304 | tf_op jit(solution)/shard_map/ppermute | solution.py:82
  78.1 17.6 %collective-permute-start.21 = (bf16[8,48,1024]{2,1,0:T(8,128)(2,1)S(1)}, bf16[8,48,1024]{2,1,0:T(8,128)(2,1)S(1)}, u32[]{:S(2)}, u32[]{:S(2)}) collective-permute-start(bf16[8,48,1024]{2,1,0:T(8,128)(2,1)S(1)} %constant_dynamic-update-slice_fusion.8.h0), channel_id=1, source_target_pairs={{0,2},{1,3},{2,0},{3,1},{4,6},{5,7},{6,4},{7,5},{8,10},{9,11},{10,... | collective-permute-start | bytes 2359304 | tf_op jit(solution)/shard_map/ppermute | solution.py:82
  129.9 32.7 %collective-permute-start.26 = (bf16[8,48,1792]{2,1,0:T(8,128)(2,1)}, bf16[8,48,1792]{2,1,0:T(8,128)(2,1)S(1)}, u32[]{:S(2)}, u32[]{:S(2)}) collective-permute-start(bf16[8,48,1792]{2,1,0:T(8,128)(2,1)} %get-tuple-element.274), channel_id=1, source_target_pairs={{0,4},{1,5},{2,6},{3,7},{4,0},{5,1},{6,2},{7,3},{8,12},{9,13},{10,... | collective-permute-start | bytes 4128776 | tf_op jit(solution)/shard_map/ppermute | solution.py:82
  131.1 32.4 %collective-permute-start.27 = (bf16[8,48,1792]{2,1,0:T(8,128)(2,1)}, bf16[8,48,1792]{2,1,0:T(8,128)(2,1)S(1)}, u32[]{:S(2)}, u32[]{:S(2)}) collective-permute-start(bf16[8,48,1792]{2,1,0:T(8,128)(2,1)} %get-tuple-element.276), channel_id=1, source_target_pairs={{0,8},{1,9},{2,10},{3,11},{4,12},{5,13},{6,14},{7,15},{8,0},{9,1},... | collective-permute-start | bytes 4128776 | tf_op jit(solution)/shard_map/ppermute | solution.py:82
  131.9 29.5 %collective-permute-start.28 = (bf16[512,768]{1,0:T(8,128)(2,1)}, bf16[512,768]{1,0:T(8,128)(2,1)S(1)}, u32[]{:S(2)}, u32[]{:S(2)}) collective-permute-start(bf16[512,768]{1,0:T(8,128)(2,1)} %get-tuple-element.292), channel_id=1, source_target_pairs={{0,2},{1,3},{2,0},{3,1},{4,6},{5,7},{6,4},{7,5},{8,10},{9,11},{10,... | collective-permute-start | bytes 2359304 | tf_op jit(solution)/shard_map/ppermute | solution.py:82
  163.8 18.4 %collective-permute-start.33 = (bf16[4,48,1792]{2,1,0:T(8,128)(2,1)S(1)}, bf16[4,48,1792]{2,1,0:T(8,128)(2,1)S(1)}, u32[]{:S(2)}, u32[]{:S(2)}) collective-permute-start(bf16[4,48,1792]{2,1,0:T(8,128)(2,1)S(1)} %get-tuple-element.297), channel_id=1, source_target_pairs={{0,2},{1,3},{2,0},{3,1},{4,6},{5,7},{6,4},{7,5},{8,10},{9,11},{10,... | collective-permute-start | bytes 2064392 | tf_op jit(solution)/shard_map/ppermute | solution.py:82
  165.7 18.4 %collective-permute-start.34 = (bf16[4,48,1792]{2,1,0:T(8,128)(2,1)S(1)}, bf16[4,48,1792]{2,1,0:T(8,128)(2,1)S(1)}, u32[]{:S(2)}, u32[]{:S(2)}) collective-permute-start(bf16[4,48,1792]{2,1,0:T(8,128)(2,1)S(1)} %get-tuple-element.298), channel_id=1, source_target_pairs={{0,4},{1,5},{2,6},{3,7},{4,0},{5,1},{6,2},{7,3},{8,12},{9,13},{10,... | collective-permute-start | bytes 2064392 | tf_op jit(solution)/shard_map/ppermute | solution.py:82
  170.9 25.8 %collective-permute-start.31 = (bf16[8,48,896]{2,1,0:T(8,128)(2,1)S(1)}, bf16[8,48,896]{2,1,0:T(8,128)(2,1)S(1)}, u32[]{:S(2)}, u32[]{:S(2)}) collective-permute-start(bf16[8,48,896]{2,1,0:T(8,128)(2,1)S(1)} %get-tuple-element.304), channel_id=1, source_target_pairs={{0,4},{1,5},{2,6},{3,7},{4,0},{5,1},{6,2},{7,3},{8,12},{9,13},{10,... | collective-permute-start | bytes 2064392 | tf_op jit(solution)/shard_map/ppermute | solution.py:82
  172.1 25.7 %collective-permute-start.32 = (bf16[8,48,896]{2,1,0:T(8,128)(2,1)S(1)}, bf16[8,48,896]{2,1,0:T(8,128)(2,1)S(1)}, u32[]{:S(2)}, u32[]{:S(2)}) collective-permute-start(bf16[8,48,896]{2,1,0:T(8,128)(2,1)S(1)} %get-tuple-element.306), channel_id=1, source_target_pairs={{0,8},{1,9},{2,10},{3,11},{4,12},{5,13},{6,14},{7,15},{8,0},{9,1},... | collective-permute-start | bytes 2064392 | tf_op jit(solution)/shard_map/ppermute | solution.py:82
  173.7 32.1 %collective-permute-start.30 = (bf16[512,768]{1,0:T(8,128)(2,1)S(1)}, bf16[512,768]{1,0:T(8,128)(2,1)S(1)}, u32[]{:S(2)}, u32[]{:S(2)}) collective-permute-start(bf16[512,768]{1,0:T(8,128)(2,1)S(1)} %finish.1.refs_2_), channel_id=1, source_target_pairs={{0,2},{1,3},{2,0},{3,1},{4,6},{5,7},{6,4},{7,5},{8,10},{9,11},{10,... | collective-permute-start | bytes 2359304 | tf_op jit(solution)/shard_map/ppermute | solution.py:82
  184.3 18.3 %collective-permute-start.37 = (bf16[2,48,1792]{2,1,0:T(8,128)(2,1)S(1)}, bf16[2,48,1792]{2,1,0:T(8,128)(2,1)S(1)}, u32[]{:S(2)}, u32[]{:S(2)}) collective-permute-start(bf16[2,48,1792]{2,1,0:T(8,128)(2,1)S(1)} %get-tuple-element.315), channel_id=1, source_target_pairs={{0,8},{1,9},{2,10},{3,11},{4,12},{5,13},{6,14},{7,15},{8,0},{9,1},... | collective-permute-start | bytes 1032200 | tf_op jit(solution)/shard_map/ppermute | solution.py:82
  185.1 17.6 %collective-permute-start.38 = (bf16[2,48,1792]{2,1,0:T(8,128)(2,1)S(1)}, bf16[2,48,1792]{2,1,0:T(8,128)(2,1)S(1)}, u32[]{:S(2)}, u32[]{:S(2)}) collective-permute-start(bf16[2,48,1792]{2,1,0:T(8,128)(2,1)S(1)} %get-tuple-element.316), channel_id=1, source_target_pairs={{0,16},{1,17},{2,18},{3,19},{4,20},{5,21},{6,22},{7,23},{8,24},{9,... | collective-permute-start | bytes 1032200 | tf_op jit(solution)/shard_map/ppermute | solution.py:82
  206.5 15.8 %collective-permute-start.43 = (bf16[2,48,896]{2,1,0:T(8,128)(2,1)S(1)}, bf16[2,48,896]{2,1,0:T(8,128)(2,1)S(1)}, u32[]{:S(2)}, u32[]{:S(2)}) collective-permute-start(bf16[2,48,896]{2,1,0:T(8,128)(2,1)S(1)} %get-tuple-element.340), channel_id=1, source_target_pairs={{0,16},{1,17},{2,18},{3,19},{4,20},{5,21},{6,22},{7,23},{8,24},{9,... | collective-permute-start | bytes 516104 | tf_op jit(solution)/shard_map/ppermute | solution.py:82
  209.7 24.1 %collective-permute-start.46 = (bf16[1,48,1792]{2,1,0:T(8,128)(2,1)}, bf16[1,48,1792]{2,1,0:T(8,128)(2,1)S(1)}, u32[]{:S(2)}, u32[]{:S(2)}) collective-permute-start(bf16[1,48,1792]{2,1,0:T(8,128)(2,1)} %get-tuple-element.331), channel_id=1, source_target_pairs={{0,16},{1,17},{2,18},{3,19},{4,20},{5,21},{6,22},{7,23},{8,24},{9,... | collective-permute-start | bytes 516104 | tf_op jit(solution)/shard_map/ppermute | solution.py:82
  209.8 24.0 %collective-permute-start.47 = (bf16[1,48,1792]{2,1,0:T(8,128)(2,1)}, bf16[1,48,1792]{2,1,0:T(8,128)(2,1)S(1)}, u32[]{:S(2)}, u32[]{:S(2)}) collective-permute-start(bf16[1,48,1792]{2,1,0:T(8,128)(2,1)} %get-tuple-element.332), channel_id=1, source_target_pairs={{0,2},{1,3},{2,0},{3,1},{4,6},{5,7},{6,4},{7,5},{8,10},{9,11},{10,... | collective-permute-start | bytes 516104 | tf_op jit(solution)/shard_map/ppermute | solution.py:82
  (67 other events, 864.8 us)

commit v4 on v3

--- a/solution.py
+++ b/solution.py
@@ -37,7 +37,8 @@
 ACROSS = ((Z_HIGH, Z_LOW, X_BIT, SIDE), (Z_HIGH, Z_LOW, SIDE, X_BIT))
 ALONG = ((Z_HIGH, Z_LOW, SIDE, X_BIT), (SIDE, Z_HIGH, X_BIT, Z_LOW))
 Z_LINE = (Z_HIGH, Z_LOW, Z_HIGH | Z_LOW)
-ROUTES = (ACROSS, ALONG)
+BESIDE = ((Z_HIGH, Z_LOW, SIDE, X_BIT), (Z_HIGH, SIDE, X_BIT, Z_LOW))
+ROUTES = (ACROSS, ALONG, BESIDE)
 
 
 def dot(left, right):
@@ -271,7 +272,7 @@
     return lax.optimization_barrier((value, *others))[0]
 
 
-def call(kernel, name, grid, in_specs, out_specs, out_shape, scratch, places, args, flops, vmem=6, aliases=None):
+def call(kernel, name, grid, in_specs, out_specs, out_shape, scratch, places, args, flops, vmem=10, aliases=None):
     moved = sum(a.size * a.dtype.itemsize for a in args)
     moved += sum(int(np.prod(s.shape)) * np.dtype(s.dtype).itemsize for s in out_shape)
     return pl.pallas_call(
@@ -359,51 +360,52 @@
     return pltpu.VMEM((2 * BLOCKS, BLOCK_ROWS, width), LOW)
 
 
-def pack_first_kernel(w, out):
+def pack_first_kernel(w, exit_layer, out):
     wide = [w[i][:, :128] for i in range(3)]
     narrow = [w[i][:, 128:] for i in range(3)]
-    out[...] = jnp.concatenate(wide + narrow, axis=1).astype(LOW)
-
-
-def pack_first(qkv):
+    live = jnp.float32(0.0)
+    for i in range(exit_layer.shape[0]):
+        live += jnp.where(exit_layer[i] >= LAYER, 1.0, 0.0)
+    row = lax.broadcasted_iota(jnp.int32, (out.shape[0], 64), 0)
+    marks = jnp.where(row == 0, live, 0.0)
+    out[...] = jnp.concatenate(wide + narrow + [marks], axis=1).astype(LOW)
+
+
+def pack_first(qkv, exit_layer):
     return pl.pallas_call(
         pack_first_kernel,
-        out_shape=shape((qkv.shape[1], 576), LOW),
+        in_specs=[whole(qkv), pl.BlockSpec(memory_space=pltpu.SMEM)],
+        out_shape=shape((qkv.shape[1], 640), LOW),
         name="pack_first",
-    )(qkv)
-
-
-def pack_kernel(places, exit_layer, up, out, down, pool, qv, upb, up_out, down_pool, biases):
-    up_out[:, 0:D] = up[...].astype(LOW)
-    up_out[:, D : D + 192] = out[...].T.astype(LOW)
-    down_pool[:, 0:D] = down[...].astype(LOW)
+    )(qkv, exit_layer)
+
+
+def pack_kernel(places, up, out, down, pool, qv, upb, up_out, down_pool, biases):
     quarter = 2 * places[CORE_AT] + places[0]
     mine = jnp.zeros((pool.shape[0], 192), WIDE)
     for i in range(4):
         mine = jnp.where(quarter == i, pool[:, 192 * i : 192 * (i + 1)], mine)
-    live = jnp.float32(0.0)
-    for i in range(exit_layer.shape[0]):
-        live += jnp.where(exit_layer[i] >= LAYER, 1.0, 0.0)
-    row = lax.broadcasted_iota(jnp.int32, (pool.shape[0], 64), 0)
-    marks = jnp.where(row == 0, live, 0.0)
-    down_pool[:, D : D + 256] = jnp.concatenate([mine, marks], axis=1).astype(LOW)
+    up_out[:, 0:D] = up[...].astype(LOW)
+    up_out[:, D : D + 256] = jnp.concatenate([out[...].T, mine[:, 0:64]], axis=1).astype(LOW)
+    down_pool[:, 0:D] = down[...].astype(LOW)
+    down_pool[:, D : D + 128] = mine[:, 64:192].astype(LOW)
     biases[...] = jnp.zeros_like(biases)
     biases[0:1, :] = upb[...].reshape(1, D)
     biases[1:2, 0:192] = qv[0:1, :]
     biases[2:3, 0:192] = qv[1:2, :]
 
 
-def pack(places, exit_layer, up, out, down, pool, qv, upb):
+def pack(places, up, out, down, pool, qv, upb):
     share = up.shape[0]
-    args = (exit_layer, up, out, down, pool, qv, upb)
+    args = (up, out, down, pool, qv, upb)
     return call(
         pack_kernel,
         "pack",
         (1,),
-        [pl.BlockSpec(memory_space=pltpu.SMEM)] + [whole(a) for a in args[1:]],
-        [pl.BlockSpec((share, 960), lambda *_: (0, 0)), pl.BlockSpec((share, 1024), lambda *_: (0, 0))]
+        [whole(a) for a in args],
+        [pl.BlockSpec((share, 1024), lambda *_: (0, 0)), pl.BlockSpec((share, 896), lambda *_: (0, 0))]
         + [pl.BlockSpec((8, D), lambda *_: (0, 0))],
-        [shape((share, 960), LOW), shape((share, 1024), LOW), shape((8, D), WIDE)],
+        [shape((share, 1024), LOW), shape((share, 896), LOW), shape((8, D), WIDE)],
         [],
         places,
         args,
@@ -417,12 +419,14 @@
     return jnp.where(upper, other, mine), jnp.where(upper, mine, other)
 
 
-def project_kernel(places, x, bias, bias_other, h0, h1, h2, h3, q, k, v, w, held, pairs):
+def project_kernel(places, x, bias, bias_other, h0, h1, h2, h3, q, k, v, w, count, held, pairs):
     @pl.when(pl.program_id(0) == 0)
     def _():
         gather_blocks(places, (h0, h1, h2, h3), held)
         for i in range(3):
             w[i] = to_pairs(held, 128 * i, 512 + 64 * i - 128)
+        live = jnp.sum(side_of(held, 0, 576, 64).astype(WIDE), axis=0, keepdims=True)
+        count[...] = jnp.broadcast_to(live[:, 0:1], count.shape)
         left, right = by_side(places, bias[...], bias_other[...])
         pairs[...] = jnp.concatenate(
             [left[:, :128], right[:, :128], left[:, 128:192], right[:, 128:192]], axis=1
@@ -443,9 +447,10 @@
         (LEN // step,),
         [pl.BlockSpec((step, D), lambda i, places: (places[0] * (LEN // step) + i, 0))]
         + [whole(a) for a in args[1:]],
-        [rows(step, 384)] * 3 + [pl.BlockSpec((3, D, 384), lambda *_: (0, 0, 0))],
-        [shape((LEN, 384), LOW)] * 3 + [shape((3, D, 384), LOW)],
-        [held_blocks(576), pltpu.VMEM((8, 384), WIDE)],
+        [rows(step, 384)] * 3
+        + [pl.BlockSpec((3, D, 384), lambda *_: (0, 0, 0)), pl.BlockSpec((8, 128), lambda *_: (0, 0))],
+        [shape((LEN, 384), LOW)] * 3 + [shape((3, D, 384), LOW), shape((8, 128), WIDE)],
+        [held_blocks(640), pltpu.VMEM((8, 384), WIDE)],
         places,
         args,
         2 * LEN * D * 1152,
@@ -501,28 +506,36 @@
     )
 
 
-def out_kernel(places, o, h0, h1, h2, h3, z, w_out, w_up, held):
+def out_kernel(places, o, h0, h1, h2, h3, z0, z1, w_out, w_up, pool, held):
     @pl.when(pl.program_id(0) == 0)
     def _():
         gather_blocks(places, (h0, h1, h2, h3), held)
         w_out[...] = to_pairs(held, D, D + 128)
         w_up[:, 0:D] = side_of(held, 0, 0, D)
         w_up[:, D : 2 * D] = side_of(held, 1, 0, D)
-
-    z[...] = dot_nt(o[...], w_out[...]).astype(LOW)
+        pool[...] = jnp.concatenate([side_of(held, i, 960, 64) for i in range(2)], axis=1)
+
+    z = dot_nt(o[...], w_out[...]).astype(LOW)
+    for i, out in enumerate((z0, z1)):
+
+        @pl.when(pl.program_id(0) == i)
+        def _(out=out):
+            out[...] = z
 
 
 def project_out(places, o, halves):
-    step = 256
+    step = 512
     return call(
         out_kernel,
         "project_out",
         (LEN // step,),
         [rows(step, 384)] + [whole(a) for a in halves],
-        [rows(step, D), pl.BlockSpec((D, 384), lambda *_: (0, 0))]
-        + [pl.BlockSpec((D, 2 * D), lambda *_: (0, 0))],
-        [shape((LEN, D), LOW), shape((D, 384), LOW), shape((D, 2 * D), LOW)],
-        [held_blocks(960)],
+        [pl.BlockSpec((step, D), lambda *_: (0, 0))] * 2
+        + [pl.BlockSpec((D, 384), lambda *_: (0, 0))]
+        + [pl.BlockSpec((D, 2 * D), lambda *_: (0, 0)), pl.BlockSpec((D, 128), lambda *_: (0, 0))],
+        [shape((step, D), LOW)] * 2
+        + [shape((D, 384), LOW), shape((D, 2 * D), LOW), shape((D, 128), LOW)],
+        [held_blocks(1024)],
         places,
         (o, *halves),
         2 * LEN * D * 384,
@@ -543,14 +556,19 @@
     )
 
 
-def up_kernel(places, x, z, zp, vec, bias_mine, bias_other, w, m, slope, n1, rs1, low, bias):
+def up_kernel(
+    places, x, z0, z1, zp0, zp1, vec, bias_mine, bias_other, w, m, slope, n1, rs1, low, bias
+):
     @pl.when(pl.program_id(0) == 0)
     def _():
         left, right = by_side(places, bias_mine[0:1, :], bias_other[0:1, :])
         bias[:, 0:D] = left
         bias[:, D : 2 * D] = right
 
-    total = z[...].astype(WIDE) + zp[...].astype(WIDE)
+    early = pl.program_id(0) < 2
+    mine = jnp.where(early, z0[...], z1[...]).astype(WIDE)
+    other = jnp.where(early, zp0[...], zp1[...]).astype(WIDE)
+    total = mine + other
     normed, spread = normalize(x[...].astype(WIDE) + total + vec[4:5, :])
     n1[...] = normed
     rs1[...] = jnp.broadcast_to(spread, rs1.shape)
@@ -566,14 +584,17 @@
 
 def feed_up(places, tokens, z, zp, vec, bias, bias_other, w_up):
     step = 256
-    args = (tokens, z, zp, vec, bias, bias_other, w_up)
+    args = (tokens, *z, *zp, vec, bias, bias_other, w_up)
     return call(
         up_kernel,
         "feed_up",
         (LEN // step,),
         [pl.BlockSpec((step, D), lambda i, places: (places[0] * (LEN // step) + i, 0))]
-        + [rows(step, D)] * 2
-        + [whole(a) for a in args[3:]],
+        + [
+            pl.BlockSpec((step, D), lambda i, *_, at=at: (jnp.clip(i - at, 0, 1), 0))
+            for at in (0, 2, 0, 2)
+        ]
+        + [whole(a) for a in args[5:]],
         [rows(step, 2 * D)] * 2
         + [rows(step, D), rows(step, 128), rows(step, D)],
         [shape((LEN, 2 * D), LOW)] * 2
@@ -585,39 +606,39 @@
     )
 
 
-def down_kernel(places, m, h0, h1, h2, h3, f, w, pool, count, held):
+def down_kernel(places, m, pool_part, h0, h1, h2, h3, f, w, pool, held):
     @pl.when(pl.program_id(0) == 0)
     def _():
         gather_blocks(places, (h0, h1, h2, h3), held)
+        pieces = []
         for side in range(2):
             w[:, D * side : D * (side + 1)] = side_of(held, side, 0, D)
-        pool[...] = jnp.concatenate([side_of(held, side, D, 192) for side in range(2)], axis=1)
-        live = jnp.sum(side_of(held, 0, D + 192, 64).astype(WIDE), axis=0, keepdims=True)
-        count[...] = jnp.broadcast_to(live[:, 0:1], count.shape)
+            pieces += [pool_part[:, 64 * side : 64 * (side + 1)], side_of(held, side, D, 128)]
+        pool[...] = jnp.concatenate(pieces, axis=1)
 
     f[...] = dot_nt(m[...], w[...]).astype(LOW)
 
 
-def feed_down(places, m, halves):
-    step = 256
+def feed_down(places, m, pool_part, halves):
+    step = 512
     return call(
         down_kernel,
         "feed_down",
         (LEN // step,),
-        [rows(step, 2 * D)] + [whole(a) for a in halves],
+        [rows(step, 2 * D), whole(pool_part)] + [whole(a) for a in halves],
         [rows(step, D), pl.BlockSpec((D, 2 * D), lambda *_: (0, 0))]
-        + [pl.BlockSpec((D, 384), lambda *_: (0, 0)), pl.BlockSpec((8, 128), lambda *_: (0, 0))],
-        [shape((LEN, D), LOW), shape((D, 2 * D), LOW), shape((D, 384), LOW), shape((8, 128), WIDE)],
-        [held_blocks(1024)],
-        places,
-        (m, *halves),
+        + [pl.BlockSpec((D, 384), lambda *_: (0, 0))],
+        [shape((LEN, D), LOW), shape((D, 2 * D), LOW), shape((D, 384), LOW)],
+        [held_blocks(896)],
+        places,
+        (m, pool_part, *halves),
         2 * LEN * D * 2 * D,
     )
 
 
 def turn_kernel(
     places, exit_layer, labels, n1, f, fp, cot, vec, pool_a, pool_b, classes, bias, live_count,
-    y, half, dh2, low, sums, ramp, pool
+    y, half, low, sums, ramp, pool, dy
 ):
     step = pl.program_id(0)
     middle = n1[...] * vec[0:1, :] + vec[1:2, :]
@@ -633,7 +654,7 @@
 
     leaves = exit_layer[places[0]]
     grad = cot[...].astype(WIDE) * jnp.where(leaves > LAYER, 1.0, 0.0)
-    dh2[...] = grad
+    dy[...] = grad
 
     @pl.when(step == 0)
     def _():
@@ -672,7 +693,7 @@
         grad_logits = jnp.where(valid & (row == 0), grad_logits, 0.0).astype(LOW)
         grad_pre = (dot_nt(grad_logits, classes[...]) * (1.0 - pooled * pooled)).astype(LOW)
         grad_head = dot_nt(grad_pre, pool[...])
-        dh2[0:count, :] = dh2[0:count, :] + grad_head
+        dy[0:count, :] = dy[0:count, :] + grad_head
         sums[3:4, :] = grad_pre[0:1, :].astype(WIDE)
         of_class = dot_tn(grad_logits, pooled_low)
         sums[4:7, :] = of_class[0:3, :]
@@ -681,12 +702,11 @@
         ramp[0:1, :] = head[0:1, :].astype(WIDE)
         ramp[1:2, :] = grad_pre[0:1, :].astype(WIDE)
 
-    grad = dh2[...]
+    grad = dy[...]
     sums[0:1, :] += jnp.sum(grad * normed, axis=0, keepdims=True)
     sums[1:2, :] += jnp.sum(grad, axis=0, keepdims=True)
     back = norm_back(grad * vec[2:3, :], normed, spread)
     sums[2:3, :] += jnp.sum(back, axis=0, keepdims=True)
-    dh2[...] = back
     low[...] = back.astype(LOW)
 
 
@@ -716,12 +736,11 @@
         + [own_rows(step)]
         + [whole(a) for a in args[6:]],
         [own_rows(step), half_rows(step)]
-        + [rows(step, D)] * 2
+        + [rows(step, D)]
         + [pl.BlockSpec((8, D), lambda *_: (0, 0))] * 2,
-        [shape((2 * LEN, D), LOW), shape((LEN // 2, D), LOW)]
-        + [shape((LEN, D), WIDE), shape((LEN, D), LOW)]
+        [shape((2 * LEN, D), LOW), shape((LEN // 2, D), LOW), shape((LEN, D), LOW)]
         + [shape((8, D), WIDE)] * 2,
-        [pltpu.VMEM((D, D), LOW)],
+        [pltpu.VMEM((D, D), LOW), pltpu.VMEM((step, D), WIDE)],
         places,
         args,
         LEN * D * 60,
@@ -742,7 +761,7 @@
 
 
 def feed_back(places, dh2, slope, w_down, w_up):
-    step = 256
+    step = 512
     args = (dh2, slope, w_down, w_up)
     return call(
         feed_back_kernel,
@@ -755,6 +774,7 @@
         places,
         args,
         4 * LEN * D * 2 * D,
+        vmem=14,
     )
 
 
@@ -809,7 +829,7 @@
         sums[12:13, :] = up_sums[0:1, D : 2 * D]
 
     total = dx[...].astype(WIDE) + dxp[...].astype(WIDE)
-    grad = dh2[...] + total
+    grad = dh2[...].astype(WIDE) + total
     normed = n1[...]
     sums[8:9, :] += jnp.sum(grad * normed, axis=0, keepdims=True)
     sums[9:10, :] += jnp.sum(grad, axis=0, keepdims=True)
@@ -850,7 +870,7 @@
     k_own = [jnp.where(first, k, zero), jnp.where(first, zero, k)]
     scaled = (do_ref[...].astype(WIDE) * inv_ref[...]).astype(LOW)
     held[...] = scaled
-    step = 256
+    step = 512
     for i in range(n // step):
         at = pl.ds(i * step, step)
         d = held[at, :]
@@ -892,7 +912,7 @@
         places,
         (q, k, v, do, inv, p),
         8 * 6 * LEN * LEN * 256,
-        vmem=18,
+        vmem=19,
     )
 
 
@@ -919,7 +939,7 @@
     block = marks[...].astype(LOW)
     for p in range(2 * BLOCKS):
         held[p, :, D : D + 128] = block
-    scatter_blocks(places, held, (h0, h1, h2, h3), ALONG)
+    scatter_blocks(places, held, (h0, h1, h2, h3), BESIDE)
 
 
 def narrow_grad(places, tokens, dh1, o, grads, sums):
@@ -936,7 +956,7 @@
         places,
         args,
         2 * LEN * D * 1536,
-        vmem=9,
+        vmem=12,
     )
 
 
@@ -947,7 +967,7 @@
         part = dot_nt(grads[i][...], w[i])
         total = part if total is None else total + part
     total = total.astype(LOW)
-    mine = pl.program_id(0) // 2 == places[CORE_AT]
+    mine = pl.program_id(0) == places[CORE_AT]
 
     @pl.when(mine)
     def _():
@@ -959,7 +979,7 @@
 
 
 def input_grad(places, grads, w):
-    step = 256
+    step = 512
     return call(
         input_kernel,
         "input_grad",
@@ -1174,11 +1194,10 @@
 
     by_kind = [a.transpose(1, 0, 2) for a in (qkv_weight, qkv_first, qkv_second)]
     down_turned = [a.T for a in (down_weight, down_first, down_second)]
-    qkv_spread = links.spread(pack_first(by_kind[0]))
+    qkv_spread = links.spread(pack_first(by_kind[0], exit_layer))
     sent = qkv_spread.step()
     up_out, down_pool, biases = pack(
         places,
-        exit_layer,
         after(up_weight, *sent),
         out_weight,
         down_turned[0],
@@ -1200,23 +1219,23 @@
     sent = down_spread.step(*sent)
 
     biases = after(biases, *sent)
-    q, k, v, w_qkv = project(places, tokens, biases, other_biases, qkv_spread.halves())
+    q, k, v, w_qkv, live_count = project(places, tokens, biases, other_biases, qkv_spread.halves())
     sent = up_out_spread.step(q)
     q = after(q, *sent)
     o, inv, p = attend(places, q, k, v)
     sent = down_spread.step(o)
     o = after(o, *sent)
-    z, w_out, w_up = project_out(places, o, up_out_spread.halves())
-    zp = links.swap(z, CORE)
-    sent = down_spread.step(z)
+    *z, w_out, w_up, pool_part = project_out(places, o, up_out_spread.halves())
+    zp = [links.swap(part, CORE) for part in z]
+    sent = down_spread.step(w_up)
     z = after(z, *sent)
     m, slope, n1, rs1, middle_low = feed_up(
         places, tokens, z, zp, layer_vectors, biases, other_biases, w_up
     )
-    f, w_down, pool_mine, live_count = feed_down(places, m, down_spread.halves())
+    f, w_down, pool_mine = feed_down(places, m, pool_part, down_spread.halves())
     fp = links.swap(f, CORE)
     pool_other = links.swap(pool_mine, CORE)
-    y, y_half, dh2, dh2_low, turn_sums, ramp = turn(
+    y, y_half, dh2_low, turn_sums, ramp = turn(
         places, exit_layer, labels, n1, f, fp, cotangent, layer_vectors, pool_mine, pool_other,
         classes, class_bias, live_count,
     )
@@ -1231,7 +1250,7 @@
     feed_fold.step()
     dx = after(dx, *feed_halves)
     dh1, dh1_low, do, sums = mid(
-        places, dh2, dx, dxp, n1, rs1, layer_vectors, w_out, turn_sums, up_sums
+        places, dh2_low, dx, dxp, n1, rs1, layer_vectors, w_out, turn_sums, up_sums
     )
     grads = attend_back(places, q, k, v, do, inv, p)
     token_keep, token_send = input_grad(places, grads, w_qkv)
@@ -1239,7 +1258,7 @@
     sent = feed_fold.step(token_keep, y_first)
     grads = after(grads, *sent)
     narrow_halves = narrow_grad(places, tokens, dh1_low, o, grads, sums)
-    narrow_fold = links.fold(narrow_halves, ALONG, D)
+    narrow_fold = links.fold(narrow_halves, BESIDE, D)
     narrow_fold.step()
     token_keep = after(token_keep, *narrow_halves)
     grad_half = finish(places, dh1, token_keep, token_other)
@@ -1254,6 +1273,20 @@
     tokens_grad = place(places, None, [first, second, grad_half, second_own])
     result = place(places, y, [y_first, after(y_second, tokens_grad)])
     sent = narrow_fold.step(result)
+    masters = [*down_turned, up_weight, up_first, up_second, pool_weight, pool_first, pool_second]
+    feed_new = update(
+        places,
+        "update_feed",
+        after(feed_fold.pieces(), *sent),
+        2 * D + 16 * slots,
+        masters,
+        update_feed_kernel,
+        [o for a in masters[0::3] for o in matrix_outs(a)],
+        [pltpu.VMEM((slots, D), WIDE)] * 2,
+    )
+    down_new, down_first_new, down_second_new, down_copy = (a.T for a in feed_new[0:4])
+    up_new, up_first_new, up_second_new, up_copy = feed_new[4:8]
+    pool_new, pool_first_new, pool_second_new, pool_copy = feed_new[8:12]
     by_class = [a.T for a in (class_weight, class_first, class_second)]
     masters = [*by_kind, out_weight, out_first, out_second]
     vectors = [qv_bias, qv_first, qv_second, up_bias, upb_first, upb_second]
@@ -1261,7 +1294,7 @@
     narrow_new = update(
         places,
         "update_narrow",
-        narrow_fold.pieces(),
+        after(narrow_fold.pieces(), feed_new[0]),
         D + 128,
         [*masters, *vectors, live_count],
         update_narrow_kernel,
@@ -1270,20 +1303,6 @@
         + [shape((1, 1), WIDE)],
         [pltpu.VMEM((16, D), WIDE)],
     )
-    masters = [*down_turned, up_weight, up_first, up_second, pool_weight, pool_first, pool_second]
-    feed_new = update(
-        places,
-        "update_feed",
-        after(feed_fold.pieces(), narrow_new[0]),
-        2 * D + 16 * slots,
-        masters,
-        update_feed_kernel,
-        [o for a in masters[0::3] for o in matrix_outs(a)],
-        [pltpu.VMEM((slots, D), WIDE)] * 2,
-    )
-    down_new, down_first_new, down_second_new, down_copy = (a.T for a in feed_new[0:4])
-    up_new, up_first_new, up_second_new, up_copy = feed_new[4:8]
-    pool_new, pool_first_new, pool_second_new, pool_copy = feed_new[8:12]
     qkv_new, qkv_first_new, qkv_second_new, qkv_copy = (
         a.transpose(1, 0, 2) for a in narrow_new[0:4]
     )

time: 241 us -> 227 us (0.942)
  waiting for transfers between devices: 71.4 us -> 64.8 us
  Pallas kernels: 105 us -> 99 us
  local copies, waits for them, and re-layouts: 10.6 us -> 6.32 us
    ppermute x48 -> x49, waiting for transfers between devices: 71.4 us -> 64.8 us  [swap(): return lax.ppermute(value, ('dp', 'mp'), pairs)]
    pallas_call x18, Pallas kernels: 101 us -> 96.1 us  [call(): pl.pallas_call(kernel, out_shape=out_shape, grid_spec=pltpu.PrefetchScala...]
    unnamed x93 -> x85, local copies, waits for them, and re-layouts: 8.49 us -> 4.23 us
    ppermute x48 -> x49, starting transfers between devices: 50.5 us -> 52.7 us  [swap(): return lax.ppermute(value, ('dp', 'mp'), pairs)]
  transfers between devices with their start and end apart: 48 -> 49, of which waited for: 25 -> 25; matrix products, arithmetic and copies ran while one was open for 1% -> 1% of each run, Pallas kernels for 33% -> 34%
where the time goes in v4:
time: 227 us; the launch traced here: 225 us
  Pallas kernels  99 us (44%)
  waiting for transfers between devices  64.8 us (29%)
  starting transfers between devices  52.7 us (23%)
  local copies, waits for them, and re-layouts  6.32 us (3%)
    pallas_call x18, Pallas kernels, call(): pl.pallas_call(kernel, out_shape=out_shape, grid_spec=pltpu.PrefetchScala...  96.1 us
    ppermute x49, waiting for transfers between devices, swap(): return lax.ppermute(value, ('dp', 'mp'), pairs)  64.8 us
    ppermute x49, starting transfers between devices, swap(): return lax.ppermute(value, ('dp', 'mp'), pairs)  52.7 us
  transfers between devices with their start and end apart: 49, of which 25 were waited for; matrix products, arithmetic and copies ran while one was open for 1% of the time, Pallas kernels for 34%

profile of v4, /device:TPU:0, one launch (start us, length us, event | category | flops | bytes accessed | tf_op | source)
XLA Modules:
  0.0 225.4 jit_solution(14195939201558946946)
XLA Ops:
  2.4 5.0 %collective-permute-start.2 = (bf16[1,96,640]{2,1,0:T(8,128)(2,1)}, bf16[1,96,640]{2,1,0:T(8,128)(2,1)S(1)}, u32[]{:S(2)}, u32[]{:S(2)}) collective-permute-start(bf16[1,96,640]{2,1,0:T(8,128)(2,1)} %bitcast.32), channel_id=1, source_target_pairs={{0,24},{1,25},{2,26},{3,27},{4,28},{5,29},{6,30},{7,31},{8,16},{9,... | collective-permute-start | bytes 368648 | tf_op jit(solution)/shard_map/ppermute | solution.py:83
  9.3 2.8 %pack.1 = (bf16[96,1024]{1,0:T(8,128)(2,1)}, bf16[96,896]{1,0:T(8,128)(2,1)}, f32[8,768]{1,0:T(8,128)}) custom-call(s32[100]{0:T(128)} %concatenate.39.places, f32[96,768]{1,0:T(8,128)} %refs_13_.2, f32[192,96]{1,0:T(8,128)} %refs_13_.3, f32[96,768]{1,0:T(8,128)} %bitcast.30, f32[96,768]{1,0:T(8,128)} %refs_16_.2, f32[2,192]{1,0:T(2,128)} %refs_16_.3, ...), custom_call_target="tpu_custom_call" | custom-call | bytes 84768 | tf_op jit(solution)/shard_map/pack/pallas_call | solution.py:278
  31.8 4.2 %collective-permute-done.4 = bf16[1,96,1024]{2,1,0:T(8,128)(2,1)S(1)} collective-permute-done((bf16[1,96,1024]{2,1,0:T(8,128)(2,1)S(1)}, bf16[1,96,1024]{2,1,0:T(8,128)(2,1)S(1)}, u32[]{:S(2)}, u32[]{:S(2)}) %collective-permute-start.4) | collective-permute-done | bytes 196640 | tf_op jit(solution)/shard_map/ppermute | solution.py:83
  36.1 3.7 %collective-permute-done.3 = bf16[1,96,1024]{2,1,0:T(8,128)(2,1)S(1)} collective-permute-done((bf16[1,96,1024]{2,1,0:T(8,128)(2,1)S(1)}, bf16[1,96,1024]{2,1,0:T(8,128)(2,1)S(1)}, u32[]{:S(2)}, u32[]{:S(2)}) %collective-permute-start.3) | collective-permute-done | bytes 196640 | tf_op jit(solution)/shard_map/ppermute | solution.py:83
  45.5 4.4 %project.1 = (bf16[1024,384]{1,0:T(8,128)(2,1)S(1)}, bf16[1024,384]{1,0:T(8,128)(2,1)S(1)}, bf16[1024,384]{1,0:T(8,128)(2,1)S(1)}, bf16[3,768,384]{2,1,0:T(8,128)(2,1)S(1)}, f32[8,128]{1,0:T(8,128)S(1)}) custom-call(s32[100]{0:T(128)S(1)} %copy-done.27, bf16[2048,768]{1,0:T(8,128)(2,1)S(1)} %copy-done, f32[8,768]{1,0:T(8,128)S(1)} %copy-done.28, ...), custom_call_target="tpu_custom_call" | custom-call | flops 113246208 | bytes 580864 | tf_op jit(solution)/shard_map/project/pallas_call | solution.py:278
  54.5 11.8 %attend_forward.1 = (bf16[1024,384]{1,0:T(8,128)(2,1)S(1)}, f32[1024,384]{1,0:T(8,128)S(1)}, bf16[6,1024,1024]{2,1,0:T(8,128)(2,1)S(1)}) custom-call(s32[100]{0:T(128)S(1)} %copy-done.27, bf16[1024,384]{1,0:T(8,128)(2,1)S(1)} %get-tuple-element.253.q_ref, bf16[1024,384]{1,0:T(8,128)(2,1)S(1)} %get-tuple-element.254.k_ref, ...), custom_call_target="tpu_custom_call" | custom-call | flops 402653184 | bytes 1081344 | tf_op jit(solution)/shard_map/attend_forward/pallas_call | solution.py:278
  80.5 7.8 %feed_up.1 = (bf16[1024,1536]{1,0:T(8,128)(2,1)S(1)}, bf16[1024,1536]{1,0:T(8,128)(2,1)S(1)}, f32[1024,768]{1,0:T(8,128)S(1)}, f32[1024,128]{1,0:T(8,128)S(1)}, bf16[1024,768]{1,0:T(8,128)(2,1)S(1)}) custom-call(s32[100]{0:T(128)S(1)} %copy-done.27, bf16[2048,768]{1,0:T(8,128)(2,1)S(1)} %copy-done, bf16[512,768]{1,0:T(8,128)(2,1)S(1)} %get-tuple-element.269.z0, ...), custom_call_target="tpu_custom_call" | custom-call | flops 150994944 | bytes 1265984 | tf_op jit(solution)/shard_map/feed_up/pallas_call | solution.py:278
  90.9 4.1 %collective-permute-done.22.h1 = bf16[8,48,896]{2,1,0:T(8,128)(2,1)S(1)} collective-permute-done((bf16[8,48,896]{2,1,0:T(8,128)(2,1)S(1)}, bf16[8,48,896]{2,1,0:T(8,128)(2,1)S(1)}, u32[]{:S(2)}, u32[]{:S(2)}) %collective-permute-start.22) | collective-permute-done | bytes 688160 | tf_op jit(solution)/shard_map/ppermute | solution.py:83
  95.0 3.8 %feed_down.1 = (bf16[1024,768]{1,0:T(8,128)(2,1)S(1)}, bf16[768,1536]{1,0:T(8,128)(2,1)S(1)}, bf16[768,384]{1,0:T(8,128)(2,1)S(1)}) custom-call(s32[100]{0:T(128)S(1)} %copy-done.27, bf16[1024,1536]{1,0:T(8,128)(2,1)S(1)} %get-tuple-element.283.m, bf16[768,128]{1,0:T(8,128)(2,1)S(1)} %get-tuple-element.273.pool_part, ...), custom_call_target="tpu_custom_call" | custom-call | flops 150994944 | bytes 663552 | tf_op jit(solution)/shard_map/feed_down/pallas_call | solution.py:278
  99.4 3.7 %collective-permute-done.25.pool_b = bf16[768,384]{1,0:T(8,128)(2,1)S(1)} collective-permute-done((bf16[768,384]{1,0:T(8,128)(2,1)S(1)}, bf16[768,384]{1,0:T(8,128)(2,1)S(1)}, u32[]{:S(2)}, u32[]{:S(2)}) %collective-permute-start.25) | collective-permute-done | bytes 589856 | tf_op jit(solution)/shard_map/ppermute | solution.py:83
  103.2 6.6 %turn.1 = (bf16[2048,768]{1,0:T(8,128)(2,1)}, bf16[512,768]{1,0:T(8,128)(2,1)}, bf16[1024,768]{1,0:T(8,128)(2,1)S(1)}, f32[8,768]{1,0:T(8,128)S(1)}, f32[8,768]{1,0:T(8,128)S(1)}) custom-call(s32[100]{0:T(128)S(1)} %copy-done.27, s32[2]{0:T(128)S(1)} %copy-done.30, s32[2]{0:T(128)S(1)} %copy-done.31, f32[1024,768]{1,0:T(8,128)S(1)} %get-tuple-element.271.n1, ...), custom_call_target="tpu_custom_call" | custom-call | flops 2949120 | bytes 1024609 | tf_op jit(solution)/shard_map/turn/pallas_call | solution.py:278
  109.8 6.7 %feed_back.1 = (bf16[1024,1536]{1,0:T(8,128)(2,1)S(1)}, bf16[1024,768]{1,0:T(8,128)(2,1)S(1)}, f32[8,1536]{1,0:T(8,128)S(1)}) custom-call(s32[100]{0:T(128)S(1)} %copy-done.27, bf16[1024,768]{1,0:T(8,128)(2,1)S(1)} %get-tuple-element.282.dh2, bf16[1024,1536]{1,0:T(8,128)(2,1)S(1)} %get-tuple-element.279.slope, ...), custom_call_target="tpu_custom_call" | custom-call | flops 301989888 | bytes 887808 | tf_op jit(solution)/shard_map/feed_back/pallas_call | solution.py:278
  116.7 7.2 %feed_grad.1 = (bf16[8,48,1792]{2,1,0:T(8,128)(2,1)S(1)}, bf16[8,48,1792]{2,1,0:T(8,128)(2,1)S(1)}, bf16[8,48,1792]{2,1,0:T(8,128)(2,1)S(1)}, bf16[8,48,1792]{2,1,0:T(8,128)(2,1)}) custom-call(s32[100]{0:T(128)S(1)} %copy-done.27, bf16[1024,768]{1,0:T(8,128)(2,1)S(1)} %get-tuple-element.282.dh2, bf16[1024,1536]{1,0:T(8,128)(2,1)S(1)} %get-tuple-element.283.m, ...), custom_call_target="tpu_custom_call" | custom-call | flops 301989888 | bytes 935424 | tf_op jit(solution)/shard_map/feed_grad/pallas_call | solution.py:278
  127.7 4.1 %middle_back.1 = (f32[1024,768]{1,0:T(8,128)S(1)}, bf16[1024,768]{1,0:T(8,128)(2,1)S(1)}, bf16[1024,384]{1,0:T(8,128)(2,1)S(1)}, f32[16,768]{1,0:T(8,128)S(1)}) custom-call(s32[100]{0:T(128)S(1)} %copy-done.27, bf16[1024,768]{1,0:T(8,128)(2,1)S(1)} %get-tuple-element.282.dh2, bf16[1024,768]{1,0:T(8,128)(2,1)S(1)} %get-tuple-element.291.dx, ...), custom_call_target="tpu_custom_call" | custom-call | flops 37748736 | bytes 914240 | tf_op jit(solution)/shard_map/middle_back/pallas_call | solution.py:278
  131.9 16.0 %attend_backward.1 = (bf16[1024,384]{1,0:T(8,128)(2,1)S(1)}, bf16[1024,384]{1,0:T(8,128)(2,1)S(1)}, bf16[1024,384]{1,0:T(8,128)(2,1)S(1)}) custom-call(s32[100]{0:T(128)S(1)} %copy-done.27, bf16[1024,384]{1,0:T(8,128)(2,1)S(1)} %get-tuple-element.253.q_ref, bf16[1024,384]{1,0:T(8,128)(2,1)S(1)} %get-tuple-element.254.k_ref, ...), custom_call_target="tpu_custom_call" | custom-call | flops 805306368 | bytes 1228800 | tf_op jit(solution)/shard_map/attend_backward/pallas_call | solution.py:278
  147.9 3.8 %input_grad.1 = (bf16[512,768]{1,0:T(8,128)(2,1)S(1)}, bf16[512,768]{1,0:T(8,128)(2,1)S(1)}) custom-call(s32[100]{0:T(128)S(1)} %copy-done.27, bf16[1024,384]{1,0:T(8,128)(2,1)S(1)} %get-tuple-element.313.refs_0_.dq, bf16[1024,384]{1,0:T(8,128)(2,1)S(1)} %get-tuple-element.314.refs_1_.dk, bf16[1024,384]{1,0:T(8,128)(2,1)S(1)} %get-tuple-element.315.refs_2_.dv, ...), custom_call_target="tpu_custom_call" | custom-call | flops 113246208 | bytes 356352 | tf_op jit(solution)/shard_map/input_grad/pallas_call | solution.py:278
  151.7 4.7 %collective-permute-done.27.refs_1_ = bf16[8,48,1792]{2,1,0:T(8,128)(2,1)S(1)} collective-permute-done((bf16[8,48,1792]{2,1,0:T(8,128)(2,1)S(1)}, bf16[8,48,1792]{2,1,0:T(8,128)(2,1)S(1)}, u32[]{:S(2)}, u32[]{:S(2)}) %collective-permute-start.27) | collective-permute-done | bytes 1376288 | tf_op jit(solution)/shard_map/ppermute | solution.py:83
  160.3 4.4 %narrow_grad.1 = (bf16[8,48,896]{2,1,0:T(8,128)(2,1)S(1)}, bf16[8,48,896]{2,1,0:T(8,128)(2,1)S(1)}, bf16[8,48,896]{2,1,0:T(8,128)(2,1)S(1)}, bf16[8,48,896]{2,1,0:T(8,128)(2,1)S(1)}) custom-call(s32[100]{0:T(128)S(1)} %copy-done.27, bf16[2048,768]{1,0:T(8,128)(2,1)S(1)} %copy-done, bf16[1024,768]{1,0:T(8,128)(2,1)S(1)} %get-tuple-element.305.dh1, ...), custom_call_target="tpu_custom_call" | custom-call | flops 150994944 | bytes 666624 | tf_op jit(solution)/shard_map/narrow_grad/pallas_call | solution.py:278
  168.4 8.2 %collective-permute-done.34.refs_2_ = bf16[4,48,1792]{2,1,0:T(8,128)(2,1)S(1)} collective-permute-done((bf16[4,48,1792]{2,1,0:T(8,128)(2,1)S(1)}, bf16[4,48,1792]{2,1,0:T(8,128)(2,1)S(1)}, u32[]{:S(2)}, u32[]{:S(2)}) %collective-permute-start.34) | collective-permute-done | bytes 688160 | tf_op jit(solution)/shard_map/ppermute | solution.py:83
  181.8 9.0 %collective-permute-done.32.refs_1_ = bf16[8,48,896]{2,1,0:T(8,128)(2,1)S(1)} collective-permute-done((bf16[8,48,896]{2,1,0:T(8,128)(2,1)S(1)}, bf16[8,48,896]{2,1,0:T(8,128)(2,1)S(1)}, u32[]{:S(2)}, u32[]{:S(2)}) %collective-permute-start.32) | collective-permute-done | bytes 688160 | tf_op jit(solution)/shard_map/ppermute | solution.py:83
  193.5 3.3 %collective-permute-done.38.refs_3_ = bf16[2,48,1792]{2,1,0:T(8,128)(2,1)S(1)} collective-permute-done((bf16[2,48,1792]{2,1,0:T(8,128)(2,1)S(1)}, bf16[2,48,1792]{2,1,0:T(8,128)(2,1)S(1)}, u32[]{:S(2)}, u32[]{:S(2)}) %collective-permute-start.38) | collective-permute-done | bytes 344096 | tf_op jit(solution)/shard_map/ppermute | solution.py:83
  202.3 3.3 %collective-permute-start.47 = (bf16[1,48,1792]{2,1,0:T(8,128)(2,1)S(1)}, bf16[1,48,1792]{2,1,0:T(8,128)(2,1)S(1)}, u32[]{:S(2)}, u32[]{:S(2)}) collective-permute-start(bf16[1,48,1792]{2,1,0:T(8,128)(2,1)S(1)} %get-tuple-element.345), channel_id=1, source_target_pairs={{0,16},{1,17},{2,18},{3,19},{4,20},{5,21},{6,22},{7,23},{8,24},{9,... | collective-permute-start | bytes 516104 | tf_op jit(solution)/shard_map/ppermute | solution.py:83
  215.2 5.6 %update_feed.1 = (f32[96,768]{1,0:T(8,128)}, f32[96,768]{1,0:T(8,128)}, f32[96,768]{1,0:T(8,128)}, bf16[96,768]{1,0:T(8,128)(2,1)}, f32[96,768]{1,0:T(8,128)}, /...) custom-call(s32[100]{0:T(128)} %concatenate.39.places, ...), custom_call_target="tpu_custom_call" | custom-call | bytes 854016 | tf_op jit(solution)/shard_map/update_feed/pallas_call | solution.py:278
  221.5 3.7 %update_narrow.1 = (f32[3,96,192]{2,1,0:T(8,128)}, f32[3,96,192]{2,1,0:T(8,128)}, f32[3,96,192]{2,1,0:T(8,128)}, bf16[3,96,192]{2,1,0:T(8,128)(2,1)}, f32[192,96...) custom-call(s32[100]{0:T(128)} %concatenate.39.places, ...), custom_call_target="tpu_custom_call" | custom-call | bytes 380612 | tf_op jit(solution)/shard_map/update_narrow/pallas_call | solution.py:278
  (213 shorter events, 85.7 us)
Async XLA Ops:
  2.4 13.8 %collective-permute-start.2 = (bf16[1,96,640]{2,1,0:T(8,128)(2,1)}, bf16[1,96,640]{2,1,0:T(8,128)(2,1)S(1)}, u32[]{:S(2)}, u32[]{:S(2)}) collective-permute-start(bf16[1,96,640]{2,1,0:T(8,128)(2,1)} %bitcast.32), channel_id=1, source_target_pairs={{0,24},{1,25},{2,26},{3,27},{4,28},{5,29},{6,30},{7,31},{8,16},{9,... | collective-permute-start | bytes 368648 | tf_op jit(solution)/shard_map/ppermute | solution.py:83
  24.7 11.4 %collective-permute-start.4 = (bf16[1,96,1024]{2,1,0:T(8,128)(2,1)S(1)}, bf16[1,96,1024]{2,1,0:T(8,128)(2,1)S(1)}, u32[]{:S(2)}, u32[]{:S(2)}) collective-permute-start(bf16[1,96,1024]{2,1,0:T(8,128)(2,1)S(1)} %bitcast.41), channel_id=1, source_target_pairs={{0,8},{1,9},{2,10},{3,11},{4,12},{5,13},{6,14},{7,15},{8,0},{9,1},... | collective-permute-start | bytes 589832 | tf_op jit(solution)/shard_map/ppermute | solution.py:83
  24.7 15.1 %collective-permute-start.3 = (bf16[1,96,1024]{2,1,0:T(8,128)(2,1)S(1)}, bf16[1,96,1024]{2,1,0:T(8,128)(2,1)S(1)}, u32[]{:S(2)}, u32[]{:S(2)}) collective-permute-start(bf16[1,96,1024]{2,1,0:T(8,128)(2,1)S(1)} %bitcast.42), channel_id=1, source_target_pairs={{0,16},{1,17},{2,18},{3,19},{4,20},{5,21},{6,22},{7,23},{8,24},{9,... | collective-permute-start | bytes 589832 | tf_op jit(solution)/shard_map/ppermute | solution.py:83
  27.5 16.2 %collective-permute-start.10 = (bf16[8,48,640]{2,1,0:T(8,128)(2,1)S(1)}, bf16[8,48,640]{2,1,0:T(8,128)(2,1)S(1)}, u32[]{:S(2)}, u32[]{:S(2)}) collective-permute-start(bf16[8,48,640]{2,1,0:T(8,128)(2,1)S(1)} %constant_dynamic-update-slice_fusion.2.h2), channel_id=1, source_target_pairs={{0,4},{1,5},{2,6},{3,7},{4,0},{5,1},{6,2},{7,3},{8,12},{9,13},{10,... | collective-permute-start | bytes 1474568 | tf_op jit(solution)/shard_map/ppermute | solution.py:83
  28.2 15.5 %collective-permute-start.9 = (bf16[8,48,640]{2,1,0:T(8,128)(2,1)S(1)}, bf16[8,48,640]{2,1,0:T(8,128)(2,1)S(1)}, u32[]{:S(2)}, u32[]{:S(2)}) collective-permute-start(bf16[8,48,640]{2,1,0:T(8,128)(2,1)S(1)} %constant_dynamic-update-slice_fusion.h0), channel_id=1, source_target_pairs={{0,2},{1,3},{2,0},{3,1},{4,6},{5,7},{6,4},{7,5},{8,10},{9,11},{10,... | collective-permute-start | bytes 1474568 | tf_op jit(solution)/shard_map/ppermute | solution.py:83
  41.1 25.3 %collective-permute-start.15 = (bf16[1,96,896]{2,1,0:T(8,128)(2,1)S(1)}, bf16[1,96,896]{2,1,0:T(8,128)(2,1)S(1)}, u32[]{:S(2)}, u32[]{:S(2)}) collective-permute-start(bf16[1,96,896]{2,1,0:T(8,128)(2,1)S(1)} %bitcast.44), channel_id=1, source_target_pairs={{0,24},{1,25},{2,26},{3,27},{4,28},{5,29},{6,30},{7,31},{8,16},{9,... | collective-permute-start | bytes 516104 | tf_op jit(solution)/shard_map/ppermute | solution.py:83
  43.7 22.7 %collective-permute-start.14 = (bf16[1,96,896]{2,1,0:T(8,128)(2,1)S(1)}, bf16[1,96,896]{2,1,0:T(8,128)(2,1)S(1)}, u32[]{:S(2)}, u32[]{:S(2)}) collective-permute-start(bf16[1,96,896]{2,1,0:T(8,128)(2,1)S(1)} %bitcast.45), channel_id=1, source_target_pairs={{0,8},{1,9},{2,10},{3,11},{4,12},{5,13},{6,14},{7,15},{8,0},{9,1},... | collective-permute-start | bytes 516104 | tf_op jit(solution)/shard_map/ppermute | solution.py:83
  43.7 22.7 %collective-permute-start.13 = (bf16[1,96,896]{2,1,0:T(8,128)(2,1)S(1)}, bf16[1,96,896]{2,1,0:T(8,128)(2,1)S(1)}, u32[]{:S(2)}, u32[]{:S(2)}) collective-permute-start(bf16[1,96,896]{2,1,0:T(8,128)(2,1)S(1)} %bitcast.46), channel_id=1, source_target_pairs={{0,16},{1,17},{2,18},{3,19},{4,20},{5,21},{6,22},{7,23},{8,24},{9,... | collective-permute-start | bytes 516104 | tf_op jit(solution)/shard_map/ppermute | solution.py:83
  51.2 18.6 %collective-permute-start.17 = (bf16[8,48,1024]{2,1,0:T(8,128)(2,1)S(1)}, bf16[8,48,1024]{2,1,0:T(8,128)(2,1)S(1)}, u32[]{:S(2)}, u32[]{:S(2)}) collective-permute-start(bf16[8,48,1024]{2,1,0:T(8,128)(2,1)S(1)} %constant_dynamic-update-slice_fusion.6.h2), channel_id=1, source_target_pairs={{0,4},{1,5},{2,6},{3,7},{4,0},{5,1},{6,2},{7,3},{8,12},{9,13},{10,... | collective-permute-start | bytes 2359304 | tf_op jit(solution)/shard_map/ppermute | solution.py:83
  52.8 19.2 %collective-permute-start.16 = (bf16[8,48,1024]{2,1,0:T(8,128)(2,1)S(1)}, bf16[8,48,1024]{2,1,0:T(8,128)(2,1)S(1)}, u32[]{:S(2)}, u32[]{:S(2)}) collective-permute-start(bf16[8,48,1024]{2,1,0:T(8,128)(2,1)S(1)} %constant_dynamic-update-slice_fusion.4.h0), channel_id=1, source_target_pairs={{0,2},{1,3},{2,0},{3,1},{4,6},{5,7},{6,4},{7,5},{8,10},{9,11},{10,... | collective-permute-start | bytes 2359304 | tf_op jit(solution)/shard_map/ppermute | solution.py:83
  76.4 14.5 %collective-permute-start.23 = (bf16[8,48,896]{2,1,0:T(8,128)(2,1)S(1)}, bf16[8,48,896]{2,1,0:T(8,128)(2,1)S(1)}, u32[]{:S(2)}, u32[]{:S(2)}) collective-permute-start(bf16[8,48,896]{2,1,0:T(8,128)(2,1)S(1)} %constant_dynamic-update-slice_fusion.10.h2), channel_id=1, source_target_pairs={{0,4},{1,5},{2,6},{3,7},{4,0},{5,1},{6,2},{7,3},{8,12},{9,13},{10,... | collective-permute-start | bytes 2064392 | tf_op jit(solution)/shard_map/ppermute | solution.py:83
  77.6 17.4 %collective-permute-start.22 = (bf16[8,48,896]{2,1,0:T(8,128)(2,1)S(1)}, bf16[8,48,896]{2,1,0:T(8,128)(2,1)S(1)}, u32[]{:S(2)}, u32[]{:S(2)}) collective-permute-start(bf16[8,48,896]{2,1,0:T(8,128)(2,1)S(1)} %constant_dynamic-update-slice_fusion.8.h0), channel_id=1, source_target_pairs={{0,2},{1,3},{2,0},{3,1},{4,6},{5,7},{6,4},{7,5},{8,10},{9,11},{10,... | collective-permute-start | bytes 2064392 | tf_op jit(solution)/shard_map/ppermute | solution.py:83
  124.0 32.5 %collective-permute-start.27 = (bf16[8,48,1792]{2,1,0:T(8,128)(2,1)S(1)}, bf16[8,48,1792]{2,1,0:T(8,128)(2,1)S(1)}, u32[]{:S(2)}, u32[]{:S(2)}) collective-permute-start(bf16[8,48,1792]{2,1,0:T(8,128)(2,1)S(1)} %get-tuple-element.288), channel_id=1, source_target_pairs={{0,4},{1,5},{2,6},{3,7},{4,0},{5,1},{6,2},{7,3},{8,12},{9,13},{10,... | collective-permute-start | bytes 4128776 | tf_op jit(solution)/shard_map/ppermute | solution.py:83
  125.5 32.4 %collective-permute-start.28 = (bf16[8,48,1792]{2,1,0:T(8,128)(2,1)}, bf16[8,48,1792]{2,1,0:T(8,128)(2,1)S(1)}, u32[]{:S(2)}, u32[]{:S(2)}) collective-permute-start(bf16[8,48,1792]{2,1,0:T(8,128)(2,1)} %get-tuple-element.290), channel_id=1, source_target_pairs={{0,8},{1,9},{2,10},{3,11},{4,12},{5,13},{6,14},{7,15},{8,0},{9,1},... | collective-permute-start | bytes 4128776 | tf_op jit(solution)/shard_map/ppermute | solution.py:83
  126.2 25.5 %collective-permute-start.29 = (bf16[512,768]{1,0:T(8,128)(2,1)}, bf16[512,768]{1,0:T(8,128)(2,1)S(1)}, u32[]{:S(2)}, u32[]{:S(2)}) collective-permute-start(bf16[512,768]{1,0:T(8,128)(2,1)} %get-tuple-element.306), channel_id=1, source_target_pairs={{0,2},{1,3},{2,0},{3,1},{4,6},{5,7},{6,4},{7,5},{8,10},{9,11},{10,... | collective-permute-start | bytes 2359304 | tf_op jit(solution)/shard_map/ppermute | solution.py:83
  151.6 15.4 %collective-permute-start.30 = (bf16[512,768]{1,0:T(8,128)(2,1)S(1)}, bf16[512,768]{1,0:T(8,128)(2,1)S(1)}, u32[]{:S(2)}, u32[]{:S(2)}) collective-permute-start(bf16[512,768]{1,0:T(8,128)(2,1)S(1)} %get-tuple-element.322), channel_id=1, source_target_pairs={{0,1},{1,0},{2,3},{3,2},{4,5},{5,4},{6,7},{7,6},{8,9},{9,8},{10,11... | collective-permute-start | bytes 2359304 | tf_op jit(solution)/shard_map/ppermute | solution.py:83
  158.2 18.4 %collective-permute-start.34 = (bf16[4,48,1792]{2,1,0:T(8,128)(2,1)S(1)}, bf16[4,48,1792]{2,1,0:T(8,128)(2,1)S(1)}, u32[]{:S(2)}, u32[]{:S(2)}) collective-permute-start(bf16[4,48,1792]{2,1,0:T(8,128)(2,1)S(1)} %get-tuple-element.311), channel_id=1, source_target_pairs={{0,2},{1,3},{2,0},{3,1},{4,6},{5,7},{6,4},{7,5},{8,10},{9,11},{10,... | collective-permute-start | bytes 2064392 | tf_op jit(solution)/shard_map/ppermute | solution.py:83
  159.8 18.4 %collective-permute-start.35 = (bf16[4,48,1792]{2,1,0:T(8,128)(2,1)S(1)}, bf16[4,48,1792]{2,1,0:T(8,128)(2,1)S(1)}, u32[]{:S(2)}, u32[]{:S(2)}) collective-permute-start(bf16[4,48,1792]{2,1,0:T(8,128)(2,1)S(1)} %get-tuple-element.312), channel_id=1, source_target_pairs={{0,4},{1,5},{2,6},{3,7},{4,0},{5,1},{6,2},{7,3},{8,12},{9,13},{10,... | collective-permute-start | bytes 2064392 | tf_op jit(solution)/shard_map/ppermute | solution.py:83
  164.7 26.1 %collective-permute-start.32 = (bf16[8,48,896]{2,1,0:T(8,128)(2,1)S(1)}, bf16[8,48,896]{2,1,0:T(8,128)(2,1)S(1)}, u32[]{:S(2)}, u32[]{:S(2)}) collective-permute-start(bf16[8,48,896]{2,1,0:T(8,128)(2,1)S(1)} %get-tuple-element.318), channel_id=1, source_target_pairs={{0,4},{1,5},{2,6},{3,7},{4,0},{5,1},{6,2},{7,3},{8,12},{9,13},{10,... | collective-permute-start | bytes 2064392 | tf_op jit(solution)/shard_map/ppermute | solution.py:83
  166.3 25.7 %collective-permute-start.33 = (bf16[8,48,896]{2,1,0:T(8,128)(2,1)S(1)}, bf16[8,48,896]{2,1,0:T(8,128)(2,1)S(1)}, u32[]{:S(2)}, u32[]{:S(2)}) collective-permute-start(bf16[8,48,896]{2,1,0:T(8,128)(2,1)S(1)} %get-tuple-element.320), channel_id=1, source_target_pairs={{0,8},{1,9},{2,10},{3,11},{4,12},{5,13},{6,14},{7,15},{8,0},{9,1},... | collective-permute-start | bytes 2064392 | tf_op jit(solution)/shard_map/ppermute | solution.py:83
  167.9 32.3 %collective-permute-start.31 = (bf16[512,768]{1,0:T(8,128)(2,1)S(1)}, bf16[512,768]{1,0:T(8,128)(2,1)S(1)}, u32[]{:S(2)}, u32[]{:S(2)}) collective-permute-start(bf16[512,768]{1,0:T(8,128)(2,1)S(1)} %finish.1.refs_2_), channel_id=1, source_target_pairs={{0,2},{1,3},{2,0},{3,1},{4,6},{5,7},{6,4},{7,5},{8,10},{9,11},{10,... | collective-permute-start | bytes 2359304 | tf_op jit(solution)/shard_map/ppermute | solution.py:83
  178.4 18.3 %collective-permute-start.38 = (bf16[2,48,1792]{2,1,0:T(8,128)(2,1)S(1)}, bf16[2,48,1792]{2,1,0:T(8,128)(2,1)S(1)}, u32[]{:S(2)}, u32[]{:S(2)}) collective-permute-start(bf16[2,48,1792]{2,1,0:T(8,128)(2,1)S(1)} %get-tuple-element.329), channel_id=1, source_target_pairs={{0,8},{1,9},{2,10},{3,11},{4,12},{5,13},{6,14},{7,15},{8,0},{9,1},... | collective-permute-start | bytes 1032200 | tf_op jit(solution)/shard_map/ppermute | solution.py:83
  179.2 17.5 %collective-permute-start.39 = (bf16[2,48,1792]{2,1,0:T(8,128)(2,1)S(1)}, bf16[2,48,1792]{2,1,0:T(8,128)(2,1)S(1)}, u32[]{:S(2)}, u32[]{:S(2)}) collective-permute-start(bf16[2,48,1792]{2,1,0:T(8,128)(2,1)S(1)} %get-tuple-element.330), channel_id=1, source_target_pairs={{0,16},{1,17},{2,18},{3,19},{4,20},{5,21},{6,22},{7,23},{8,24},{9,... | collective-permute-start | bytes 1032200 | tf_op jit(solution)/shard_map/ppermute | solution.py:83
  202.3 12.2 %collective-permute-start.47 = (bf16[1,48,1792]{2,1,0:T(8,128)(2,1)S(1)}, bf16[1,48,1792]{2,1,0:T(8,128)(2,1)S(1)}, u32[]{:S(2)}, u32[]{:S(2)}) collective-permute-start(bf16[1,48,1792]{2,1,0:T(8,128)(2,1)S(1)} %get-tuple-element.345), channel_id=1, source_target_pairs={{0,16},{1,17},{2,18},{3,19},{4,20},{5,21},{6,22},{7,23},{8,24},{9,... | collective-permute-start | bytes 516104 | tf_op jit(solution)/shard_map/ppermute | solution.py:83
  (64 other events, 852.6 us)

commit v5 on v4

--- a/solution.py
+++ b/solution.py
@@ -314,12 +314,13 @@
             held[target, i * PART_ROWS : (i + 1) * PART_ROWS, :] = source[j % BLOCKS]
 
 
-def scatter_blocks(places, held, halves, route=ACROSS):
+def scatter_blocks(places, held, halves, route=ACROSS, at=0):
     for i in range(2):
         for j in range(2 * BLOCKS):
             target = halves[2 * i + j // BLOCKS]
             source = places[1 + 2 * BLOCKS * (2 * ROUTES.index(route) + i) + j]
-            target[j % BLOCKS] = held[source, i * PART_ROWS : (i + 1) * PART_ROWS, :]
+            block = held[source, i * PART_ROWS : (i + 1) * PART_ROWS, :]
+            target[j % BLOCKS, :, at : at + held.shape[2]] = block
 
 
 CORE_AT = 1 + 4 * BLOCKS * len(ROUTES)
@@ -439,7 +440,7 @@
 
 
 def project(places, tokens, bias, bias_other, halves):
-    step = 256
+    step = 512
     args = (tokens, bias, bias_other, *halves)
     return call(
         project_kernel,
@@ -557,7 +558,7 @@
 
 
 def up_kernel(
-    places, x, z0, z1, zp0, zp1, vec, bias_mine, bias_other, w, m, slope, n1, rs1, low, bias
+    places, x, z0, z1, zp0, zp1, vec, bias_mine, bias_other, w, m, slope, n1, rs1, low_t, bias
 ):
     @pl.when(pl.program_id(0) == 0)
     def _():
@@ -573,7 +574,7 @@
     n1[...] = normed
     rs1[...] = jnp.broadcast_to(spread, rs1.shape)
     middle = (normed * vec[0:1, :] + vec[1:2, :]).astype(LOW)
-    low[...] = middle
+    low_t[...] = middle.T
     for c in range(4):
         at = pl.ds(c * 384, 384)
         u = dot(middle, w[:, at]) + bias[0:1, at]
@@ -596,9 +597,10 @@
         ]
         + [whole(a) for a in args[5:]],
         [rows(step, 2 * D)] * 2
-        + [rows(step, D), rows(step, 128), rows(step, D)],
+        + [rows(step, D), rows(step, 128)]
+        + [pl.BlockSpec((D, step), lambda i, *_: (0, i))],
         [shape((LEN, 2 * D), LOW)] * 2
-        + [shape((LEN, D), WIDE), shape((LEN, 128), WIDE), shape((LEN, D), LOW)],
+        + [shape((LEN, D), WIDE), shape((LEN, 128), WIDE), shape((D, LEN), LOW)],
         [pltpu.VMEM((1, 2 * D), WIDE)],
         places,
         args,
@@ -778,17 +780,18 @@
     )
 
 
-def feed_grad_kernel(places, dh2, m, middle, du, ramp, h0, h1, h2, h3, held, turned):
-    for at, left, right in ((0, dh2, m), (D, middle, du)):
-        turned[...] = left[...].T
+def feed_grad_kernel(places, dh2, m, middle_t, du, ramp, h0, h1, h2, h3, held, turned):
+    turned[...] = dh2[...].T
+    for at, left, right in ((0, turned, m), (D, middle_t, du)):
         for side in range(2):
             for c in range(0, D, 256):
-                part = dot(turned[...], right[:, D * side + c : D * side + c + 256]).astype(LOW)
-                held[side * BLOCKS : (side + 1) * BLOCKS, :, at + c : at + c + 256] = part.reshape(
+                part = dot(left[...], right[:, D * side + c : D * side + c + 256]).astype(LOW)
+                held[side * BLOCKS : (side + 1) * BLOCKS, :, c : c + 256] = part.reshape(
                     BLOCKS, BLOCK_ROWS, 256
                 )
+        scatter_blocks(places, held, (h0, h1, h2, h3), ALONG, at)
     row = lax.broadcasted_iota(jnp.int32, (BLOCK_ROWS, 256), 0)
-    for group in range((held.shape[2] - 2 * D) // 256):
+    for group in range((h0.shape[2] - 2 * D) // 256):
         slot = places[SLOT_AT] - 16 * group
         block = jnp.zeros((BLOCK_ROWS, 256), WIDE)
         for i in range(6):
@@ -797,13 +800,14 @@
             block = jnp.where(mine, values, block)
         block = block.astype(LOW)
         at = 2 * D + 256 * group
-        for p in range(2 * BLOCKS):
-            held[p, :, at : at + 256] = block
-    scatter_blocks(places, held, (h0, h1, h2, h3), ALONG)
-
-
-def feed_grad(places, slots, dh2, m, middle, du, ramp):
-    args = (dh2, m, middle, du, ramp)
+        for i, half in enumerate((h0, h1, h2, h3)):
+            first = PART_ROWS * (i // 2)
+            for p in range(BLOCKS):
+                half[p, :, at : at + 256] = block[first : first + PART_ROWS, :]
+
+
+def feed_grad(places, slots, dh2, m, middle_t, du, ramp):
+    args = (dh2, m, middle_t, du, ramp)
     width = 2 * D + 16 * slots
     return call(
         feed_grad_kernel,
@@ -812,11 +816,11 @@
         [whole(a) for a in args],
         half_specs(width),
         half_shapes(width),
-        [held_blocks(width), pltpu.VMEM((D, LEN), LOW)],
+        [held_blocks(D), pltpu.VMEM((D, LEN), LOW)],
         places,
         args,
         4 * LEN * D * 2 * D,
-        vmem=12 if slots == 16 else 56,
+        vmem=9 if slots == 16 else 48,
     )
 
 
@@ -842,7 +846,7 @@
 
 
 def mid(places, dh2, dx, dxp, n1, rs1, vec, w_out, turn_sums, up_sums):
-    step = 256
+    step = 512
     args = (dh2, dx, dxp, n1, rs1, vec, w_out, turn_sums, up_sums)
     count = 16
     return call(
@@ -1229,7 +1233,7 @@
     zp = [links.swap(part, CORE) for part in z]
     sent = down_spread.step(w_up)
     z = after(z, *sent)
-    m, slope, n1, rs1, middle_low = feed_up(
+    m, slope, n1, rs1, middle_t = feed_up(
         places, tokens, z, zp, layer_vectors, biases, other_biases, w_up
     )
     f, w_down, pool_mine = feed_down(places, m, pool_part, down_spread.halves())
@@ -1245,7 +1249,7 @@
     dxp = links.swap(dx, CORE)
     m, dh2_low = after((m, dh2_low), dx)
     slots = 2 * dp_count
-    feed_halves = feed_grad(places, slots, dh2_low, m, middle_low, du, ramp)
+    feed_halves = feed_grad(places, slots, dh2_low, m, middle_t, du, ramp)
     feed_fold = links.fold(feed_halves, ALONG, 2 * D)
     feed_fold.step()
     dx = after(dx, *feed_halves)

time: 227 us -> 228 us (level)
    unnamed x85 -> x95, local copies, waits for them, and re-layouts: 4.23 us -> 5.67 us
where the time goes in v5:
time: 228 us; the launch traced here: 224 us
  Pallas kernels  98 us (43%)
  waiting for transfers between devices  63.3 us (28%)
  starting transfers between devices  52.5 us (23%)
  local copies, waits for them, and re-layouts  7.71 us (3%)
    pallas_call x18, Pallas kernels, call(): pl.pallas_call(kernel, out_shape=out_shape, grid_spec=pltpu.PrefetchScala...  95.1 us
    ppermute x49, waiting for transfers between devices, swap(): return lax.ppermute(value, ('dp', 'mp'), pairs)  63.3 us
    ppermute x49, starting transfers between devices, swap(): return lax.ppermute(value, ('dp', 'mp'), pairs)  52.5 us
    unnamed x95, local copies, waits for them, and re-layouts  5.67 us
  transfers between devices with their start and end apart: 49, of which 25 were waited for; matrix products, arithmetic and copies ran while one was open for 1% of the time, Pallas kernels for 34%

profile of v5, /device:TPU:0, one launch (start us, length us, event | category | flops | bytes accessed | tf_op | source)
XLA Modules:
  0.0 224.3 jit_solution(12890168247426620270)
XLA Ops:
  2.4 5.0 %collective-permute-start.2 = (bf16[1,96,640]{2,1,0:T(8,128)(2,1)}, bf16[1,96,640]{2,1,0:T(8,128)(2,1)S(1)}, u32[]{:S(2)}, u32[]{:S(2)}) collective-permute-start(bf16[1,96,640]{2,1,0:T(8,128)(2,1)} %bitcast.32), channel_id=1, source_target_pairs={{0,24},{1,25},{2,26},{3,27},{4,28},{5,29},{6,30},{7,31},{8,16},{9,... | collective-permute-start | bytes 368648 | tf_op jit(solution)/shard_map/ppermute | solution.py:83
  9.3 2.8 %pack.1 = (bf16[96,1024]{1,0:T(8,128)(2,1)}, bf16[96,896]{1,0:T(8,128)(2,1)}, f32[8,768]{1,0:T(8,128)}) custom-call(s32[100]{0:T(128)} %concatenate.39.places, f32[96,768]{1,0:T(8,128)} %refs_13_.2, f32[192,96]{1,0:T(8,128)} %refs_13_.3, f32[96,768]{1,0:T(8,128)} %bitcast.30, f32[96,768]{1,0:T(8,128)} %refs_16_.2, f32[2,192]{1,0:T(2,128)} %refs_16_.3, ...), custom_call_target="tpu_custom_call" | custom-call | bytes 84768 | tf_op jit(solution)/shard_map/pack/pallas_call | solution.py:278
  31.8 4.2 %collective-permute-done.4 = bf16[1,96,1024]{2,1,0:T(8,128)(2,1)S(1)} collective-permute-done((bf16[1,96,1024]{2,1,0:T(8,128)(2,1)S(1)}, bf16[1,96,1024]{2,1,0:T(8,128)(2,1)S(1)}, u32[]{:S(2)}, u32[]{:S(2)}) %collective-permute-start.4) | collective-permute-done | bytes 196640 | tf_op jit(solution)/shard_map/ppermute | solution.py:83
  36.1 3.7 %collective-permute-done.3 = bf16[1,96,1024]{2,1,0:T(8,128)(2,1)S(1)} collective-permute-done((bf16[1,96,1024]{2,1,0:T(8,128)(2,1)S(1)}, bf16[1,96,1024]{2,1,0:T(8,128)(2,1)S(1)}, u32[]{:S(2)}, u32[]{:S(2)}) %collective-permute-start.3) | collective-permute-done | bytes 196640 | tf_op jit(solution)/shard_map/ppermute | solution.py:83
  45.5 4.4 %project.1 = (bf16[1024,384]{1,0:T(8,128)(2,1)S(1)}, bf16[1024,384]{1,0:T(8,128)(2,1)S(1)}, bf16[1024,384]{1,0:T(8,128)(2,1)S(1)}, bf16[3,768,384]{2,1,0:T(8,128)(2,1)S(1)}, f32[8,128]{1,0:T(8,128)S(1)}) custom-call(s32[100]{0:T(128)S(1)} %copy-done.31, bf16[2048,768]{1,0:T(8,128)(2,1)S(1)} %copy-done, f32[8,768]{1,0:T(8,128)S(1)} %copy-done.33, ...), custom_call_target="tpu_custom_call" | custom-call | flops 113246208 | bytes 580864 | tf_op jit(solution)/shard_map/project/pallas_call | solution.py:278
  54.5 11.8 %attend_forward.1 = (bf16[1024,384]{1,0:T(8,128)(2,1)S(1)}, f32[1024,384]{1,0:T(8,128)S(1)}, bf16[6,1024,1024]{2,1,0:T(8,128)(2,1)S(1)}) custom-call(s32[100]{0:T(128)S(1)} %copy-done.31, bf16[1024,384]{1,0:T(8,128)(2,1)S(1)} %get-tuple-element.253.q_ref, bf16[1024,384]{1,0:T(8,128)(2,1)S(1)} %get-tuple-element.254.k_ref, ...), custom_call_target="tpu_custom_call" | custom-call | flops 402653184 | bytes 1081344 | tf_op jit(solution)/shard_map/attend_forward/pallas_call | solution.py:278
  80.5 8.1 %feed_up.1 = (bf16[1024,1536]{1,0:T(8,128)(2,1)S(1)}, bf16[1024,1536]{1,0:T(8,128)(2,1)S(1)}, f32[1024,768]{1,0:T(8,128)S(1)}, f32[1024,128]{1,0:T(8,128)S(1)}, bf16[768,1024]{1,0:T(8,128)(2,1)S(1)}) custom-call(s32[100]{0:T(128)S(1)} %copy-done.31, bf16[2048,768]{1,0:T(8,128)(2,1)S(1)} %copy-done, bf16[512,768]{1,0:T(8,128)(2,1)S(1)} %get-tuple-element.269.z0, ...), custom_call_target="tpu_custom_call" | custom-call | flops 150994944 | bytes 1265984 | tf_op jit(solution)/shard_map/feed_up/pallas_call | solution.py:278
  90.9 4.1 %collective-permute-done.22.h1 = bf16[8,48,896]{2,1,0:T(8,128)(2,1)S(1)} collective-permute-done((bf16[8,48,896]{2,1,0:T(8,128)(2,1)S(1)}, bf16[8,48,896]{2,1,0:T(8,128)(2,1)S(1)}, u32[]{:S(2)}, u32[]{:S(2)}) %collective-permute-start.22) | collective-permute-done | bytes 688160 | tf_op jit(solution)/shard_map/ppermute | solution.py:83
  95.0 3.8 %feed_down.1 = (bf16[1024,768]{1,0:T(8,128)(2,1)S(1)}, bf16[768,1536]{1,0:T(8,128)(2,1)S(1)}, bf16[768,384]{1,0:T(8,128)(2,1)S(1)}) custom-call(s32[100]{0:T(128)S(1)} %copy-done.31, bf16[1024,1536]{1,0:T(8,128)(2,1)S(1)} %get-tuple-element.283.m, bf16[768,128]{1,0:T(8,128)(2,1)S(1)} %get-tuple-element.273.pool_part, ...), custom_call_target="tpu_custom_call" | custom-call | flops 150994944 | bytes 663552 | tf_op jit(solution)/shard_map/feed_down/pallas_call | solution.py:278
  99.5 3.7 %collective-permute-done.25.pool_b = bf16[768,384]{1,0:T(8,128)(2,1)S(1)} collective-permute-done((bf16[768,384]{1,0:T(8,128)(2,1)S(1)}, bf16[768,384]{1,0:T(8,128)(2,1)S(1)}, u32[]{:S(2)}, u32[]{:S(2)}) %collective-permute-start.25) | collective-permute-done | bytes 589856 | tf_op jit(solution)/shard_map/ppermute | solution.py:83
  103.2 6.6 %turn.1 = (bf16[2048,768]{1,0:T(8,128)(2,1)}, bf16[512,768]{1,0:T(8,128)(2,1)}, bf16[1024,768]{1,0:T(8,128)(2,1)S(1)}, f32[8,768]{1,0:T(8,128)S(1)}, f32[8,768]{1,0:T(8,128)S(1)}) custom-call(s32[100]{0:T(128)S(1)} %copy-done.31, s32[2]{0:T(128)S(1)} %copy-done.35, s32[2]{0:T(128)S(1)} %copy-done.36, f32[1024,768]{1,0:T(8,128)S(1)} %get-tuple-element.271.n1, ...), custom_call_target="tpu_custom_call" | custom-call | flops 2949120 | bytes 1024609 | tf_op jit(solution)/shard_map/turn/pallas_call | solution.py:278
  109.9 6.7 %feed_back.1 = (bf16[1024,1536]{1,0:T(8,128)(2,1)S(1)}, bf16[1024,768]{1,0:T(8,128)(2,1)S(1)}, f32[8,1536]{1,0:T(8,128)S(1)}) custom-call(s32[100]{0:T(128)S(1)} %copy-done.31, bf16[1024,768]{1,0:T(8,128)(2,1)S(1)} %get-tuple-element.282.dh2, bf16[1024,1536]{1,0:T(8,128)(2,1)S(1)} %get-tuple-element.279.slope, ...), custom_call_target="tpu_custom_call" | custom-call | flops 301989888 | bytes 887808 | tf_op jit(solution)/shard_map/feed_back/pallas_call | solution.py:278
  116.7 6.2 %feed_grad.1 = (bf16[8,48,1792]{2,1,0:T(8,128)(2,1)S(1)}, bf16[8,48,1792]{2,1,0:T(8,128)(2,1)S(1)}, bf16[8,48,1792]{2,1,0:T(8,128)(2,1)S(1)}, bf16[8,48,1792]{2,1,0:T(8,128)(2,1)S(1)}) custom-call(s32[100]{0:T(128)S(1)} %copy-done.31, bf16[1024,768]{1,0:T(8,128)(2,1)S(1)} %get-tuple-element.282.dh2, bf16[1024,1536]{1,0:T(8,128)(2,1)S(1)} %get-tuple-element.283.m, ...), custom_call_target="tpu_custom_call" | custom-call | flops 301989888 | bytes 935424 | tf_op jit(solution)/shard_map/feed_grad/pallas_call | solution.py:278
  128.2 3.7 %middle_back.1 = (f32[1024,768]{1,0:T(8,128)S(1)}, bf16[1024,768]{1,0:T(8,128)(2,1)S(1)}, bf16[1024,384]{1,0:T(8,128)(2,1)S(1)}, f32[16,768]{1,0:T(8,128)S(1)}) custom-call(s32[100]{0:T(128)S(1)} %copy-done.31, bf16[1024,768]{1,0:T(8,128)(2,1)S(1)} %get-tuple-element.282.dh2, bf16[1024,768]{1,0:T(8,128)(2,1)S(1)} %copy-done.19, ...), custom_call_target="tpu_custom_call" | custom-call | flops 37748736 | bytes 914240 | tf_op jit(solution)/shard_map/middle_back/pallas_call | solution.py:278
  131.9 16.2 %attend_backward.1 = (bf16[1024,384]{1,0:T(8,128)(2,1)S(1)}, bf16[1024,384]{1,0:T(8,128)(2,1)S(1)}, bf16[1024,384]{1,0:T(8,128)(2,1)S(1)}) custom-call(s32[100]{0:T(128)S(1)} %copy-done.31, bf16[1024,384]{1,0:T(8,128)(2,1)S(1)} %get-tuple-element.253.q_ref, bf16[1024,384]{1,0:T(8,128)(2,1)S(1)} %get-tuple-element.254.k_ref, ...), custom_call_target="tpu_custom_call" | custom-call | flops 805306368 | bytes 1228800 | tf_op jit(solution)/shard_map/attend_backward/pallas_call | solution.py:278
  148.1 3.5 %input_grad.1 = (bf16[512,768]{1,0:T(8,128)(2,1)S(1)}, bf16[512,768]{1,0:T(8,128)(2,1)S(1)}) custom-call(s32[100]{0:T(128)S(1)} %copy-done.31, bf16[1024,384]{1,0:T(8,128)(2,1)S(1)} %get-tuple-element.313.refs_0_.dq, bf16[1024,384]{1,0:T(8,128)(2,1)S(1)} %get-tuple-element.314.refs_1_.dk, bf16[1024,384]{1,0:T(8,128)(2,1)S(1)} %get-tuple-element.315.refs_2_.dv, ...), custom_call_target="tpu_custom_call" | custom-call | flops 113246208 | bytes 356352 | tf_op jit(solution)/shard_map/input_grad/pallas_call | solution.py:278
  151.7 3.8 %collective-permute-done.27.refs_1_ = bf16[8,48,1792]{2,1,0:T(8,128)(2,1)S(1)} collective-permute-done((bf16[8,48,1792]{2,1,0:T(8,128)(2,1)S(1)}, bf16[8,48,1792]{2,1,0:T(8,128)(2,1)S(1)}, u32[]{:S(2)}, u32[]{:S(2)}) %collective-permute-start.27) | collective-permute-done | bytes 1376288 | tf_op jit(solution)/shard_map/ppermute | solution.py:83
  159.1 4.4 %narrow_grad.1 = (bf16[8,48,896]{2,1,0:T(8,128)(2,1)S(1)}, bf16[8,48,896]{2,1,0:T(8,128)(2,1)S(1)}, bf16[8,48,896]{2,1,0:T(8,128)(2,1)S(1)}, bf16[8,48,896]{2,1,0:T(8,128)(2,1)S(1)}) custom-call(s32[100]{0:T(128)S(1)} %copy-done.32, bf16[2048,768]{1,0:T(8,128)(2,1)S(1)} %copy-done, bf16[1024,768]{1,0:T(8,128)(2,1)S(1)} %get-tuple-element.305.dh1, ...), custom_call_target="tpu_custom_call" | custom-call | flops 150994944 | bytes 666624 | tf_op jit(solution)/shard_map/narrow_grad/pallas_call | solution.py:278
  167.5 8.0 %collective-permute-done.34.refs_2_ = bf16[4,48,1792]{2,1,0:T(8,128)(2,1)S(1)} collective-permute-done((bf16[4,48,1792]{2,1,0:T(8,128)(2,1)S(1)}, bf16[4,48,1792]{2,1,0:T(8,128)(2,1)S(1)}, u32[]{:S(2)}, u32[]{:S(2)}) %collective-permute-start.34) | collective-permute-done | bytes 688160 | tf_op jit(solution)/shard_map/ppermute | solution.py:83
  180.7 9.0 %collective-permute-done.32.refs_1_ = bf16[8,48,896]{2,1,0:T(8,128)(2,1)S(1)} collective-permute-done((bf16[8,48,896]{2,1,0:T(8,128)(2,1)S(1)}, bf16[8,48,896]{2,1,0:T(8,128)(2,1)S(1)}, u32[]{:S(2)}, u32[]{:S(2)}) %collective-permute-start.32) | collective-permute-done | bytes 688160 | tf_op jit(solution)/shard_map/ppermute | solution.py:83
  192.1 3.5 %collective-permute-done.38.refs_3_ = bf16[2,48,1792]{2,1,0:T(8,128)(2,1)S(1)} collective-permute-done((bf16[2,48,1792]{2,1,0:T(8,128)(2,1)S(1)}, bf16[2,48,1792]{2,1,0:T(8,128)(2,1)S(1)}, u32[]{:S(2)}, u32[]{:S(2)}) %collective-permute-start.38) | collective-permute-done | bytes 344096 | tf_op jit(solution)/shard_map/ppermute | solution.py:83
  201.1 3.3 %collective-permute-start.47 = (bf16[1,48,1792]{2,1,0:T(8,128)(2,1)S(1)}, bf16[1,48,1792]{2,1,0:T(8,128)(2,1)S(1)}, u32[]{:S(2)}, u32[]{:S(2)}) collective-permute-start(bf16[1,48,1792]{2,1,0:T(8,128)(2,1)S(1)} %get-tuple-element.345), channel_id=1, source_target_pairs={{0,16},{1,17},{2,18},{3,19},{4,20},{5,21},{6,22},{7,23},{8,24},{9,... | collective-permute-start | bytes 516104 | tf_op jit(solution)/shard_map/ppermute | solution.py:83
  214.1 5.6 %update_feed.1 = (f32[96,768]{1,0:T(8,128)}, f32[96,768]{1,0:T(8,128)}, f32[96,768]{1,0:T(8,128)}, bf16[96,768]{1,0:T(8,128)(2,1)}, f32[96,768]{1,0:T(8,128)}, /...) custom-call(s32[100]{0:T(128)} %concatenate.39.places, ...), custom_call_target="tpu_custom_call" | custom-call | bytes 854016 | tf_op jit(solution)/shard_map/update_feed/pallas_call | solution.py:278
  220.3 3.7 %update_narrow.1 = (f32[3,96,192]{2,1,0:T(8,128)}, f32[3,96,192]{2,1,0:T(8,128)}, f32[3,96,192]{2,1,0:T(8,128)}, bf16[3,96,192]{2,1,0:T(8,128)(2,1)}, f32[192,96...) custom-call(s32[100]{0:T(128)} %concatenate.39.places, ...), custom_call_target="tpu_custom_call" | custom-call | bytes 380612 | tf_op jit(solution)/shard_map/update_narrow/pallas_call | solution.py:278
  (223 shorter events, 86.6 us)
Async XLA Ops:
  2.4 13.7 %collective-permute-start.2 = (bf16[1,96,640]{2,1,0:T(8,128)(2,1)}, bf16[1,96,640]{2,1,0:T(8,128)(2,1)S(1)}, u32[]{:S(2)}, u32[]{:S(2)}) collective-permute-start(bf16[1,96,640]{2,1,0:T(8,128)(2,1)} %bitcast.32), channel_id=1, source_target_pairs={{0,24},{1,25},{2,26},{3,27},{4,28},{5,29},{6,30},{7,31},{8,16},{9,... | collective-permute-start | bytes 368648 | tf_op jit(solution)/shard_map/ppermute | solution.py:83
  24.7 11.4 %collective-permute-start.4 = (bf16[1,96,1024]{2,1,0:T(8,128)(2,1)S(1)}, bf16[1,96,1024]{2,1,0:T(8,128)(2,1)S(1)}, u32[]{:S(2)}, u32[]{:S(2)}) collective-permute-start(bf16[1,96,1024]{2,1,0:T(8,128)(2,1)S(1)} %bitcast.41), channel_id=1, source_target_pairs={{0,8},{1,9},{2,10},{3,11},{4,12},{5,13},{6,14},{7,15},{8,0},{9,1},... | collective-permute-start | bytes 589832 | tf_op jit(solution)/shard_map/ppermute | solution.py:83
  24.7 15.1 %collective-permute-start.3 = (bf16[1,96,1024]{2,1,0:T(8,128)(2,1)S(1)}, bf16[1,96,1024]{2,1,0:T(8,128)(2,1)S(1)}, u32[]{:S(2)}, u32[]{:S(2)}) collective-permute-start(bf16[1,96,1024]{2,1,0:T(8,128)(2,1)S(1)} %bitcast.42), channel_id=1, source_target_pairs={{0,16},{1,17},{2,18},{3,19},{4,20},{5,21},{6,22},{7,23},{8,24},{9,... | collective-permute-start | bytes 589832 | tf_op jit(solution)/shard_map/ppermute | solution.py:83
  27.5 16.2 %collective-permute-start.10 = (bf16[8,48,640]{2,1,0:T(8,128)(2,1)S(1)}, bf16[8,48,640]{2,1,0:T(8,128)(2,1)S(1)}, u32[]{:S(2)}, u32[]{:S(2)}) collective-permute-start(bf16[8,48,640]{2,1,0:T(8,128)(2,1)S(1)} %constant_dynamic-update-slice_fusion.2.h2), channel_id=1, source_target_pairs={{0,4},{1,5},{2,6},{3,7},{4,0},{5,1},{6,2},{7,3},{8,12},{9,13},{10,... | collective-permute-start | bytes 1474568 | tf_op jit(solution)/shard_map/ppermute | solution.py:83
  28.2 15.5 %collective-permute-start.9 = (bf16[8,48,640]{2,1,0:T(8,128)(2,1)S(1)}, bf16[8,48,640]{2,1,0:T(8,128)(2,1)S(1)}, u32[]{:S(2)}, u32[]{:S(2)}) collective-permute-start(bf16[8,48,640]{2,1,0:T(8,128)(2,1)S(1)} %constant_dynamic-update-slice_fusion.h0), channel_id=1, source_target_pairs={{0,2},{1,3},{2,0},{3,1},{4,6},{5,7},{6,4},{7,5},{8,10},{9,11},{10,... | collective-permute-start | bytes 1474568 | tf_op jit(solution)/shard_map/ppermute | solution.py:83
  41.1 25.3 %collective-permute-start.15 = (bf16[1,96,896]{2,1,0:T(8,128)(2,1)S(1)}, bf16[1,96,896]{2,1,0:T(8,128)(2,1)S(1)}, u32[]{:S(2)}, u32[]{:S(2)}) collective-permute-start(bf16[1,96,896]{2,1,0:T(8,128)(2,1)S(1)} %bitcast.44), channel_id=1, source_target_pairs={{0,24},{1,25},{2,26},{3,27},{4,28},{5,29},{6,30},{7,31},{8,16},{9,... | collective-permute-start | bytes 516104 | tf_op jit(solution)/shard_map/ppermute | solution.py:83
  43.7 22.7 %collective-permute-start.14 = (bf16[1,96,896]{2,1,0:T(8,128)(2,1)S(1)}, bf16[1,96,896]{2,1,0:T(8,128)(2,1)S(1)}, u32[]{:S(2)}, u32[]{:S(2)}) collective-permute-start(bf16[1,96,896]{2,1,0:T(8,128)(2,1)S(1)} %bitcast.45), channel_id=1, source_target_pairs={{0,8},{1,9},{2,10},{3,11},{4,12},{5,13},{6,14},{7,15},{8,0},{9,1},... | collective-permute-start | bytes 516104 | tf_op jit(solution)/shard_map/ppermute | solution.py:83
  43.7 22.7 %collective-permute-start.13 = (bf16[1,96,896]{2,1,0:T(8,128)(2,1)S(1)}, bf16[1,96,896]{2,1,0:T(8,128)(2,1)S(1)}, u32[]{:S(2)}, u32[]{:S(2)}) collective-permute-start(bf16[1,96,896]{2,1,0:T(8,128)(2,1)S(1)} %bitcast.46), channel_id=1, source_target_pairs={{0,16},{1,17},{2,18},{3,19},{4,20},{5,21},{6,22},{7,23},{8,24},{9,... | collective-permute-start | bytes 516104 | tf_op jit(solution)/shard_map/ppermute | solution.py:83
  51.2 18.6 %collective-permute-start.17 = (bf16[8,48,1024]{2,1,0:T(8,128)(2,1)S(1)}, bf16[8,48,1024]{2,1,0:T(8,128)(2,1)S(1)}, u32[]{:S(2)}, u32[]{:S(2)}) collective-permute-start(bf16[8,48,1024]{2,1,0:T(8,128)(2,1)S(1)} %constant_dynamic-update-slice_fusion.6.h2), channel_id=1, source_target_pairs={{0,4},{1,5},{2,6},{3,7},{4,0},{5,1},{6,2},{7,3},{8,12},{9,13},{10,... | collective-permute-start | bytes 2359304 | tf_op jit(solution)/shard_map/ppermute | solution.py:83
  52.8 19.2 %collective-permute-start.16 = (bf16[8,48,1024]{2,1,0:T(8,128)(2,1)S(1)}, bf16[8,48,1024]{2,1,0:T(8,128)(2,1)S(1)}, u32[]{:S(2)}, u32[]{:S(2)}) collective-permute-start(bf16[8,48,1024]{2,1,0:T(8,128)(2,1)S(1)} %constant_dynamic-update-slice_fusion.4.h0), channel_id=1, source_target_pairs={{0,2},{1,3},{2,0},{3,1},{4,6},{5,7},{6,4},{7,5},{8,10},{9,11},{10,... | collective-permute-start | bytes 2359304 | tf_op jit(solution)/shard_map/ppermute | solution.py:83
  76.5 14.5 %collective-permute-start.23 = (bf16[8,48,896]{2,1,0:T(8,128)(2,1)S(1)}, bf16[8,48,896]{2,1,0:T(8,128)(2,1)S(1)}, u32[]{:S(2)}, u32[]{:S(2)}) collective-permute-start(bf16[8,48,896]{2,1,0:T(8,128)(2,1)S(1)} %constant_dynamic-update-slice_fusion.10.h2), channel_id=1, source_target_pairs={{0,4},{1,5},{2,6},{3,7},{4,0},{5,1},{6,2},{7,3},{8,12},{9,13},{10,... | collective-permute-start | bytes 2064392 | tf_op jit(solution)/shard_map/ppermute | solution.py:83
  77.6 17.4 %collective-permute-start.22 = (bf16[8,48,896]{2,1,0:T(8,128)(2,1)S(1)}, bf16[8,48,896]{2,1,0:T(8,128)(2,1)S(1)}, u32[]{:S(2)}, u32[]{:S(2)}) collective-permute-start(bf16[8,48,896]{2,1,0:T(8,128)(2,1)S(1)} %constant_dynamic-update-slice_fusion.8.h0), channel_id=1, source_target_pairs={{0,2},{1,3},{2,0},{3,1},{4,6},{5,7},{6,4},{7,5},{8,10},{9,11},{10,... | collective-permute-start | bytes 2064392 | tf_op jit(solution)/shard_map/ppermute | solution.py:83
  122.9 32.5 %collective-permute-start.27 = (bf16[8,48,1792]{2,1,0:T(8,128)(2,1)S(1)}, bf16[8,48,1792]{2,1,0:T(8,128)(2,1)S(1)}, u32[]{:S(2)}, u32[]{:S(2)}) collective-permute-start(bf16[8,48,1792]{2,1,0:T(8,128)(2,1)S(1)} %get-tuple-element.288), channel_id=1, source_target_pairs={{0,4},{1,5},{2,6},{3,7},{4,0},{5,1},{6,2},{7,3},{8,12},{9,13},{10,... | collective-permute-start | bytes 4128776 | tf_op jit(solution)/shard_map/ppermute | solution.py:83
  124.5 32.2 %collective-permute-start.28 = (bf16[8,48,1792]{2,1,0:T(8,128)(2,1)S(1)}, bf16[8,48,1792]{2,1,0:T(8,128)(2,1)S(1)}, u32[]{:S(2)}, u32[]{:S(2)}) collective-permute-start(bf16[8,48,1792]{2,1,0:T(8,128)(2,1)S(1)} %get-tuple-element.290), channel_id=1, source_target_pairs={{0,8},{1,9},{2,10},{3,11},{4,12},{5,13},{6,14},{7,15},{8,0},{9,1},... | collective-permute-start | bytes 4128776 | tf_op jit(solution)/shard_map/ppermute | solution.py:83
  125.2 26.5 %collective-permute-start.29 = (bf16[512,768]{1,0:T(8,128)(2,1)}, bf16[512,768]{1,0:T(8,128)(2,1)S(1)}, u32[]{:S(2)}, u32[]{:S(2)}) collective-permute-start(bf16[512,768]{1,0:T(8,128)(2,1)} %get-tuple-element.306), channel_id=1, source_target_pairs={{0,2},{1,3},{2,0},{3,1},{4,6},{5,7},{6,4},{7,5},{8,10},{9,11},{10,... | collective-permute-start | bytes 2359304 | tf_op jit(solution)/shard_map/ppermute | solution.py:83
  151.6 14.2 %collective-permute-start.30 = (bf16[512,768]{1,0:T(8,128)(2,1)S(1)}, bf16[512,768]{1,0:T(8,128)(2,1)S(1)}, u32[]{:S(2)}, u32[]{:S(2)}) collective-permute-start(bf16[512,768]{1,0:T(8,128)(2,1)S(1)} %get-tuple-element.322), channel_id=1, source_target_pairs={{0,1},{1,0},{2,3},{3,2},{4,5},{5,4},{6,7},{7,6},{8,9},{9,8},{10,11... | collective-permute-start | bytes 2359304 | tf_op jit(solution)/shard_map/ppermute | solution.py:83
  157.0 18.4 %collective-permute-start.34 = (bf16[4,48,1792]{2,1,0:T(8,128)(2,1)S(1)}, bf16[4,48,1792]{2,1,0:T(8,128)(2,1)S(1)}, u32[]{:S(2)}, u32[]{:S(2)}) collective-permute-start(bf16[4,48,1792]{2,1,0:T(8,128)(2,1)S(1)} %get-tuple-element.311), channel_id=1, source_target_pairs={{0,2},{1,3},{2,0},{3,1},{4,6},{5,7},{6,4},{7,5},{8,10},{9,11},{10,... | collective-permute-start | bytes 2064392 | tf_op jit(solution)/shard_map/ppermute | solution.py:83
  158.6 18.4 %collective-permute-start.35 = (bf16[4,48,1792]{2,1,0:T(8,128)(2,1)S(1)}, bf16[4,48,1792]{2,1,0:T(8,128)(2,1)S(1)}, u32[]{:S(2)}, u32[]{:S(2)}) collective-permute-start(bf16[4,48,1792]{2,1,0:T(8,128)(2,1)S(1)} %get-tuple-element.312), channel_id=1, source_target_pairs={{0,4},{1,5},{2,6},{3,7},{4,0},{5,1},{6,2},{7,3},{8,12},{9,13},{10,... | collective-permute-start | bytes 2064392 | tf_op jit(solution)/shard_map/ppermute | solution.py:83
  163.5 26.1 %collective-permute-start.32 = (bf16[8,48,896]{2,1,0:T(8,128)(2,1)S(1)}, bf16[8,48,896]{2,1,0:T(8,128)(2,1)S(1)}, u32[]{:S(2)}, u32[]{:S(2)}) collective-permute-start(bf16[8,48,896]{2,1,0:T(8,128)(2,1)S(1)} %get-tuple-element.318), channel_id=1, source_target_pairs={{0,4},{1,5},{2,6},{3,7},{4,0},{5,1},{6,2},{7,3},{8,12},{9,13},{10,... | collective-permute-start | bytes 2064392 | tf_op jit(solution)/shard_map/ppermute | solution.py:83
  165.1 25.7 %collective-permute-start.33 = (bf16[8,48,896]{2,1,0:T(8,128)(2,1)S(1)}, bf16[8,48,896]{2,1,0:T(8,128)(2,1)S(1)}, u32[]{:S(2)}, u32[]{:S(2)}) collective-permute-start(bf16[8,48,896]{2,1,0:T(8,128)(2,1)S(1)} %get-tuple-element.320), channel_id=1, source_target_pairs={{0,8},{1,9},{2,10},{3,11},{4,12},{5,13},{6,14},{7,15},{8,0},{9,1},... | collective-permute-start | bytes 2064392 | tf_op jit(solution)/shard_map/ppermute | solution.py:83
  166.9 32.0 %collective-permute-start.31 = (bf16[512,768]{1,0:T(8,128)(2,1)S(1)}, bf16[512,768]{1,0:T(8,128)(2,1)S(1)}, u32[]{:S(2)}, u32[]{:S(2)}) collective-permute-start(bf16[512,768]{1,0:T(8,128)(2,1)S(1)} %finish.1.refs_2_), channel_id=1, source_target_pairs={{0,2},{1,3},{2,0},{3,1},{4,6},{5,7},{6,4},{7,5},{8,10},{9,11},{10,... | collective-permute-start | bytes 2359304 | tf_op jit(solution)/shard_map/ppermute | solution.py:83
  177.2 18.3 %collective-permute-start.38 = (bf16[2,48,1792]{2,1,0:T(8,128)(2,1)S(1)}, bf16[2,48,1792]{2,1,0:T(8,128)(2,1)S(1)}, u32[]{:S(2)}, u32[]{:S(2)}) collective-permute-start(bf16[2,48,1792]{2,1,0:T(8,128)(2,1)S(1)} %get-tuple-element.329), channel_id=1, source_target_pairs={{0,8},{1,9},{2,10},{3,11},{4,12},{5,13},{6,14},{7,15},{8,0},{9,1},... | collective-permute-start | bytes 1032200 | tf_op jit(solution)/shard_map/ppermute | solution.py:83
  178.0 17.5 %collective-permute-start.39 = (bf16[2,48,1792]{2,1,0:T(8,128)(2,1)S(1)}, bf16[2,48,1792]{2,1,0:T(8,128)(2,1)S(1)}, u32[]{:S(2)}, u32[]{:S(2)}) collective-permute-start(bf16[2,48,1792]{2,1,0:T(8,128)(2,1)S(1)} %get-tuple-element.330), channel_id=1, source_target_pairs={{0,16},{1,17},{2,18},{3,19},{4,20},{5,21},{6,22},{7,23},{8,24},{9,... | collective-permute-start | bytes 1032200 | tf_op jit(solution)/shard_map/ppermute | solution.py:83
  201.1 12.2 %collective-permute-start.47 = (bf16[1,48,1792]{2,1,0:T(8,128)(2,1)S(1)}, bf16[1,48,1792]{2,1,0:T(8,128)(2,1)S(1)}, u32[]{:S(2)}, u32[]{:S(2)}) collective-permute-start(bf16[1,48,1792]{2,1,0:T(8,128)(2,1)S(1)} %get-tuple-element.345), channel_id=1, source_target_pairs={{0,16},{1,17},{2,18},{3,19},{4,20},{5,21},{6,22},{7,23},{8,24},{9,... | collective-permute-start | bytes 516104 | tf_op jit(solution)/shard_map/ppermute | solution.py:83
  (69 other events, 894.5 us)
